TPU v7x, 32 devices: a whole 2x2x4 slice. The times are simulated.
32 devices in a mesh: ctx: 4 (over z), tp: 4 (over x, core), dp: 2 (over y).
Axes of the slice: x: 2, y: 2, z: 4, core: 2. Of those that a mesh axis runs over, the one named last changes fastest.
Arguments:
- queries: bfloat16 [512, 8192], P(('dp', 'ctx'), 'tp'), parts along dimension 0, may hold values from -12 to 12
- cache_keys: bfloat16 [4096, 1024], P(('dp', 'ctx'), 'tp'), parts along dimension 0, may hold values from -4 to 4
- cache_values: bfloat16 [4096, 1024], P(('dp', 'ctx'), 'tp'), parts along dimension 0, may hold values from -6 to 6
- new_keys: bfloat16 [512, 1024], P(('dp', 'ctx'), 'tp'), parts along dimension 0, may hold values from -6 to 6
- new_values: bfloat16 [512, 1024], P(('dp', 'ctx'), 'tp'), parts along dimension 0, may hold values from -6 to 6
- prefix_len: int32 [2], P('dp'), parts along dimension 0, may hold values from 1024 to 2048
Outputs:
- attended: bfloat16 [512, 8192], P(('dp', 'ctx'), 'tp'), parts along dimension 0
There are 2 independent parts, one for each index of `dp`. A program takes and returns all parts, laid end to end along the dimension named above; each array names one. Nothing has to cross between parts.
All inputs are finite; a program needn't handle non-finite values.
Results may differ from a plain program's by a relative error of at most 0.038.
Values may be sent and summed in bfloat16 or wider, within the bound.
No kernel may reach another device: no remote copies, remote signals or barrier semaphores. Data moves between devices by JAX's collectives and lax.ppermute only.
A program may use at most 64 MiB of HBM per device.

v0:
```python
import jax
import jax.numpy as jnp
from jax import lax
from jax.sharding import PartitionSpec as P

HEAD_DIM = 128


def passed_along(value, axis, steps):
    count = lax.axis_size(axis)
    pairs = [(source, (source + steps) % count) for source in range(count)]
    return lax.ppermute(value, axis, pairs)


def allowed_for(source, query_tok, cache_rows, query_rows, length):
    key_rows = cache_rows + query_rows
    key_index = jnp.arange(key_rows, dtype=jnp.int32)
    cache_pos = source * cache_rows + key_index
    new_pos = source * query_rows + key_index - cache_rows
    return jnp.where(
        (key_index < cache_rows)[None, :],
        (cache_pos < length)[None, :],
        new_pos[None, :] <= query_tok[:, None],
    )


def softmax_block(running, query_heads, kv_block, allowed):
    old_max, old_total, old_acc = running
    scale = HEAD_DIM ** (-0.5)
    scores = (
        jnp.einsum("hrd,hkd->hrk", query_heads, kv_block[0], preferred_element_type=jnp.float32)
        * scale
    )
    scores = jnp.where(allowed[None], scores, jnp.float32(-1e30))
    new_max = jnp.maximum(old_max, jnp.max(scores, -1))
    weights = jnp.where(allowed[None], jnp.exp(scores - new_max[..., None]), jnp.float32(0.0))
    rescale = jnp.exp(old_max - new_max)
    new_total = old_total * rescale + jnp.sum(weights, -1)
    new_acc = old_acc * rescale[..., None] + jnp.einsum(
        "hrk,hkd->hrd",
        weights.astype(jnp.bfloat16),
        kv_block[1],
        preferred_element_type=jnp.float32,
    )
    return (new_max, new_total, new_acc)


def empty_state(heads, rows):
    return (
        jnp.full((heads, rows), -1e30, jnp.float32),
        jnp.zeros((heads, rows), jnp.float32),
        jnp.zeros((heads, rows, HEAD_DIM), jnp.float32),
    )


def local(queries, cache_keys, cache_values, new_keys, new_values, prefix_len):
    length = prefix_len[0]
    cycle_size = lax.axis_size("ctx")
    my_index = lax.axis_index("ctx")
    cache_rows = cache_keys.shape[0]
    query_rows = queries.shape[0]
    kv_width = cache_keys.shape[1]
    kv_heads = kv_width // HEAD_DIM
    groups = queries.shape[1] // kv_width
    key_rows = cache_rows + query_rows
    stacked = jnp.stack(
        [jnp.concatenate([cache_keys, new_keys], 0), jnp.concatenate([cache_values, new_values], 0)]
    )
    kv_block = stacked.reshape(2, key_rows, kv_heads, HEAD_DIM).transpose(0, 2, 1, 3)
    query_heads = (
        queries.reshape(query_rows, kv_heads, groups, HEAD_DIM)
        .transpose(1, 0, 2, 3)
        .reshape(kv_heads, query_rows * groups, HEAD_DIM)
    )
    query_tok = my_index * query_rows + jnp.arange(query_rows * groups, dtype=jnp.int32) // groups
    running = softmax_block(
        empty_state(kv_heads, query_rows * groups),
        query_heads,
        kv_block,
        allowed_for(my_index, query_tok, cache_rows, query_rows, length),
    )

    def one_turn(turn_index, loop_state):
        running_now, held = loop_state
        held = passed_along(held, "ctx", 1)
        source = (my_index - turn_index) % cycle_size
        allowed = allowed_for(source, query_tok, cache_rows, query_rows, length)
        return (softmax_block(running_now, query_heads, held, allowed), held)

    running, held = lax.fori_loop(1, cycle_size, one_turn, (running, kv_block))
    final_max, final_total, final_acc = running
    result = final_acc / final_total[..., None]
    result = result.reshape(kv_heads, query_rows, groups, HEAD_DIM).transpose(1, 0, 2, 3)
    return result.reshape(query_rows, kv_width * groups).astype(jnp.bfloat16)


def solution(mesh):
    in_specs = (
        P(("dp", "ctx"), "tp"),
        P(("dp", "ctx"), "tp"),
        P(("dp", "ctx"), "tp"),
        P(("dp", "ctx"), "tp"),
        P(("dp", "ctx"), "tp"),
        P("dp"),
    )
    out_specs = P(("dp", "ctx"), "tp")
    return jax.shard_map(local, mesh=mesh, in_specs=in_specs, out_specs=out_specs, check_vma=False)
```

profile of v0, /device:TPU:0, one launch (start us, length us, event | category | flops | bytes accessed | tf_op | source)
XLA Modules:
  0.0 65.0 jit_solution(4492523790669558419)
XLA Ops:
  0.7 0.3 compare_select_fusion.1
  1.0 0.0 copy-start
  1.0 1.0 %pad_maximum_fusion.1 = bf16[576,256]{1,0:T(8,128)(2,1)S(1)} fusion(bf16[64,256]{1,0:T(8,128)(2,1)} %param.12, bf16[512,256]{1,0:T(8,128)(2,1)} %param.10), kind=kLoop, calls=%fused_computation.48 | loop fusion | flops 589824 | bytes 589824 | tf_op jit(solution)/shard_map/concatenate | solution.py:67
  2.0 0.1 stack.10
  2.2 1.0 %pad_maximum_fusion = bf16[576,256]{1,0:T(8,128)(2,1)S(1)} fusion(bf16[64,256]{1,0:T(8,128)(2,1)} %param.11, bf16[512,256]{1,0:T(8,128)(2,1)} %param.9), kind=kLoop, calls=%fused_computation.47 | loop fusion | flops 589824 | bytes 589824 | tf_op jit(solution)/shard_map/concatenate | solution.py:67
  3.2 0.1 stack.9
  3.3 0.1 maximum_bitcast_fusion
  3.4 0.0 copy-done
  3.4 0.6 fusion.18
  4.0 0.7 %fusion.20 = f32[2,512]{1,0:T(2,128)S(1)} fusion(f32[2,576,512]{2,1,0:T(8,128)S(1)} %get-tuple-element.278, f32[2,512]{1,0:T(2,128)S(1)} %broadcast_maximum_fusion, pred[512,576]{0,1:T(8,128)(4,1)S(1)} %compare_select_fusion.1), kind=kLoop, calls=%fused_computation.35 | loop fusion | flops 2948096 | bytes 2662400 | tf_op jit(solution)/shard_map/reduce_sum | solution.py:38
  4.7 1.2 %convolution_add_fusion.1 = f32[2,512,128]{2,1,0:T(8,128)S(1)} fusion(f32[2,576,512]{2,1,0:T(8,128)S(1)} %get-tuple-element.278, f32[2,512]{1,0:T(2,128)S(1)} %broadcast_maximum_fusion, pred[512,576]{0,1:T(8,128)(4,1)S(1)} %compare_select_fusion.1, bf16[2,2,576,128]{3,2,1,0:T(8,128)(2,1)S(1)} %maximum_bitcast_fusion, f32[2,512]{1,0:T(2,128)S(1)} %get-tuple-element.275), kind=kOutput, calls=%fused_computation.36 | convolution fusion | flops 154075136 | bytes 3481600 | tf_op jit(solution)/shard_map/hrk,hkd->hrd/dot_general | solution.py:39
  5.9 58.0 %while.22 = (s32[]{:T(128)}, f32[2,512]{1,0:T(2,128)S(1)}, f32[2,512]{1,0:T(2,128)S(1)}, f32[2,512,128]{2,1,0:T(8,128)S(1)}, bf16[2,2,576,128]{3,2,1,0:T(8,128)(...) while((s32[]{:T(128)}, f32[2,512]{1,0:T(2,128)S(1)}, ...), condition=%wide.region_5.6_spmd.clone, body=%wide.region_2.5_spmd.clone.sunk | while | flops 310519104 | bytes 13773910 | solution.py:90
  5.9 3.1 %collective-permute-start = (bf16[2,2,576,128]{3,2,1,0:T(8,128)(2,1)S(1)}, bf16[2,2,576,128]{3,2,1,0:T(8,128)(2,1)S(1)}, u32[]{:S(2)}, u32[]{:S(2)}) collective-permute-start(bf16[2,2,576,128]{3,2,1,0:T(8,128)(2,1)S(1)} %get-tuple-element.367), channel_id=1, source_target_pairs={{0,8},{8,16},{16,24},{24,0},{1,9},{9,17},{17,25},{25,1},{2,10},{10... | collective-permute-start | bytes 1769480 | tf_op jit(solution)/shard_map/while/body/eval_jaxpr/ppermute | solution.py:12
  9.0 0.7 %add_compare_fusion.3 = (pred[576]{0:T(1024)(128)(4,1)S(1)}, pred[576]{0:T(1024)(128)(4,1)S(1)}) fusion(s32[]{:T(128)} %get-tuple-element.384, s32[]{:T(128)S(6)} %mul.134), kind=kLoop, calls=%fused_computation.21.clone.1 | loop fusion | flops 1728 | bytes 1160 | tf_op jit(solution)/shard_map/while/body/eval_jaxpr/lt | solution.py:22
  9.7 0.3 compare_select_fusion.3
  10.0 14.4 %collective-permute-done = bf16[2,2,576,128]{3,2,1,0:T(8,128)(2,1)S(1)} collective-permute-done((bf16[2,2,576,128]{3,2,1,0:T(8,128)(2,1)S(1)}, bf16[2,2,576,128]{3,2,1,0:T(8,128)(2,1)S(1)}, u32[]{:S(2)}, u32[]{:S(2)}) %collective-permute-start) | collective-permute-done | bytes 589856 | tf_op jit(solution)/shard_map/while/body/eval_jaxpr/ppermute | solution.py:12
  24.3 0.6 fusion.45
  25.0 0.6 fusion.46
  25.7 1.2 %convolution_add_fusion.3 = f32[2,512,128]{2,1,0:T(8,128)S(1)} fusion(f32[2,512,576]{1,2,0:T(8,128)S(1)} %get-tuple-element.345, f32[2,512]{1,0:T(2,128)S(1)} %max.12, pred[512,576]{0,1:T(8,128)(4,1)S(1)} %compare_select_fusion.3, f32[2,512,128]{2,1,0:T(8,128)S(1)} %get-tuple-element.366, bf16[2,2,576,128]{3,2,1,0:T(8,128)(2,1)S(1)} %collective-permute-done, ...), kind=kOutput, calls=%fused_computation.6.clone.1 | convolution fusion | flops 154206208 | bytes 4005888 | tf_op jit(solution)/shard_map/while/body/eval_jaxpr/hrk,hkd->hrd/dot_general | solution.py:39
  26.9 0.1 collective-permute-start
  27.0 0.7 %add_compare_fusion.3 = (pred[576]{0:T(1024)(128)(4,1)S(1)}, pred[576]{0:T(1024)(128)(4,1)S(1)}) fusion(s32[]{:T(128)} %get-tuple-element.384, s32[]{:T(128)S(6)} %mul.134), kind=kLoop, calls=%fused_computation.21.clone.1 | loop fusion | flops 1728 | bytes 1160 | tf_op jit(solution)/shard_map/while/body/eval_jaxpr/lt | solution.py:22
  27.7 0.3 compare_select_fusion.3
  28.0 15.3 %collective-permute-done = bf16[2,2,576,128]{3,2,1,0:T(8,128)(2,1)S(1)} collective-permute-done((bf16[2,2,576,128]{3,2,1,0:T(8,128)(2,1)S(1)}, bf16[2,2,576,128]{3,2,1,0:T(8,128)(2,1)S(1)}, u32[]{:S(2)}, u32[]{:S(2)}) %collective-permute-start) | collective-permute-done | bytes 589856 | tf_op jit(solution)/shard_map/while/body/eval_jaxpr/ppermute | solution.py:12
  43.3 0.6 fusion.45
  43.9 0.6 fusion.46
  44.6 1.2 %convolution_add_fusion.3 = f32[2,512,128]{2,1,0:T(8,128)S(1)} fusion(f32[2,512,576]{1,2,0:T(8,128)S(1)} %get-tuple-element.345, f32[2,512]{1,0:T(2,128)S(1)} %max.12, pred[512,576]{0,1:T(8,128)(4,1)S(1)} %compare_select_fusion.3, f32[2,512,128]{2,1,0:T(8,128)S(1)} %get-tuple-element.366, bf16[2,2,576,128]{3,2,1,0:T(8,128)(2,1)S(1)} %collective-permute-done, ...), kind=kOutput, calls=%fused_computation.6.clone.1 | convolution fusion | flops 154206208 | bytes 4005888 | tf_op jit(solution)/shard_map/while/body/eval_jaxpr/hrk,hkd->hrd/dot_general | solution.py:39
  45.9 0.1 collective-permute-start
  46.0 0.7 %add_compare_fusion.3 = (pred[576]{0:T(1024)(128)(4,1)S(1)}, pred[576]{0:T(1024)(128)(4,1)S(1)}) fusion(s32[]{:T(128)} %get-tuple-element.384, s32[]{:T(128)S(6)} %mul.134), kind=kLoop, calls=%fused_computation.21.clone.1 | loop fusion | flops 1728 | bytes 1160 | tf_op jit(solution)/shard_map/while/body/eval_jaxpr/lt | solution.py:22
  46.7 0.3 compare_select_fusion.3
  47.0 14.4 %collective-permute-done = bf16[2,2,576,128]{3,2,1,0:T(8,128)(2,1)S(1)} collective-permute-done((bf16[2,2,576,128]{3,2,1,0:T(8,128)(2,1)S(1)}, bf16[2,2,576,128]{3,2,1,0:T(8,128)(2,1)S(1)}, u32[]{:S(2)}, u32[]{:S(2)}) %collective-permute-start) | collective-permute-done | bytes 589856 | tf_op jit(solution)/shard_map/while/body/eval_jaxpr/ppermute | solution.py:12
  61.3 0.6 fusion.45
  61.9 0.6 fusion.46
  62.7 1.2 %convolution_add_fusion.3 = f32[2,512,128]{2,1,0:T(8,128)S(1)} fusion(f32[2,512,576]{1,2,0:T(8,128)S(1)} %get-tuple-element.345, f32[2,512]{1,0:T(2,128)S(1)} %max.12, pred[512,576]{0,1:T(8,128)(4,1)S(1)} %compare_select_fusion.3, f32[2,512,128]{2,1,0:T(8,128)S(1)} %get-tuple-element.366, bf16[2,2,576,128]{3,2,1,0:T(8,128)(2,1)S(1)} %collective-permute-done, ...), kind=kOutput, calls=%fused_computation.6.clone.1 | convolution fusion | flops 154206208 | bytes 4005888 | tf_op jit(solution)/shard_map/while/body/eval_jaxpr/hrk,hkd->hrd/dot_general | solution.py:39
  63.9 0.2 fusion.27
  64.2 0.8 %copy.20 = bf16[8,8,16,128]{3,1,2,0:T(8,128)(2,1)} copy(bf16[8,8,16,128]{3,2,1,0:T(8,128)(2,1)S(1)} %bitcast.59) | data formatting | bytes 524288
  (28 shorter events, 0.5 us)
Async XLA Ops:
  1.0 2.4 %copy-start = (bf16[64,2048]{1,0:T(8,128)(2,1)S(1)}, bf16[64,2048]{1,0:T(8,128)(2,1)}, u32[]{:S(2)}) copy-start(bf16[64,2048]{1,0:T(8,128)(2,1)} %param.8) | copy-start | bytes 786436
  5.9 18.4 %collective-permute-start = (bf16[2,2,576,128]{3,2,1,0:T(8,128)(2,1)S(1)}, bf16[2,2,576,128]{3,2,1,0:T(8,128)(2,1)S(1)}, u32[]{:S(2)}, u32[]{:S(2)}) collective-permute-start(bf16[2,2,576,128]{3,2,1,0:T(8,128)(2,1)S(1)} %get-tuple-element.367), channel_id=1, source_target_pairs={{0,8},{8,16},{16,24},{24,0},{1,9},{9,17},{17,25},{25,1},{2,10},{10... | collective-permute-start | bytes 1769480 | tf_op jit(solution)/shard_map/while/body/eval_jaxpr/ppermute | solution.py:12
  26.9 16.4 %collective-permute-start = (bf16[2,2,576,128]{3,2,1,0:T(8,128)(2,1)S(1)}, bf16[2,2,576,128]{3,2,1,0:T(8,128)(2,1)S(1)}, u32[]{:S(2)}, u32[]{:S(2)}) collective-permute-start(bf16[2,2,576,128]{3,2,1,0:T(8,128)(2,1)S(1)} %get-tuple-element.367), channel_id=1, source_target_pairs={{0,8},{8,16},{16,24},{24,0},{1,9},{9,17},{17,25},{25,1},{2,10},{10... | collective-permute-start | bytes 1769480 | tf_op jit(solution)/shard_map/while/body/eval_jaxpr/ppermute | solution.py:12
  45.9 15.4 %collective-permute-start = (bf16[2,2,576,128]{3,2,1,0:T(8,128)(2,1)S(1)}, bf16[2,2,576,128]{3,2,1,0:T(8,128)(2,1)S(1)}, u32[]{:S(2)}, u32[]{:S(2)}) collective-permute-start(bf16[2,2,576,128]{3,2,1,0:T(8,128)(2,1)S(1)} %get-tuple-element.367), channel_id=1, source_target_pairs={{0,8},{8,16},{16,24},{24,0},{1,9},{9,17},{17,25},{25,1},{2,10},{10... | collective-permute-start | bytes 1769480 | tf_op jit(solution)/shard_map/while/body/eval_jaxpr/ppermute | solution.py:12
where the time goes:
time: 65.1 us; the launch traced here: 65 us
  waiting for transfers between devices  44 us (68%)
  other arithmetic  8.16 us (13%)
  matrix products  7.3 us (11%)
  starting transfers between devices  3.19 us (5%)
  local copies, waits for them, and re-layouts  1.24 us (2%)
  between operations  0.79 us (1%)
    ppermute x3, waiting for transfers between devices, passed_along(): return lax.ppermute(value, axis, pairs)  44 us
    dot_general x4, matrix products, softmax_block(): jnp.einsum('hrk,hkd->hrd', weights.astype(jnp.bfloat16), kv_block[1], pre...  4.89 us
    ppermute x3, starting transfers between devices, passed_along(): return lax.ppermute(value, axis, pairs)  3.19 us
    reduce_sum x4, other arithmetic, softmax_block(): new_total = old_total * rescale + jnp.sum(weights, -1)  2.56 us
    dot_general x4, matrix products, softmax_block(): jnp.einsum('hrd,hkd->hrk', query_heads, kv_block[0], preferred_element_ty...  2.41 us
    lt x4, other arithmetic, allowed_for(): cache_pos < length  1.96 us
  transfers between devices with their start and end apart: 3, of which 3 were waited for; matrix products, arithmetic and copies ran while one was open for 4% of the time, Pallas kernels for 0%

commit v1 on v0

--- a/solution.py
+++ b/solution.py
@@ -1,9 +1,242 @@
+import functools
+
 import jax
 import jax.numpy as jnp
 from jax import lax
+from jax.experimental import pallas as pl
+from jax.experimental.pallas import tpu as pltpu
 from jax.sharding import PartitionSpec as P
 
 HEAD_DIM = 128
+LOW = -1e30
+SLOPE = HEAD_DIM ** (-0.5) * 1.4426950408889634
+STATS = 16
+TRADES = ((1, 2), (2, 1))
+
+VMEM = pl.BlockSpec(memory_space=pltpu.VMEM)
+SMEM = pl.BlockSpec(memory_space=pltpu.SMEM)
+ANY = pl.BlockSpec(memory_space=pl.ANY)
+LIMIT = 24 * 1024 * 1024
+
+
+def lead(array, row):
+    return array[row : row + 1, :]
+
+
+def attend(query, kv_ref, source, token_dev, length, cache_rows, new_rows, lane0):
+    key_rows = cache_rows + new_rows
+    keys = kv_ref[0:key_rows, :]
+    scores = lax.dot_general(
+        keys, query, (((1,), (1,)), ((), ())), preferred_element_type=jnp.float32
+    )
+    rows = query.shape[0]
+    slot = lax.broadcasted_iota(jnp.int32, (cache_rows, rows), 0)
+    cached = jnp.where(slot < length - source * cache_rows, scores[:cache_rows], LOW)
+    new = lax.broadcasted_iota(jnp.int32, (new_rows, rows), 0) + source * new_rows
+    token = lax.rem(
+        lax.broadcasted_iota(jnp.int32, (new_rows, rows), 1), new_rows
+    ) + token_dev * new_rows
+    fresh = jnp.where(new <= token, scores[cache_rows:], LOW)
+    scores = jnp.concatenate([cached, fresh], 0)
+    top = jnp.max(scores, axis=0, keepdims=True)
+    weights = jnp.exp2((scores - top) * SLOPE)
+    total = jnp.sum(weights, axis=0, keepdims=True)
+    values = kv_ref[key_rows : 2 * key_rows, :]
+    summed = lax.dot_general(
+        values,
+        weights.astype(jnp.bfloat16),
+        (((0,), (0,)), ((), ())),
+        preferred_element_type=jnp.float32,
+    )
+    return top, total, summed
+
+
+def joined(one, two):
+    top = jnp.maximum(one[0], two[0])
+    left, right = jnp.exp2((one[0] - top) * SLOPE), jnp.exp2((two[0] - top) * SLOPE)
+    return top, one[1] * left + two[1] * right, one[2] * left + two[2] * right
+
+
+def stacked_heads(q_ref, first, count):
+    return jnp.concatenate(
+        [q_ref[:, pl.ds((first + g) * HEAD_DIM, HEAD_DIM)] for g in range(count)], 0
+    )
+
+
+def start_kernel(dims, kv_xor, q_xor, len_ref, q_ref, kv_ref, state_ref):
+    cache_rows, new_rows, groups, step = dims
+    me = lax.axis_index("ctx")
+    for at in range(0, groups, step):
+        query = stacked_heads(q_ref, at, step)
+        lanes = pl.ds(at * new_rows, step * new_rows)
+        top, total, summed = attend(
+            query, kv_ref, me ^ kv_xor, me ^ q_xor, len_ref[0], cache_rows, new_rows, at
+        )
+        state_ref[0:HEAD_DIM, lanes] = summed
+        state_ref[HEAD_DIM : HEAD_DIM + 1, lanes] = top
+        state_ref[HEAD_DIM + 1 : HEAD_DIM + 2, lanes] = total
+
+
+def finish_kernel(dims, kv_xor, q_xor, packed, len_ref, q_ref, kv_ref, state_ref, out_ref):
+    cache_rows, new_rows, groups, step = dims
+    me = lax.axis_index("ctx")
+    for at in range(0, groups, step):
+        query = stacked_heads(q_ref, at, step)
+        lanes = pl.ds(at * new_rows, step * new_rows)
+        ours = attend(
+            query, kv_ref, me ^ kv_xor, me ^ q_xor, len_ref[0], cache_rows, new_rows, at
+        )
+        before = (
+            state_ref[HEAD_DIM : HEAD_DIM + 1, lanes],
+            state_ref[HEAD_DIM + 1 : HEAD_DIM + 2, lanes],
+            state_ref[0:HEAD_DIM, lanes],
+        )
+        top, total, summed = joined(before, ours)
+        result = summed * (1.0 / total)
+        log = top * SLOPE + jnp.log2(total)
+        if packed:
+            high = log.astype(jnp.bfloat16).astype(jnp.float32)
+            rest = log - high
+            middle = rest.astype(jnp.bfloat16).astype(jnp.float32)
+            low = rest - middle
+            row = lax.broadcasted_iota(jnp.int32, (STATS, step * new_rows), 0)
+            stats = jnp.where(row == 0, high, jnp.where(row == 1, middle, jnp.where(row == 2, low, 0.0)))
+            out_ref[0:HEAD_DIM, lanes] = result.astype(jnp.bfloat16)
+            out_ref[HEAD_DIM : HEAD_DIM + STATS, lanes] = stats.astype(jnp.bfloat16)
+        else:
+            out_ref[0:HEAD_DIM, lanes] = result
+            out_ref[HEAD_DIM : HEAD_DIM + 1, lanes] = log
+
+
+def merge_kernel(dims, heads, *refs):
+    cache_rows, new_rows, groups, step = dims
+    out_ref = refs[-1]
+    pair = HEAD_DIM // new_rows
+    for head in range(heads):
+        own_ref, got_ref = refs[2 * head], refs[2 * head + 1]
+        for at in range(0, groups, pair):
+            lanes = pl.ds(at * new_rows, pair * new_rows)
+            stats = got_ref[HEAD_DIM : HEAD_DIM + STATS, lanes].astype(jnp.float32)
+            theirs = stats[0:1] + stats[1:2] + stats[2:3]
+            mine = own_ref[HEAD_DIM : HEAD_DIM + 1, lanes]
+            top = jnp.maximum(mine, theirs)
+            left, right = jnp.exp2(mine - top), jnp.exp2(theirs - top)
+            scale = 1.0 / (left + right)
+            whole = own_ref[0:HEAD_DIM, lanes] * (left * scale) + got_ref[
+                0:HEAD_DIM, lanes
+            ].astype(jnp.float32) * (right * scale)
+            turned = whole.T.astype(jnp.bfloat16)
+            for g in range(pair):
+                column = (head * groups + at + g) * HEAD_DIM
+                out_ref[:, column : column + HEAD_DIM] = turned[g * new_rows : (g + 1) * new_rows, :]
+
+
+def pack_kernel(heads, q_ref, ck_ref, cv_ref, nk_ref, nv_ref, *rest):
+    sems = rest[-1]
+    kv_refs, q_refs = rest[0:heads], rest[heads : 2 * heads]
+    cache_rows, new_rows = ck_ref.shape[0], nk_ref.shape[0]
+    key_rows = cache_rows + new_rows
+    width = q_ref.shape[1] // heads
+    copies = []
+    for head in range(heads):
+        columns = pl.ds(head * HEAD_DIM, HEAD_DIM)
+        kv = kv_refs[head]
+        for source, at, rows in (
+            (ck_ref, 0, cache_rows),
+            (nk_ref, cache_rows, new_rows),
+            (cv_ref, key_rows, cache_rows),
+            (nv_ref, key_rows + cache_rows, new_rows),
+        ):
+            copies.append((source.at[:, columns], kv.at[pl.ds(at, rows), :]))
+        copies.append((q_ref.at[:, pl.ds(head * width, width)], q_refs[head]))
+    handles = [
+        pltpu.make_async_copy(source, target, sems.at[n])
+        for n, (source, target) in enumerate(copies)
+    ]
+    for handle in handles:
+        handle.start()
+    for handle in handles:
+        handle.wait()
+
+
+def traded(value, xor):
+    count = lax.axis_size("ctx")
+    return lax.ppermute(value, "ctx", [(source, source ^ xor) for source in range(count)])
+
+
+def cost(dims):
+    cache_rows, new_rows, groups, _ = dims
+    pairs = (cache_rows + new_rows) * groups * new_rows
+    return pl.CostEstimate(
+        flops=4 * HEAD_DIM * pairs, bytes_accessed=1 << 20, transcendentals=pairs
+    )
+
+
+def local_four(queries, cache_keys, cache_values, new_keys, new_values, prefix_len):
+    cache_rows, kv_width = cache_keys.shape
+    new_rows = queries.shape[0]
+    heads = kv_width // HEAD_DIM
+    groups = queries.shape[1] // kv_width
+    key_rows = cache_rows + new_rows
+    rows = groups * new_rows
+    dims = (cache_rows, new_rows, groups, 4)
+    params = pltpu.CompilerParams(vmem_limit_bytes=LIMIT)
+    bf16, f32 = jnp.bfloat16, jnp.float32
+    packed = pl.pallas_call(
+        functools.partial(pack_kernel, heads),
+        out_shape=[jax.ShapeDtypeStruct((2 * key_rows, HEAD_DIM), bf16)] * heads
+        + [jax.ShapeDtypeStruct((new_rows, groups * HEAD_DIM), bf16)] * heads,
+        in_specs=[ANY] * 5,
+        out_specs=[ANY] * (2 * heads),
+        scratch_shapes=[pltpu.SemaphoreType.DMA((5 * heads,))],
+        compiler_params=params,
+        name="pack",
+    )(queries, cache_keys, cache_values, new_keys, new_values)
+    kv, q = packed[:heads], packed[heads:]
+    state = jax.ShapeDtypeStruct((HEAD_DIM + 8, rows), f32)
+    sent = jax.ShapeDtypeStruct((HEAD_DIM + STATS, rows), bf16)
+
+    def start(head, kv_xor, q_xor, query, keys):
+        return pl.pallas_call(
+            functools.partial(start_kernel, dims, kv_xor, q_xor),
+            out_shape=state,
+            in_specs=[SMEM, VMEM, VMEM],
+            out_specs=VMEM,
+            compiler_params=params,
+            cost_estimate=cost(dims),
+            name="start",
+        )(prefix_len, query, keys)
+
+    def finish(head, kv_xor, q_xor, query, keys, before, out):
+        return pl.pallas_call(
+            functools.partial(finish_kernel, dims, kv_xor, q_xor, out is sent),
+            out_shape=out,
+            in_specs=[SMEM, VMEM, VMEM, VMEM],
+            out_specs=VMEM,
+            compiler_params=params,
+            cost_estimate=cost(dims),
+            name="finish",
+        )(prefix_len, query, keys, before)
+
+    far_q = [traded(q[h], TRADES[h % 2][1]) for h in range(heads)]
+    far_kv = [traded(kv[h], TRADES[h % 2][0]) for h in range(heads)]
+    mine = [start(h, 0, 0, q[h], kv[h]) for h in range(heads)]
+    theirs = [start(h, 0, TRADES[h % 2][1], far_q[h], kv[h]) for h in range(heads)]
+    pieces = []
+    for h in range(heads):
+        kv_xor, q_xor = TRADES[h % 2]
+        out = finish(h, kv_xor, q_xor, far_q[h], far_kv[h], theirs[h], sent)
+        got = traded(out, q_xor)
+        own = finish(h, kv_xor, 0, q[h], far_kv[h], mine[h], state)
+        pieces += [own, got]
+    return pl.pallas_call(
+        functools.partial(merge_kernel, dims, heads),
+        out_shape=jax.ShapeDtypeStruct(queries.shape, bf16),
+        in_specs=[VMEM] * (2 * heads),
+        out_specs=VMEM,
+        compiler_params=params,
+        name="merge",
+    )(*pieces)
 
 
 def passed_along(value, axis, steps):
@@ -53,7 +286,7 @@
     )
 
 
-def local(queries, cache_keys, cache_values, new_keys, new_values, prefix_len):
+def local_ring(queries, cache_keys, cache_values, new_keys, new_values, prefix_len):
     length = prefix_len[0]
     cycle_size = lax.axis_size("ctx")
     my_index = lax.axis_index("ctx")
@@ -104,4 +337,5 @@
         P("dp"),
     )
     out_specs = P(("dp", "ctx"), "tp")
+    local = local_four if mesh.shape["ctx"] == 4 else local_ring
     return jax.shard_map(local, mesh=mesh, in_specs=in_specs, out_specs=out_specs, check_vma=False)

time: 65.1 us -> 42.6 us (0.65)
  waiting for transfers between devices: 44 us -> 17.8 us
  Pallas kernels: 0 us -> 9.85 us
  other arithmetic: 8.16 us -> 0 us
  matrix products: 7.3 us -> 0 us
  starting transfers between devices: 3.19 us -> 9.43 us
  local copies, waits for them, and re-layouts: 1.24 us -> 4.36 us
    ppermute x3 -> x6, waiting for transfers between devices: 44 us -> 17.8 us  [traded(): lax.ppermute(value, 'ctx', [(source, source ^ xor) for source in range(co...]
    pallas_call x0 -> x10, Pallas kernels: none -> 9.85 us  [the longest x4 4.38 us: finish(): pl.pallas_call(functools.partial(finish_kernel, dims, kv_xor, q_xor, out...]
    dot_general x8 -> x0, matrix products: 7.3 us -> none  [the longest x4 4.89 us: softmax_block(): jnp.einsum('hrk,hkd->hrd', weights.astype(jnp.bfloat16), kv_block[1], pre...]
    ppermute x3 -> x6, starting transfers between devices: 3.19 us -> 9.43 us  [traded(): lax.ppermute(value, 'ctx', [(source, source ^ xor) for source in range(co...]
    unnamed x4 -> x10, local copies, waits for them, and re-layouts: 0.81 us -> 4.36 us
    reduce_sum x4 -> x0, other arithmetic: 2.56 us -> none  [softmax_block(): new_total = old_total * rescale + jnp.sum(weights, -1)]
    concatenate x2 -> x0, other arithmetic: 2.03 us -> none  [the longest x1 1.03 us: local(): jnp.concatenate([cache_values, new_values], 0)]
    lt x4 -> x0, other arithmetic: 1.96 us -> none  [allowed_for(): cache_pos < length]
  transfers between devices with their start and end apart: 3 -> 6, of which waited for: 3 -> 2; matrix products, arithmetic and copies ran while one was open for 4% -> 0% of each run, Pallas kernels for 0% -> 21%
where the time goes in v1:
time: 42.6 us; the launch traced here: 42.2 us
  waiting for transfers between devices  17.8 us (42%)
  Pallas kernels  9.85 us (23%)
  starting transfers between devices  9.43 us (22%)
  local copies, waits for them, and re-layouts  4.36 us (10%)
  between operations  0.75 us (2%)
    ppermute x6, waiting for transfers between devices, traded(): lax.ppermute(value, 'ctx', [(source, source ^ xor) for source in range(co...  17.8 us
    ppermute x6, starting transfers between devices, traded(): lax.ppermute(value, 'ctx', [(source, source ^ xor) for source in range(co...  9.43 us
    pallas_call x4, Pallas kernels, finish(): pl.pallas_call(functools.partial(finish_kernel, dims, kv_xor, q_xor, out...  4.38 us
    unnamed x10, local copies, waits for them, and re-layouts  4.36 us
    pallas_call x4, Pallas kernels, start(): pl.pallas_call(functools.partial(start_kernel, dims, kv_xor, q_xor), out_...  4.33 us
    pallas_call x1, Pallas kernels, local_four(): pl.pallas_call(functools.partial(merge_kernel, dims, heads), out_shape=ja...  0.89 us
  transfers between devices with their start and end apart: 6, of which 2 were waited for; matrix products, arithmetic and copies ran while one was open for 0% of the time, Pallas kernels for 21%

profile of v1, /device:TPU:0, one launch (start us, length us, event | category | flops | bytes accessed | tf_op | source)
XLA Modules:
  0.0 42.2 jit_solution(18238507280370456833)
XLA Ops:
  0.0 0.0 copy-start
  0.0 0.9 %copy-done = bf16[64,2048]{1,0:T(8,128)(2,1)S(1)} copy-done((bf16[64,2048]{1,0:T(8,128)(2,1)S(1)}, bf16[64,2048]{1,0:T(8,128)(2,1)}, u32[]{:S(2)}) %copy-start) | copy-done | bytes 262168
  1.0 0.0 copy-start.1
  1.0 0.9 %copy-done.1 = bf16[512,256]{1,0:T(8,128)(2,1)S(1)} copy-done((bf16[512,256]{1,0:T(8,128)(2,1)S(1)}, bf16[512,256]{1,0:T(8,128)(2,1)}, u32[]{:S(2)}) %copy-start.1) | copy-done | bytes 262168
  1.9 0.0 copy-start.2
  1.9 0.9 %copy-done.2 = bf16[512,256]{1,0:T(8,128)(2,1)S(1)} copy-done((bf16[512,256]{1,0:T(8,128)(2,1)S(1)}, bf16[512,256]{1,0:T(8,128)(2,1)}, u32[]{:S(2)}) %copy-start.2) | copy-done | bytes 262168
  2.9 0.0 copy-start.3
  2.9 0.8 %copy-done.3 = bf16[64,256]{1,0:T(8,128)(2,1)S(1)} copy-done((bf16[64,256]{1,0:T(8,128)(2,1)S(1)}, bf16[64,256]{1,0:T(8,128)(2,1)}, u32[]{:S(2)}) %copy-start.3) | copy-done | bytes 32792
  3.6 0.0 copy-start.4
  3.6 0.8 %copy-done.4 = bf16[64,256]{1,0:T(8,128)(2,1)S(1)} copy-done((bf16[64,256]{1,0:T(8,128)(2,1)S(1)}, bf16[64,256]{1,0:T(8,128)(2,1)}, u32[]{:S(2)}) %copy-start.4) | copy-done | bytes 32792
  4.4 0.3 pack.1
  4.6 4.1 %collective-permute-start.3 = (bf16[1152,128]{1,0:T(8,128)(2,1)S(1)}, bf16[1152,128]{1,0:T(8,128)(2,1)S(1)}, u32[]{:S(2)}, u32[]{:S(2)}) collective-permute-start(bf16[1152,128]{1,0:T(8,128)(2,1)S(1)} %get-tuple-element.12.kv_ref), channel_id=1, source_target_pairs={{0,16},{8,24},{16,0},{24,8},{1,17},{9,25},{17,1},{25,9},{2,18},{10... | collective-permute-start | bytes 884744 | tf_op jit(solution)/shard_map/ppermute | solution.py:164
  8.7 1.6 %collective-permute-start = (bf16[1152,128]{1,0:T(8,128)(2,1)S(1)}, bf16[1152,128]{1,0:T(8,128)(2,1)S(1)}, u32[]{:S(2)}, u32[]{:S(2)}) collective-permute-start(bf16[1152,128]{1,0:T(8,128)(2,1)S(1)} %get-tuple-element.10.kv_ref), channel_id=1, source_target_pairs={{0,8},{8,0},{16,24},{24,16},{1,9},{9,1},{17,25},{25,17},{2,10},{10... | collective-permute-start | bytes 884744 | tf_op jit(solution)/shard_map/ppermute | solution.py:164
  10.3 0.4 %collective-permute-start.4 = (bf16[64,1024]{1,0:T(8,128)(2,1)S(1)}, bf16[64,1024]{1,0:T(8,128)(2,1)S(1)}, u32[]{:S(2)}, u32[]{:S(2)}) collective-permute-start(bf16[64,1024]{1,0:T(8,128)(2,1)S(1)} %get-tuple-element.11.q_ref), channel_id=1, source_target_pairs={{0,8},{8,0},{16,24},{24,16},{1,9},{9,1},{17,25},{25,17},{2,10},{10... | collective-permute-start | bytes 393224 | tf_op jit(solution)/shard_map/ppermute | solution.py:164
  10.8 0.1 collective-permute-start.1
  11.5 16.5 %collective-permute-done.4.q_ref = bf16[64,1024]{1,0:T(8,128)(2,1)S(1)} collective-permute-done((bf16[64,1024]{1,0:T(8,128)(2,1)S(1)}, bf16[64,1024]{1,0:T(8,128)(2,1)S(1)}, u32[]{:S(2)}, u32[]{:S(2)}) %collective-permute-start.4) | collective-permute-done | bytes 131104 | tf_op jit(solution)/shard_map/ppermute | solution.py:164
  28.0 1.1 %start.7.state_ref = f32[136,512]{1,0:T(8,128)S(1)} custom-call(s32[1]{0:T(128)S(6)} %copy.7.len_ref, bf16[64,1024]{1,0:T(8,128)(2,1)S(1)} %collective-permute-done.4.q_ref, bf16[1152,128]{1,0:T(8,128)(2,1)S(1)} %get-tuple-element.12.kv_ref), custom_call_target="tpu_custom_call" | custom-call | flops 150994944 | bytes 1048576 | tf_op jit(solution)/shard_map/start/pallas_call | solution.py:200
  29.1 0.0 collective-permute-done.1.q_ref
  29.1 1.1 %start.5.state_ref = f32[136,512]{1,0:T(8,128)S(1)} custom-call(s32[1]{0:T(128)S(6)} %copy.7.len_ref, bf16[64,1024]{1,0:T(8,128)(2,1)S(1)} %collective-permute-done.1.q_ref, bf16[1152,128]{1,0:T(8,128)(2,1)S(1)} %get-tuple-element.10.kv_ref), custom_call_target="tpu_custom_call" | custom-call | flops 150994944 | bytes 1048576 | tf_op jit(solution)/shard_map/start/pallas_call | solution.py:200
  30.2 0.0 collective-permute-done.3.kv_ref
  30.2 1.1 %finish.7 = bf16[144,512]{1,0:T(8,128)(2,1)S(1)} custom-call(s32[1]{0:T(128)S(6)} %copy.7.len_ref, bf16[64,1024]{1,0:T(8,128)(2,1)S(1)} %collective-permute-done.4.q_ref, bf16[1152,128]{1,0:T(8,128)(2,1)S(1)} %collective-permute-done.3.kv_ref, f32[136,512]{1,0:T(8,128)S(1)} %start.7.state_ref), custom_call_target="tpu_custom_call" | custom-call | flops 150994944 | bytes 1048576 | tf_op jit(solution)/shard_map/finish/pallas_call | solution.py:211
  31.3 0.3 collective-permute-start.5
  31.6 0.0 collective-permute-done.kv_ref
  31.6 1.1 %finish.5 = bf16[144,512]{1,0:T(8,128)(2,1)S(1)} custom-call(s32[1]{0:T(128)S(6)} %copy.7.len_ref, bf16[64,1024]{1,0:T(8,128)(2,1)S(1)} %collective-permute-done.1.q_ref, bf16[1152,128]{1,0:T(8,128)(2,1)S(1)} %collective-permute-done.kv_ref, f32[136,512]{1,0:T(8,128)S(1)} %start.5.state_ref), custom_call_target="tpu_custom_call" | custom-call | flops 150994944 | bytes 1048576 | tf_op jit(solution)/shard_map/finish/pallas_call | solution.py:211
  32.7 2.9 %collective-permute-start.2 = (bf16[144,512]{1,0:T(8,128)(2,1)S(1)}, bf16[144,512]{1,0:T(8,128)(2,1)S(1)}, u32[]{:S(2)}, u32[]{:S(2)}) collective-permute-start(bf16[144,512]{1,0:T(8,128)(2,1)S(1)} %finish.5), channel_id=1, source_target_pairs={{0,16},{8,24},{16,0},{24,8},{1,17},{9,25},{17,1},{25,9},{2,18},{10... | collective-permute-start | bytes 442376 | tf_op jit(solution)/shard_map/ppermute | solution.py:164
  35.6 1.1 %start.6.state_ref = f32[136,512]{1,0:T(8,128)S(1)} custom-call(s32[1]{0:T(128)S(6)} %copy.7.len_ref, bf16[64,1024]{1,0:T(8,128)(2,1)S(1)} %get-tuple-element.11.q_ref, bf16[1152,128]{1,0:T(8,128)(2,1)S(1)} %get-tuple-element.12.kv_ref), custom_call_target="tpu_custom_call" | custom-call | flops 150994944 | bytes 1048576 | tf_op jit(solution)/shard_map/start/pallas_call | solution.py:200
  36.7 1.1 %start.4.state_ref = f32[136,512]{1,0:T(8,128)S(1)} custom-call(s32[1]{0:T(128)S(6)} %copy.7.len_ref, bf16[64,1024]{1,0:T(8,128)(2,1)S(1)} %get-tuple-element.9.q_ref, bf16[1152,128]{1,0:T(8,128)(2,1)S(1)} %get-tuple-element.10.kv_ref), custom_call_target="tpu_custom_call" | custom-call | flops 150994944 | bytes 1048576 | tf_op jit(solution)/shard_map/start/pallas_call | solution.py:200
  37.8 1.1 %finish.6.refs_2_ = f32[136,512]{1,0:T(8,128)S(1)} custom-call(s32[1]{0:T(128)S(6)} %copy.7.len_ref, bf16[64,1024]{1,0:T(8,128)(2,1)S(1)} %get-tuple-element.11.q_ref, bf16[1152,128]{1,0:T(8,128)(2,1)S(1)} %collective-permute-done.3.kv_ref, f32[136,512]{1,0:T(8,128)S(1)} %start.6.state_ref), custom_call_target="tpu_custom_call" | custom-call | flops 150994944 | bytes 1048576 | tf_op jit(solution)/shard_map/finish/pallas_call | solution.py:211
  38.9 1.1 %finish.4.refs_0_ = f32[136,512]{1,0:T(8,128)S(1)} custom-call(s32[1]{0:T(128)S(6)} %copy.7.len_ref, bf16[64,1024]{1,0:T(8,128)(2,1)S(1)} %get-tuple-element.9.q_ref, bf16[1152,128]{1,0:T(8,128)(2,1)S(1)} %collective-permute-done.kv_ref, f32[136,512]{1,0:T(8,128)S(1)} %start.4.state_ref), custom_call_target="tpu_custom_call" | custom-call | flops 150994944 | bytes 1048576 | tf_op jit(solution)/shard_map/finish/pallas_call | solution.py:211
  40.0 0.0 collective-permute-done.5.refs_3_
  40.0 1.3 %collective-permute-done.2.refs_1_ = bf16[144,512]{1,0:T(8,128)(2,1)S(1)} collective-permute-done((bf16[144,512]{1,0:T(8,128)(2,1)S(1)}, bf16[144,512]{1,0:T(8,128)(2,1)S(1)}, u32[]{:S(2)}, u32[]{:S(2)}) %collective-permute-start.2) | collective-permute-done | bytes 147488 | tf_op jit(solution)/shard_map/ppermute | solution.py:164
  41.3 0.9 %merge.1 = bf16[64,2048]{1,0:T(8,128)(2,1)} custom-call(f32[136,512]{1,0:T(8,128)S(1)} %finish.4.refs_0_, bf16[144,512]{1,0:T(8,128)(2,1)S(1)} %collective-permute-done.2.refs_1_, f32[136,512]{1,0:T(8,128)S(1)} %finish.6.refs_2_, bf16[144,512]{1,0:T(8,128)(2,1)S(1)} %collective-permute-done.5.refs_3_), custom_call_target="tpu_custom_call" | custom-call | tf_op jit(solution)/shard_map/merge/pallas_call | solution.py:232
Async XLA Ops:
  0.0 0.9 %copy-start = (bf16[64,2048]{1,0:T(8,128)(2,1)S(1)}, bf16[64,2048]{1,0:T(8,128)(2,1)}, u32[]{:S(2)}) copy-start(bf16[64,2048]{1,0:T(8,128)(2,1)} %q_ref.1) | copy-start | bytes 786436
  1.0 0.9 %copy-start.1 = (bf16[512,256]{1,0:T(8,128)(2,1)S(1)}, bf16[512,256]{1,0:T(8,128)(2,1)}, u32[]{:S(2)}) copy-start(bf16[512,256]{1,0:T(8,128)(2,1)} %ck_ref.1) | copy-start | bytes 786436
  1.9 0.9 %copy-start.2 = (bf16[512,256]{1,0:T(8,128)(2,1)S(1)}, bf16[512,256]{1,0:T(8,128)(2,1)}, u32[]{:S(2)}) copy-start(bf16[512,256]{1,0:T(8,128)(2,1)} %cv_ref.1) | copy-start | bytes 786436
  2.9 0.8 %copy-start.3 = (bf16[64,256]{1,0:T(8,128)(2,1)S(1)}, bf16[64,256]{1,0:T(8,128)(2,1)}, u32[]{:S(2)}) copy-start(bf16[64,256]{1,0:T(8,128)(2,1)} %nk_ref.1) | copy-start | bytes 98308
  3.6 0.8 %copy-start.4 = (bf16[64,256]{1,0:T(8,128)(2,1)S(1)}, bf16[64,256]{1,0:T(8,128)(2,1)}, u32[]{:S(2)}) copy-start(bf16[64,256]{1,0:T(8,128)(2,1)} %nv_ref.1) | copy-start | bytes 98308
  4.6 25.5 %collective-permute-start.3 = (bf16[1152,128]{1,0:T(8,128)(2,1)S(1)}, bf16[1152,128]{1,0:T(8,128)(2,1)S(1)}, u32[]{:S(2)}, u32[]{:S(2)}) collective-permute-start(bf16[1152,128]{1,0:T(8,128)(2,1)S(1)} %get-tuple-element.12.kv_ref), channel_id=1, source_target_pairs={{0,16},{8,24},{16,0},{24,8},{1,17},{9,25},{17,1},{25,9},{2,18},{10... | collective-permute-start | bytes 884744 | tf_op jit(solution)/shard_map/ppermute | solution.py:164
  8.7 22.9 %collective-permute-start = (bf16[1152,128]{1,0:T(8,128)(2,1)S(1)}, bf16[1152,128]{1,0:T(8,128)(2,1)S(1)}, u32[]{:S(2)}, u32[]{:S(2)}) collective-permute-start(bf16[1152,128]{1,0:T(8,128)(2,1)S(1)} %get-tuple-element.10.kv_ref), channel_id=1, source_target_pairs={{0,8},{8,0},{16,24},{24,16},{1,9},{9,1},{17,25},{25,17},{2,10},{10... | collective-permute-start | bytes 884744 | tf_op jit(solution)/shard_map/ppermute | solution.py:164
  10.3 17.7 %collective-permute-start.4 = (bf16[64,1024]{1,0:T(8,128)(2,1)S(1)}, bf16[64,1024]{1,0:T(8,128)(2,1)S(1)}, u32[]{:S(2)}, u32[]{:S(2)}) collective-permute-start(bf16[64,1024]{1,0:T(8,128)(2,1)S(1)} %get-tuple-element.11.q_ref), channel_id=1, source_target_pairs={{0,8},{8,0},{16,24},{24,16},{1,9},{9,1},{17,25},{25,17},{2,10},{10... | collective-permute-start | bytes 393224 | tf_op jit(solution)/shard_map/ppermute | solution.py:164
  10.8 18.3 %collective-permute-start.1 = (bf16[64,1024]{1,0:T(8,128)(2,1)S(1)}, bf16[64,1024]{1,0:T(8,128)(2,1)S(1)}, u32[]{:S(2)}, u32[]{:S(2)}) collective-permute-start(bf16[64,1024]{1,0:T(8,128)(2,1)S(1)} %get-tuple-element.9.q_ref), channel_id=1, source_target_pairs={{0,16},{8,24},{16,0},{24,8},{1,17},{9,25},{17,1},{25,9},{2,18},{10... | collective-permute-start | bytes 393224 | tf_op jit(solution)/shard_map/ppermute | solution.py:164
  31.3 8.7 %collective-permute-start.5 = (bf16[144,512]{1,0:T(8,128)(2,1)S(1)}, bf16[144,512]{1,0:T(8,128)(2,1)S(1)}, u32[]{:S(2)}, u32[]{:S(2)}) collective-permute-start(bf16[144,512]{1,0:T(8,128)(2,1)S(1)} %finish.7), channel_id=1, source_target_pairs={{0,8},{8,0},{16,24},{24,16},{1,9},{9,1},{17,25},{25,17},{2,10},{10... | collective-permute-start | bytes 442376 | tf_op jit(solution)/shard_map/ppermute | solution.py:164
  32.7 8.6 %collective-permute-start.2 = (bf16[144,512]{1,0:T(8,128)(2,1)S(1)}, bf16[144,512]{1,0:T(8,128)(2,1)S(1)}, u32[]{:S(2)}, u32[]{:S(2)}) collective-permute-start(bf16[144,512]{1,0:T(8,128)(2,1)S(1)} %finish.5), channel_id=1, source_target_pairs={{0,16},{8,24},{16,0},{24,8},{1,17},{9,25},{17,1},{25,9},{2,18},{10... | collective-permute-start | bytes 442376 | tf_op jit(solution)/shard_map/ppermute | solution.py:164

commit v2 on v0

--- a/solution.py
+++ b/solution.py
@@ -1,9 +1,266 @@
+import functools
+
 import jax
 import jax.numpy as jnp
 from jax import lax
+from jax.experimental import pallas as pl
+from jax.experimental.pallas import tpu as pltpu
 from jax.sharding import PartitionSpec as P
 
 HEAD_DIM = 128
+LOW = -1e30
+SLOPE = HEAD_DIM ** (-0.5) * 1.4426950408889634
+STATS = 16
+STEP = 4
+
+VMEM = pl.BlockSpec(memory_space=pltpu.VMEM)
+SMEM = pl.BlockSpec(memory_space=pltpu.SMEM)
+HBM = pl.BlockSpec(memory_space=pltpu.HBM)
+ANY = pl.BlockSpec(memory_space=pl.ANY)
+LIMIT = 24 * 1024 * 1024
+
+
+def attend(query, kv_ref, source, token_dev, length, cache_rows, new_rows):
+    key_rows = cache_rows + new_rows
+    keys = kv_ref[0:key_rows, :]
+    scores = lax.dot_general(
+        keys, query, (((1,), (1,)), ((), ())), preferred_element_type=jnp.float32
+    )
+    rows = query.shape[0]
+    slot = lax.broadcasted_iota(jnp.int32, (cache_rows, rows), 0)
+    cached = jnp.where(slot < length - source * cache_rows, scores[:cache_rows], LOW)
+    new = lax.broadcasted_iota(jnp.int32, (new_rows, rows), 0) + source * new_rows
+    token = lax.rem(
+        lax.broadcasted_iota(jnp.int32, (new_rows, rows), 1), new_rows
+    ) + token_dev * new_rows
+    fresh = jnp.where(new <= token, scores[cache_rows:], LOW)
+    scores = jnp.concatenate([cached, fresh], 0)
+    top = jnp.max(scores, axis=0, keepdims=True)
+    weights = jnp.exp2((scores - top) * SLOPE)
+    total = jnp.sum(weights, axis=0, keepdims=True)
+    values = kv_ref[key_rows : 2 * key_rows, :]
+    summed = lax.dot_general(
+        values,
+        weights.astype(jnp.bfloat16),
+        (((0,), (0,)), ((), ())),
+        preferred_element_type=jnp.float32,
+    )
+    return top, total, summed
+
+
+def joined(one, two):
+    top = jnp.maximum(one[0], two[0])
+    left, right = jnp.exp2((one[0] - top) * SLOPE), jnp.exp2((two[0] - top) * SLOPE)
+    return top, one[1] * left + two[1] * right, one[2] * left + two[2] * right
+
+
+def stacked_heads(q_ref, first, count):
+    return jnp.concatenate(
+        [q_ref[:, pl.ds((first + g) * HEAD_DIM, HEAD_DIM)] for g in range(count)], 0
+    )
+
+
+def load_state(ref, lanes):
+    return (
+        ref[HEAD_DIM : HEAD_DIM + 1, lanes],
+        ref[HEAD_DIM + 1 : HEAD_DIM + 2, lanes],
+        ref[0:HEAD_DIM, lanes],
+    )
+
+
+def store_state(ref, lanes, state):
+    top, total, summed = state
+    ref[0:HEAD_DIM, lanes] = summed
+    ref[HEAD_DIM : HEAD_DIM + 1, lanes] = top
+    ref[HEAD_DIM + 1 : HEAD_DIM + 2, lanes] = total
+
+
+def store_own(ref, lanes, state):
+    top, total, summed = state
+    ref[0:HEAD_DIM, lanes] = summed * (1.0 / total)
+    ref[HEAD_DIM : HEAD_DIM + 1, lanes] = top * SLOPE + jnp.log2(total)
+
+
+def store_sent(ref, lanes, state):
+    top, total, summed = state
+    log = top * SLOPE + jnp.log2(total)
+    high = log.astype(jnp.bfloat16).astype(jnp.float32)
+    rest = log - high
+    middle = rest.astype(jnp.bfloat16).astype(jnp.float32)
+    row = lax.broadcasted_iota(jnp.int32, (STATS, log.shape[1]), 0)
+    stats = jnp.where(
+        row == 0, high, jnp.where(row == 1, middle, jnp.where(row == 2, rest - middle, 0.0))
+    )
+    ref[0:HEAD_DIM, lanes] = (summed * (1.0 / total)).astype(jnp.bfloat16)
+    ref[HEAD_DIM : HEAD_DIM + STATS, lanes] = stats.astype(jnp.bfloat16)
+
+
+STORES = {"state": store_state, "own": store_own, "sent": store_sent}
+
+
+def attend_kernel(dims, blocks, q_xor, store, carried, after, len_ref, q_ref, *refs):
+    cache_rows, new_rows, step = dims
+    kv_refs, out_ref = refs[: len(blocks)], refs[-1]
+    me = lax.axis_index("ctx")
+    groups = q_ref.shape[1] // HEAD_DIM
+    for at in range(0, groups, step):
+        query = stacked_heads(q_ref, at, step)
+        lanes = pl.ds(at * new_rows, step * new_rows)
+        state = load_state(refs[len(blocks)], lanes) if carried else None
+        for block, kv_ref in zip(blocks, kv_refs):
+            ours = attend(
+                query, kv_ref, me ^ block, me ^ q_xor, len_ref[0], cache_rows, new_rows
+            )
+            state = ours if state is None else joined(state, ours)
+        STORES[store](out_ref, lanes, state)
+
+
+def merge_kernel(dims, columns, aliased, own_ref, got_ref, *refs):
+    cache_rows, new_rows, _ = dims
+    out_ref, block_ref, sem = refs[-3:]
+    first, own_first, groups = columns
+    pair = HEAD_DIM // new_rows
+    for at in range(0, groups, pair):
+        lanes = pl.ds(at * new_rows, pair * new_rows)
+        own_lanes = pl.ds((own_first + at) * new_rows, pair * new_rows)
+        stats = got_ref[HEAD_DIM : HEAD_DIM + STATS, lanes].astype(jnp.float32)
+        theirs = stats[0:1] + stats[1:2] + stats[2:3]
+        mine = own_ref[HEAD_DIM : HEAD_DIM + 1, own_lanes]
+        top = jnp.maximum(mine, theirs)
+        left, right = jnp.exp2(mine - top), jnp.exp2(theirs - top)
+        scale = 1.0 / (left + right)
+        whole = own_ref[0:HEAD_DIM, own_lanes] * (left * scale) + got_ref[
+            0:HEAD_DIM, lanes
+        ].astype(jnp.float32) * (right * scale)
+        turned = whole.T.astype(jnp.bfloat16)
+        for g in range(pair):
+            column = (at + g) * HEAD_DIM
+            block_ref[:, column : column + HEAD_DIM] = turned[g * new_rows : (g + 1) * new_rows, :]
+    copy = pltpu.make_async_copy(
+        block_ref, out_ref.at[:, pl.ds(first * HEAD_DIM, groups * HEAD_DIM)], sem
+    )
+    copy.start()
+    copy.wait()
+
+
+def pack_kernel(head, pieces, q_ref, ck_ref, cv_ref, nk_ref, nv_ref, *rest):
+    sems = rest[-1]
+    kv, q_refs = rest[-2 - pieces], rest[-1 - pieces : -1]
+    cache_rows, new_rows = ck_ref.shape[0], nk_ref.shape[0]
+    key_rows = cache_rows + new_rows
+    width = q_refs[0].shape[1]
+    columns = pl.ds(head * HEAD_DIM, HEAD_DIM)
+    copies = [
+        (source.at[:, columns], kv.at[pl.ds(at, rows), :])
+        for source, at, rows in (
+            (ck_ref, 0, cache_rows),
+            (nk_ref, cache_rows, new_rows),
+            (cv_ref, key_rows, cache_rows),
+            (nv_ref, key_rows + cache_rows, new_rows),
+        )
+    ] + [
+        (q_ref.at[:, pl.ds((head * pieces + piece) * width, width)], q_refs[piece])
+        for piece in range(pieces)
+    ]
+    handles = [
+        pltpu.make_async_copy(source, target, sems.at[n])
+        for n, (source, target) in enumerate(copies)
+    ]
+    for handle in handles:
+        handle.start()
+    for handle in handles:
+        handle.wait()
+
+
+def traded(value, xor):
+    count = lax.axis_size("ctx")
+    return lax.ppermute(value, "ctx", [(source, source ^ xor) for source in range(count)])
+
+
+def local_four(queries, cache_keys, cache_values, new_keys, new_values, prefix_len):
+    cache_rows, kv_width = cache_keys.shape
+    new_rows = queries.shape[0]
+    heads = kv_width // HEAD_DIM
+    groups = queries.shape[1] // kv_width
+    key_rows = cache_rows + new_rows
+    dims = (cache_rows, new_rows, STEP)
+    bf16, f32 = jnp.bfloat16, jnp.float32
+    shape = jax.ShapeDtypeStruct
+    arguments = [
+        pltpu.with_memory_space_constraint(argument, pltpu.HBM)
+        for argument in (queries, cache_keys, cache_values, new_keys, new_values)
+    ]
+
+    def pack(head, pieces, after):
+        return pl.pallas_call(
+            functools.partial(pack_kernel, head, pieces),
+            out_shape=[shape((2 * key_rows, HEAD_DIM), bf16)]
+            + [shape((new_rows, groups * HEAD_DIM // pieces), bf16)] * pieces,
+            in_specs=[HBM] * 5 + [ANY] * len(after),
+            out_specs=[ANY] * (1 + pieces),
+            scratch_shapes=[pltpu.SemaphoreType.DMA((4 + pieces,))],
+            name="pack",
+        )(*arguments, *after)
+
+    def work(query, blocks, q_xor, store, state=None, after=()):
+        rows = query.shape[1] // HEAD_DIM * new_rows
+        pairs = key_rows * rows * len(blocks)
+        out = shape((HEAD_DIM + STATS, rows), bf16) if store == "sent" else shape((HEAD_DIM + 8, rows), f32)
+        carried = () if state is None else (state,)
+        return pl.pallas_call(
+            functools.partial(
+                attend_kernel, dims, tuple(b for b, _ in blocks), q_xor, store, bool(carried), len(after)
+            ),
+            out_shape=out,
+            in_specs=[SMEM] + [VMEM] * (1 + len(blocks) + len(carried)) + [ANY] * len(after),
+            out_specs=VMEM,
+            compiler_params=pltpu.CompilerParams(vmem_limit_bytes=LIMIT),
+            cost_estimate=pl.CostEstimate(
+                flops=4 * HEAD_DIM * pairs, bytes_accessed=1 << 20, transcendentals=pairs
+            ),
+            name="work",
+        )(prefix_len, query, *[ref for _, ref in blocks], *carried, *after)
+
+    def merge(own, got, columns, out=None, after=()):
+        aliased = () if out is None else (out,)
+        return pl.pallas_call(
+            functools.partial(merge_kernel, dims, columns, bool(aliased)),
+            out_shape=shape(queries.shape, bf16),
+            in_specs=[VMEM] * 2 + [HBM] * len(aliased) + [ANY] * len(after),
+            out_specs=HBM,
+            scratch_shapes=[
+                pltpu.VMEM((new_rows, columns[2] * HEAD_DIM), bf16),
+                pltpu.SemaphoreType.DMA(()),
+            ],
+            compiler_params=pltpu.CompilerParams(vmem_limit_bytes=LIMIT),
+            input_output_aliases={2: 0} if aliased else {},
+            name="merge",
+        )(own, got, *aliased, *after)
+
+    half = groups // 2
+    kv1, q1 = pack(1, 1, ())
+    far_kv1 = traded(kv1, 2)
+    kv0, q0a, q0b = pack(0, 2, (kv1,))
+    far_q1 = traded(q1, 1)
+    far_kv0 = traded(kv0, 1)
+    far_q0 = [traded(q0a, 2), traded(q0b, 2)]
+    mine1 = work(q1, [(0, kv1)], 0, "state", after=(kv0,))
+    mine0 = [work(q, [(0, kv0)], 0, "state", after=(mine1,)) for q in (q0a, q0b)]
+    theirs1 = work(far_q1, [(0, kv1)], 1, "state", after=tuple(mine0))
+    sent1 = work(far_q1, [(2, far_kv1)], 1, "sent", state=theirs1)
+    got1 = traded(sent1, 1)
+    own1 = work(q1, [(2, far_kv1)], 0, "own", state=mine1, after=(sent1,))
+    own0 = [
+        work(q, [(1, far_kv0)], 0, "own", state=state, after=(own1,))
+        for q, state in zip((q0a, q0b), mine0)
+    ]
+    sent0a = work(far_q0[0], [(0, kv0), (1, far_kv0)], 2, "sent", after=tuple(own0))
+    got0a = traded(sent0a, 2)
+    sent0b = work(far_q0[1], [(0, kv0), (1, far_kv0)], 2, "sent", after=(sent0a,))
+    got0b = traded(sent0b, 2)
+    out = merge(own1, got1, (groups, 0, groups), after=(sent0b,))
+    out = merge(own0[0], got0a, (0, 0, half), out)
+    return merge(own0[1], got0b, (half, 0, half), out)
 
 
 def passed_along(value, axis, steps):
@@ -53,7 +310,7 @@
     )
 
 
-def local(queries, cache_keys, cache_values, new_keys, new_values, prefix_len):
+def local_ring(queries, cache_keys, cache_values, new_keys, new_values, prefix_len):
     length = prefix_len[0]
     cycle_size = lax.axis_size("ctx")
     my_index = lax.axis_index("ctx")
@@ -104,4 +361,5 @@
         P("dp"),
     )
     out_specs = P(("dp", "ctx"), "tp")
+    local = local_four if mesh.shape["ctx"] == 4 else local_ring
     return jax.shard_map(local, mesh=mesh, in_specs=in_specs, out_specs=out_specs, check_vma=False)

time: 65.1 us -> 62.6 us (0.962)
  Pallas kernels: 0 us -> 39.4 us
  waiting for transfers between devices: 44 us -> 8.57 us
  starting transfers between devices: 3.19 us -> 12.4 us
  other arithmetic: 8.16 us -> 0 us
  matrix products: 7.3 us -> 0 us
    pallas_call x0 -> x15, Pallas kernels: none -> 39.4 us  [the longest x2 28.1 us: pack(): pl.pallas_call(functools.partial(pack_kernel, head, pieces), out_shape=[s...]
    ppermute x3 -> x8, waiting for transfers between devices: 44 us -> 8.57 us  [traded(): lax.ppermute(value, 'ctx', [(source, source ^ xor) for source in range(co...]
    ppermute x3 -> x8, starting transfers between devices: 3.19 us -> 12.4 us  [traded(): lax.ppermute(value, 'ctx', [(source, source ^ xor) for source in range(co...]
    dot_general x8 -> x0, matrix products: 7.3 us -> none  [the longest x4 4.89 us: softmax_block(): jnp.einsum('hrk,hkd->hrd', weights.astype(jnp.bfloat16), kv_block[1], pre...]
    reduce_sum x4 -> x0, other arithmetic: 2.56 us -> none  [softmax_block(): new_total = old_total * rescale + jnp.sum(weights, -1)]
    concatenate x2 -> x0, other arithmetic: 2.03 us -> none  [the longest x1 1.03 us: local(): jnp.concatenate([cache_values, new_values], 0)]
    lt x4 -> x0, other arithmetic: 1.96 us -> none  [allowed_for(): cache_pos < length]
    select_n x4 -> x0, other arithmetic: 1.22 us -> none  [allowed_for(): jnp.where((key_index < cache_rows)[None, :], (cache_pos < length)[None, :...]
  transfers between devices with their start and end apart: 3 -> 8, of which waited for: 3 -> 2; matrix products, arithmetic and copies ran while one was open for 4% -> 0% of each run, Pallas kernels for 0% -> 39%
where the time goes in v2:
time: 62.6 us; the launch traced here: 62.4 us
  Pallas kernels  39.4 us (63%)
  starting transfers between devices  12.4 us (20%)
  waiting for transfers between devices  8.57 us (14%)
  local copies, waits for them, and re-layouts  1.19 us (2%)
  between operations  0.85 us (1%)
    pallas_call x2, Pallas kernels, pack(): pl.pallas_call(functools.partial(pack_kernel, head, pieces), out_shape=[s...  28.1 us
    ppermute x8, starting transfers between devices, traded(): lax.ppermute(value, 'ctx', [(source, source ^ xor) for source in range(co...  12.4 us
    pallas_call x10, Pallas kernels, work(): pl.pallas_call(functools.partial(attend_kernel, dims, tuple((b for b, _ i...  8.97 us
    ppermute x8, waiting for transfers between devices, traded(): lax.ppermute(value, 'ctx', [(source, source ^ xor) for source in range(co...  8.57 us
    pallas_call x3, Pallas kernels, merge(): pl.pallas_call(functools.partial(merge_kernel, dims, columns, bool(aliase...  2.33 us
  transfers between devices with their start and end apart: 8, of which 2 were waited for; matrix products, arithmetic and copies ran while one was open for 0% of the time, Pallas kernels for 39%

profile of v2, /device:TPU:0, one launch (start us, length us, event | category | flops | bytes accessed | tf_op | source)
XLA Modules:
  0.0 62.4 jit_solution(15721357524415249460)
XLA Ops:
  0.0 14.0 %pack.2 = (bf16[1152,128]{1,0:T(8,128)(2,1)}, bf16[64,1024]{1,0:T(8,128)(2,1)}) custom-call(bf16[64,2048]{1,0:T(8,128)(2,1)} %q_ref.3, bf16[512,256]{1,0:T(8,128)(2,1)} %ck_ref.3, bf16[512,256]{1,0:T(8,128)(2,1)} %cv_ref.3, bf16[64,256]{1,0:T(8,128)(2,1)} %nk_ref.3, bf16[64,256]{1,0:T(8,128)(2,1)} %nv_ref.3), custom_call_target="tpu_custom_call" | custom-call | tf_op jit(solution)/shard_map/pack/pallas_call | solution.py:195
  14.1 0.0 copy-start.3
  14.1 0.0 copy-start.2
  14.1 4.1 %collective-permute-start.1 = (bf16[1152,128]{1,0:T(8,128)(2,1)}, bf16[1152,128]{1,0:T(8,128)(2,1)S(1)}, u32[]{:S(2)}, u32[]{:S(2)}) collective-permute-start(bf16[1152,128]{1,0:T(8,128)(2,1)} %get-tuple-element.10.rest_0_.refs_0_), channel_id=1, source_target_pairs={{0,16},{8,24},{16,0},{24,8},{1,17},{9,25},{17,1},{25,9},{2,18},{10... | collective-permute-start | bytes 884744 | tf_op jit(solution)/shard_map/ppermute | solution.py:177
  18.2 14.1 %pack.3 = (bf16[1152,128]{1,0:T(8,128)(2,1)}, bf16[64,512]{1,0:T(8,128)(2,1)}, bf16[64,512]{1,0:T(8,128)(2,1)}) custom-call(bf16[64,2048]{1,0:T(8,128)(2,1)} %q_ref.3, bf16[512,256]{1,0:T(8,128)(2,1)} %ck_ref.3, bf16[512,256]{1,0:T(8,128)(2,1)} %cv_ref.3, bf16[64,256]{1,0:T(8,128)(2,1)} %nk_ref.3, bf16[64,256]{1,0:T(8,128)(2,1)} %nv_ref.3, ...), custom_call_target="tpu_custom_call" | custom-call | tf_op jit(solution)/shard_map/pack/pallas_call | solution.py:195
  32.2 1.6 %collective-permute-start = (bf16[1152,128]{1,0:T(8,128)(2,1)}, bf16[1152,128]{1,0:T(8,128)(2,1)S(1)}, u32[]{:S(2)}, u32[]{:S(2)}) collective-permute-start(bf16[1152,128]{1,0:T(8,128)(2,1)} %get-tuple-element.12.refs_1_.refs_0_), channel_id=1, source_target_pairs={{0,8},{8,0},{16,24},{24,16},{1,9},{9,1},{17,25},{25,17},{2,10},{10... | collective-permute-start | bytes 884744 | tf_op jit(solution)/shard_map/ppermute | solution.py:177
  33.9 0.0 copy-done.3
  33.9 0.4 collective-permute-start.2
  34.3 0.0 collective-permute-start.4
  34.4 2.9 %collective-permute-start.3 = (bf16[64,512]{1,0:T(8,128)(2,1)}, bf16[64,512]{1,0:T(8,128)(2,1)S(1)}, u32[]{:S(2)}, u32[]{:S(2)}) collective-permute-start(bf16[64,512]{1,0:T(8,128)(2,1)} %get-tuple-element.11.q_ref), channel_id=1, source_target_pairs={{0,16},{8,24},{16,0},{24,8},{1,17},{9,25},{17,1},{25,9},{2,18},{10... | collective-permute-start | bytes 196616 | tf_op jit(solution)/shard_map/ppermute | solution.py:177
  37.9 0.0 copy-done.2
  37.9 0.0 copy-start
  37.9 1.0 %copy-done = bf16[1152,128]{1,0:T(8,128)(2,1)S(1)} copy-done((bf16[1152,128]{1,0:T(8,128)(2,1)S(1)}, bf16[1152,128]{1,0:T(8,128)(2,1)}, u32[]{:S(2)}) %copy-start) | copy-done | bytes 294936
  38.9 0.0 copy-start.1
  38.9 0.0 copy-start.5
  38.9 1.1 %work.10.refs_1_ = f32[136,512]{1,0:T(8,128)S(1)} custom-call(s32[1]{0:T(128)S(6)} %copy.11.len_ref, bf16[64,1024]{1,0:T(8,128)(2,1)S(1)} %copy-done.3, bf16[1152,128]{1,0:T(8,128)(2,1)S(1)} %copy-done.2, bf16[1152,128]{1,0:T(8,128)(2,1)S(1)} %copy-done), custom_call_target="tpu_custom_call" | custom-call | flops 150994944 | bytes 1048576 | tf_op jit(solution)/shard_map/work/pallas_call | solution.py:210
  40.0 0.0 copy-done.1
  40.0 0.0 copy-done.5
  40.0 0.0 copy-start.4
  40.0 0.6 work.12.refs_1_
  40.6 0.2 copy-done.4
  40.8 0.6 work.11.refs_2_.refs_1_
  41.5 5.2 %collective-permute-done.2.q_ref = bf16[64,1024]{1,0:T(8,128)(2,1)S(1)} collective-permute-done((bf16[64,1024]{1,0:T(8,128)(2,1)S(1)}, bf16[64,1024]{1,0:T(8,128)(2,1)S(1)}, u32[]{:S(2)}, u32[]{:S(2)}) %collective-permute-start.2) | collective-permute-done | bytes 131104 | tf_op jit(solution)/shard_map/ppermute | solution.py:177
  46.6 1.1 %work.13.refs_1_ = f32[136,512]{1,0:T(8,128)S(1)} custom-call(s32[1]{0:T(128)S(6)} %copy.11.len_ref, bf16[64,1024]{1,0:T(8,128)(2,1)S(1)} %collective-permute-done.2.q_ref, bf16[1152,128]{1,0:T(8,128)(2,1)S(1)} %copy-done.2, f32[136,256]{1,0:T(8,128)S(1)} %work.12.refs_1_, f32[136,256]{1,0:T(8,128)S(1)} %work.11.refs_2_.refs_1_), custom_call_target="tpu_custom_call" | custom-call | flops 150994944 | bytes 1048576 | tf_op jit(solution)/shard_map/work/pallas_call | solution.py:210
  47.7 0.0 collective-permute-done.1.refs_0_
  47.7 1.1 %work.14.refs_2_ = bf16[144,512]{1,0:T(8,128)(2,1)S(1)} custom-call(s32[1]{0:T(128)S(6)} %copy.11.len_ref, bf16[64,1024]{1,0:T(8,128)(2,1)S(1)} %collective-permute-done.2.q_ref, bf16[1152,128]{1,0:T(8,128)(2,1)S(1)} %collective-permute-done.1.refs_0_, f32[136,512]{1,0:T(8,128)S(1)} %work.13.refs_1_), custom_call_target="tpu_custom_call" | custom-call | flops 150994944 | bytes 1048576 | tf_op jit(solution)/shard_map/work/pallas_call | solution.py:210
  48.8 0.2 collective-permute-start.7
  49.0 1.1 %work.15.refs_2_.own_ref = f32[136,512]{1,0:T(8,128)S(1)} custom-call(s32[1]{0:T(128)S(6)} %copy.11.len_ref, bf16[64,1024]{1,0:T(8,128)(2,1)S(1)} %copy-done.3, bf16[1152,128]{1,0:T(8,128)(2,1)S(1)} %collective-permute-done.1.refs_0_, f32[136,512]{1,0:T(8,128)S(1)} %work.10.refs_1_, bf16[144,512]{1,0:T(8,128)(2,1)S(1)} %work.14.refs_2_), custom_call_target="tpu_custom_call" | custom-call | flops 150994944 | bytes 1048576 | tf_op jit(solution)/shard_map/work/pallas_call | solution.py:210
  50.1 0.0 collective-permute-done.refs_0_.refs_1_
  50.2 0.6 work.17.refs_2_.own_ref
  50.8 0.6 work.16.refs_3_.own_ref
  51.4 0.0 collective-permute-done.4.q_ref
  51.4 1.1 %work.18.refs_2_ = bf16[144,256]{1,0:T(8,128)(2,1)S(1)} custom-call(s32[1]{0:T(128)S(6)} %copy.11.len_ref, bf16[64,512]{1,0:T(8,128)(2,1)S(1)} %collective-permute-done.4.q_ref, bf16[1152,128]{1,0:T(8,128)(2,1)S(1)} %copy-done.1, bf16[1152,128]{1,0:T(8,128)(2,1)S(1)} %collective-permute-done.refs_0_.refs_1_, f32[136,256]{1,0:T(8,128)S(1)} %work.17.refs_2_.own_ref, ...), custom_call_target="tpu_custom_call" | custom-call | flops 150994944 | bytes 1048576 | tf_op jit(solution)/shard_map/work/pallas_call | solution.py:210
  52.5 1.8 %collective-permute-start.6 = (bf16[144,256]{1,0:T(8,128)(2,1)S(1)}, bf16[144,256]{1,0:T(8,128)(2,1)S(1)}, u32[]{:S(2)}, u32[]{:S(2)}) collective-permute-start(bf16[144,256]{1,0:T(8,128)(2,1)S(1)} %work.18.refs_2_), channel_id=1, source_target_pairs={{0,16},{8,24},{16,0},{24,8},{1,17},{9,25},{17,1},{25,9},{2,18},{10... | collective-permute-start | bytes 221192 | tf_op jit(solution)/shard_map/ppermute | solution.py:177
  54.3 0.0 collective-permute-done.3.q_ref
  54.3 1.1 %work.19.refs_0_ = bf16[144,256]{1,0:T(8,128)(2,1)S(1)} custom-call(s32[1]{0:T(128)S(6)} %copy.11.len_ref, bf16[64,512]{1,0:T(8,128)(2,1)S(1)} %collective-permute-done.3.q_ref, bf16[1152,128]{1,0:T(8,128)(2,1)S(1)} %copy-done.1, bf16[1152,128]{1,0:T(8,128)(2,1)S(1)} %collective-permute-done.refs_0_.refs_1_, bf16[144,256]{1,0:T(8,128)(2,1)S(1)} %work.18.refs_2_), custom_call_target="tpu_custom_call" | custom-call | flops 150994944 | bytes 1048576 | tf_op jit(solution)/shard_map/work/pallas_call | solution.py:210
  55.4 1.2 %collective-permute-start.5 = (bf16[144,256]{1,0:T(8,128)(2,1)S(1)}, bf16[144,256]{1,0:T(8,128)(2,1)S(1)}, u32[]{:S(2)}, u32[]{:S(2)}) collective-permute-start(bf16[144,256]{1,0:T(8,128)(2,1)S(1)} %work.19.refs_0_), channel_id=1, source_target_pairs={{0,16},{8,24},{16,0},{24,8},{1,17},{9,25},{17,1},{25,9},{2,18},{10... | collective-permute-start | bytes 221192 | tf_op jit(solution)/shard_map/ppermute | solution.py:177
  56.7 0.0 collective-permute-done.7.got_ref
  56.7 0.8 %merge.3.refs_0_ = bf16[64,2048]{1,0:T(8,128)(2,1)} custom-call(f32[136,512]{1,0:T(8,128)S(1)} %work.15.refs_2_.own_ref, bf16[144,512]{1,0:T(8,128)(2,1)S(1)} %collective-permute-done.7.got_ref, bf16[144,256]{1,0:T(8,128)(2,1)S(1)} %work.19.refs_0_), custom_call_target="tpu_custom_call" | custom-call | tf_op jit(solution)/shard_map/merge/pallas_call | solution.py:226
  57.5 3.4 %collective-permute-done.6.got_ref = bf16[144,256]{1,0:T(8,128)(2,1)S(1)} collective-permute-done((bf16[144,256]{1,0:T(8,128)(2,1)S(1)}, bf16[144,256]{1,0:T(8,128)(2,1)S(1)}, u32[]{:S(2)}, u32[]{:S(2)}) %collective-permute-start.6) | collective-permute-done | bytes 73760 | tf_op jit(solution)/shard_map/ppermute | solution.py:177
  60.9 0.8 %merge.4.refs_0_ = bf16[64,2048]{1,0:T(8,128)(2,1)} custom-call(f32[136,256]{1,0:T(8,128)S(1)} %work.17.refs_2_.own_ref, bf16[144,256]{1,0:T(8,128)(2,1)S(1)} %collective-permute-done.6.got_ref, bf16[64,2048]{1,0:T(8,128)(2,1)} %merge.3.refs_0_), custom_call_target="tpu_custom_call", output_to_operand_aliasing={{}: (2, {})} | custom-call | tf_op jit(solution)/shard_map/merge/pallas_call | solution.py:226
  61.6 0.0 collective-permute-done.5.got_ref
  61.7 0.8 %merge.5 = bf16[64,2048]{1,0:T(8,128)(2,1)} custom-call(f32[136,256]{1,0:T(8,128)S(1)} %work.16.refs_3_.own_ref, bf16[144,256]{1,0:T(8,128)(2,1)S(1)} %collective-permute-done.5.got_ref, bf16[64,2048]{1,0:T(8,128)(2,1)} %merge.4.refs_0_), custom_call_target="tpu_custom_call", output_to_operand_aliasing={{}: (2, {})} | custom-call | tf_op jit(solution)/shard_map/merge/pallas_call | solution.py:226
Async XLA Ops:
  14.1 19.8 %copy-start.3 = (bf16[64,1024]{1,0:T(8,128)(2,1)S(1)}, bf16[64,1024]{1,0:T(8,128)(2,1)}, u32[]{:S(2)}) copy-start(bf16[64,1024]{1,0:T(8,128)(2,1)} %get-tuple-element.13.q_ref) | copy-start | bytes 393220
  14.1 23.9 %copy-start.2 = (bf16[1152,128]{1,0:T(8,128)(2,1)S(1)}, bf16[1152,128]{1,0:T(8,128)(2,1)}, u32[]{:S(2)}) copy-start(bf16[1152,128]{1,0:T(8,128)(2,1)} %get-tuple-element.10.rest_0_.refs_0_) | copy-start | bytes 884740
  14.1 33.6 %collective-permute-start.1 = (bf16[1152,128]{1,0:T(8,128)(2,1)}, bf16[1152,128]{1,0:T(8,128)(2,1)S(1)}, u32[]{:S(2)}, u32[]{:S(2)}) collective-permute-start(bf16[1152,128]{1,0:T(8,128)(2,1)} %get-tuple-element.10.rest_0_.refs_0_), channel_id=1, source_target_pairs={{0,16},{8,24},{16,0},{24,8},{1,17},{9,25},{17,1},{25,9},{2,18},{10... | collective-permute-start | bytes 884744 | tf_op jit(solution)/shard_map/ppermute | solution.py:177
  32.2 17.9 %collective-permute-start = (bf16[1152,128]{1,0:T(8,128)(2,1)}, bf16[1152,128]{1,0:T(8,128)(2,1)S(1)}, u32[]{:S(2)}, u32[]{:S(2)}) collective-permute-start(bf16[1152,128]{1,0:T(8,128)(2,1)} %get-tuple-element.12.refs_1_.refs_0_), channel_id=1, source_target_pairs={{0,8},{8,0},{16,24},{24,16},{1,9},{9,1},{17,25},{25,17},{2,10},{10... | collective-permute-start | bytes 884744 | tf_op jit(solution)/shard_map/ppermute | solution.py:177
  33.9 12.7 %collective-permute-start.2 = (bf16[64,1024]{1,0:T(8,128)(2,1)S(1)}, bf16[64,1024]{1,0:T(8,128)(2,1)S(1)}, u32[]{:S(2)}, u32[]{:S(2)}) collective-permute-start(bf16[64,1024]{1,0:T(8,128)(2,1)S(1)} %copy-done.3), channel_id=1, source_target_pairs={{0,8},{8,0},{16,24},{24,16},{1,9},{9,1},{17,25},{25,17},{2,10},{10... | collective-permute-start | bytes 393224 | tf_op jit(solution)/shard_map/ppermute | solution.py:177
  34.3 17.1 %collective-permute-start.4 = (bf16[64,512]{1,0:T(8,128)(2,1)}, bf16[64,512]{1,0:T(8,128)(2,1)S(1)}, u32[]{:S(2)}, u32[]{:S(2)}) collective-permute-start(bf16[64,512]{1,0:T(8,128)(2,1)} %get-tuple-element.14.q_ref), channel_id=1, source_target_pairs={{0,16},{8,24},{16,0},{24,8},{1,17},{9,25},{17,1},{25,9},{2,18},{10... | collective-permute-start | bytes 196616 | tf_op jit(solution)/shard_map/ppermute | solution.py:177
  34.4 20.0 %collective-permute-start.3 = (bf16[64,512]{1,0:T(8,128)(2,1)}, bf16[64,512]{1,0:T(8,128)(2,1)S(1)}, u32[]{:S(2)}, u32[]{:S(2)}) collective-permute-start(bf16[64,512]{1,0:T(8,128)(2,1)} %get-tuple-element.11.q_ref), channel_id=1, source_target_pairs={{0,16},{8,24},{16,0},{24,8},{1,17},{9,25},{17,1},{25,9},{2,18},{10... | collective-permute-start | bytes 196616 | tf_op jit(solution)/shard_map/ppermute | solution.py:177
  37.9 1.0 %copy-start = (bf16[1152,128]{1,0:T(8,128)(2,1)S(1)}, bf16[1152,128]{1,0:T(8,128)(2,1)}, u32[]{:S(2)}) copy-start(bf16[1152,128]{1,0:T(8,128)(2,1)} %get-tuple-element.12.refs_1_.refs_0_) | copy-start | bytes 884740
  38.9 1.1 %copy-start.1 = (bf16[1152,128]{1,0:T(8,128)(2,1)S(1)}, bf16[1152,128]{1,0:T(8,128)(2,1)}, u32[]{:S(2)}) copy-start(bf16[1152,128]{1,0:T(8,128)(2,1)} %get-tuple-element.12.refs_1_.refs_0_) | copy-start | bytes 884740
  38.9 1.1 %copy-start.5 = (bf16[64,512]{1,0:T(8,128)(2,1)S(1)}, bf16[64,512]{1,0:T(8,128)(2,1)}, u32[]{:S(2)}) copy-start(bf16[64,512]{1,0:T(8,128)(2,1)} %get-tuple-element.14.q_ref) | copy-start | bytes 196612
  40.0 0.8 %copy-start.4 = (bf16[64,512]{1,0:T(8,128)(2,1)S(1)}, bf16[64,512]{1,0:T(8,128)(2,1)}, u32[]{:S(2)}) copy-start(bf16[64,512]{1,0:T(8,128)(2,1)} %get-tuple-element.11.q_ref) | copy-start | bytes 196612
  48.8 7.9 %collective-permute-start.7 = (bf16[144,512]{1,0:T(8,128)(2,1)S(1)}, bf16[144,512]{1,0:T(8,128)(2,1)S(1)}, u32[]{:S(2)}, u32[]{:S(2)}) collective-permute-start(bf16[144,512]{1,0:T(8,128)(2,1)S(1)} %work.14.refs_2_), channel_id=1, source_target_pairs={{0,8},{8,0},{16,24},{24,16},{1,9},{9,1},{17,25},{25,17},{2,10},{10... | collective-permute-start | bytes 442376 | tf_op jit(solution)/shard_map/ppermute | solution.py:177
  52.5 8.3 %collective-permute-start.6 = (bf16[144,256]{1,0:T(8,128)(2,1)S(1)}, bf16[144,256]{1,0:T(8,128)(2,1)S(1)}, u32[]{:S(2)}, u32[]{:S(2)}) collective-permute-start(bf16[144,256]{1,0:T(8,128)(2,1)S(1)} %work.18.refs_2_), channel_id=1, source_target_pairs={{0,16},{8,24},{16,0},{24,8},{1,17},{9,25},{17,1},{25,9},{2,18},{10... | collective-permute-start | bytes 221192 | tf_op jit(solution)/shard_map/ppermute | solution.py:177
  55.4 6.2 %collective-permute-start.5 = (bf16[144,256]{1,0:T(8,128)(2,1)S(1)}, bf16[144,256]{1,0:T(8,128)(2,1)S(1)}, u32[]{:S(2)}, u32[]{:S(2)}) collective-permute-start(bf16[144,256]{1,0:T(8,128)(2,1)S(1)} %work.19.refs_0_), channel_id=1, source_target_pairs={{0,16},{8,24},{16,0},{24,8},{1,17},{9,25},{17,1},{25,9},{2,18},{10... | collective-permute-start | bytes 221192 | tf_op jit(solution)/shard_map/ppermute | solution.py:177

commit v3 on v2

--- a/solution.py
+++ b/solution.py
@@ -194,10 +194,10 @@
     def pack(head, pieces, after):
         return pl.pallas_call(
             functools.partial(pack_kernel, head, pieces),
-            out_shape=[shape((2 * key_rows, HEAD_DIM), bf16)]
-            + [shape((new_rows, groups * HEAD_DIM // pieces), bf16)] * pieces,
+            out_shape=[pltpu.VMEM((2 * key_rows, HEAD_DIM), bf16)]
+            + [pltpu.VMEM((new_rows, groups * HEAD_DIM // pieces), bf16)] * pieces,
             in_specs=[HBM] * 5 + [ANY] * len(after),
-            out_specs=[ANY] * (1 + pieces),
+            out_specs=[VMEM] * (1 + pieces),
             scratch_shapes=[pltpu.SemaphoreType.DMA((4 + pieces,))],
             name="pack",
         )(*arguments, *after)
@@ -205,7 +205,10 @@
     def work(query, blocks, q_xor, store, state=None, after=()):
         rows = query.shape[1] // HEAD_DIM * new_rows
         pairs = key_rows * rows * len(blocks)
-        out = shape((HEAD_DIM + STATS, rows), bf16) if store == "sent" else shape((HEAD_DIM + 8, rows), f32)
+        if store == "sent":
+            out = pltpu.VMEM((HEAD_DIM + STATS, rows), bf16)
+        else:
+            out = pltpu.VMEM((HEAD_DIM + 8, rows), f32)
         carried = () if state is None else (state,)
         return pl.pallas_call(
             functools.partial(
@@ -216,7 +219,7 @@
             out_specs=VMEM,
             compiler_params=pltpu.CompilerParams(vmem_limit_bytes=LIMIT),
             cost_estimate=pl.CostEstimate(
-                flops=4 * HEAD_DIM * pairs, bytes_accessed=1 << 20, transcendentals=pairs
+                flops=4 * HEAD_DIM * pairs * 40, bytes_accessed=1 << 20, transcendentals=pairs
             ),
             name="work",
         )(prefix_len, query, *[ref for _, ref in blocks], *carried, *after)
@@ -237,30 +240,22 @@
             name="merge",
         )(own, got, *aliased, *after)
 
-    half = groups // 2
-    kv1, q1 = pack(1, 1, ())
-    far_kv1 = traded(kv1, 2)
-    kv0, q0a, q0b = pack(0, 2, (kv1,))
-    far_q1 = traded(q1, 1)
-    far_kv0 = traded(kv0, 1)
-    far_q0 = [traded(q0a, 2), traded(q0b, 2)]
-    mine1 = work(q1, [(0, kv1)], 0, "state", after=(kv0,))
-    mine0 = [work(q, [(0, kv0)], 0, "state", after=(mine1,)) for q in (q0a, q0b)]
-    theirs1 = work(far_q1, [(0, kv1)], 1, "state", after=tuple(mine0))
+    kv0, q0 = pack(0, 1, ())
+    far_kv0, far_q0 = traded(kv0, 1), traded(q0, 2)
+    kv1, q1 = pack(1, 1, (kv0,))
+    far_kv1, far_q1 = traded(kv1, 2), traded(q1, 1)
+    mine0 = work(q0, [(0, kv0)], 0, "state", after=(kv1,))
+    mine1 = work(q1, [(0, kv1)], 0, "state", after=(mine0,))
+    theirs0 = work(far_q0, [(0, kv0)], 2, "state", after=(mine1,))
+    sent0 = work(far_q0, [(1, far_kv0)], 2, "sent", state=theirs0)
+    got0 = traded(sent0, 2)
+    own0 = work(q0, [(1, far_kv0)], 0, "own", state=mine0, after=(sent0,))
+    theirs1 = work(far_q1, [(0, kv1)], 1, "state", after=(own0,))
     sent1 = work(far_q1, [(2, far_kv1)], 1, "sent", state=theirs1)
     got1 = traded(sent1, 1)
     own1 = work(q1, [(2, far_kv1)], 0, "own", state=mine1, after=(sent1,))
-    own0 = [
-        work(q, [(1, far_kv0)], 0, "own", state=state, after=(own1,))
-        for q, state in zip((q0a, q0b), mine0)
-    ]
-    sent0a = work(far_q0[0], [(0, kv0), (1, far_kv0)], 2, "sent", after=tuple(own0))
-    got0a = traded(sent0a, 2)
-    sent0b = work(far_q0[1], [(0, kv0), (1, far_kv0)], 2, "sent", after=(sent0a,))
-    got0b = traded(sent0b, 2)
-    out = merge(own1, got1, (groups, 0, groups), after=(sent0b,))
-    out = merge(own0[0], got0a, (0, 0, half), out)
-    return merge(own0[1], got0b, (half, 0, half), out)
+    out = merge(own0, got0, (0, 0, groups), after=(own1,))
+    return merge(own1, got1, (groups, 0, groups), out)
 
 
 def passed_along(value, axis, steps):

time: 62.6 us -> 34.8 us (0.56)
  Pallas kernels: 39.4 us -> 12.5 us
  starting transfers between devices: 12.4 us -> 9.59 us
  waiting for transfers between devices: 8.57 us -> 10.7 us
    pallas_call x2, Pallas kernels: 28.1 us -> 2.21 us  [pack(): pl.pallas_call(functools.partial(pack_kernel, head, pieces), out_shape=[p...]
    ppermute x8 -> x6, starting transfers between devices: 12.4 us -> 9.59 us  [traded(): lax.ppermute(value, 'ctx', [(source, source ^ xor) for source in range(co...]
    ppermute x8 -> x6, waiting for transfers between devices: 8.57 us -> 10.7 us  [traded(): lax.ppermute(value, 'ctx', [(source, source ^ xor) for source in range(co...]
    pallas_call x3 -> x2, Pallas kernels: 2.33 us -> 1.59 us  [merge(): pl.pallas_call(functools.partial(merge_kernel, dims, columns, bool(aliase...]
    pallas_call x10 -> x8, Pallas kernels: 8.97 us -> 8.71 us  [work(): pl.pallas_call(functools.partial(attend_kernel, dims, tuple((b for b, _ i...]
  transfers between devices with their start and end apart: 8 -> 6, of which waited for: 2 -> 2; matrix products, arithmetic and copies ran while one was open for 0% -> 0% of each run, Pallas kernels for 39% -> 31%
where the time goes in v3:
time: 34.8 us; the launch traced here: 34.6 us
  Pallas kernels  12.5 us (36%)
  waiting for transfers between devices  10.7 us (31%)
  starting transfers between devices  9.59 us (28%)
  local copies, waits for them, and re-layouts  0.96 us (3%)
  between operations  0.8 us (2%)
    ppermute x6, waiting for transfers between devices, traded(): lax.ppermute(value, 'ctx', [(source, source ^ xor) for source in range(co...  10.7 us
    ppermute x6, starting transfers between devices, traded(): lax.ppermute(value, 'ctx', [(source, source ^ xor) for source in range(co...  9.59 us
    pallas_call x8, Pallas kernels, work(): pl.pallas_call(functools.partial(attend_kernel, dims, tuple((b for b, _ i...  8.71 us
    pallas_call x2, Pallas kernels, pack(): pl.pallas_call(functools.partial(pack_kernel, head, pieces), out_shape=[p...  2.21 us
    pallas_call x2, Pallas kernels, merge(): pl.pallas_call(functools.partial(merge_kernel, dims, columns, bool(aliase...  1.59 us
    unnamed x6, local copies, waits for them, and re-layouts  0.96 us
  transfers between devices with their start and end apart: 6, of which 2 were waited for; matrix products, arithmetic and copies ran while one was open for 0% of the time, Pallas kernels for 31%

profile of v3, /device:TPU:0, one launch (start us, length us, event | category | flops | bytes accessed | tf_op | source)
XLA Modules:
  0.0 34.6 jit_solution(14306643829372719865)
XLA Ops:
  0.0 1.1 %pack.2 = (bf16[1152,128]{1,0:T(8,128)(2,1)S(1)}, bf16[64,1024]{1,0:T(8,128)(2,1)S(1)}) custom-call(bf16[64,2048]{1,0:T(8,128)(2,1)} %q_ref.3, bf16[512,256]{1,0:T(8,128)(2,1)} %ck_ref.3, bf16[512,256]{1,0:T(8,128)(2,1)} %cv_ref.3, bf16[64,256]{1,0:T(8,128)(2,1)} %nk_ref.3, bf16[64,256]{1,0:T(8,128)(2,1)} %nv_ref.3), custom_call_target="tpu_custom_call" | custom-call | tf_op jit(solution)/shard_map/pack/pallas_call | solution.py:195
  1.1 0.0 copy-start
  1.1 4.1 %collective-permute-start.3 = (bf16[64,1024]{1,0:T(8,128)(2,1)S(1)}, bf16[64,1024]{1,0:T(8,128)(2,1)S(1)}, u32[]{:S(2)}, u32[]{:S(2)}) collective-permute-start(bf16[64,1024]{1,0:T(8,128)(2,1)S(1)} %get-tuple-element.12.q_ref), channel_id=1, source_target_pairs={{0,16},{8,24},{16,0},{24,8},{1,17},{9,25},{17,1},{25,9},{2,18},{10... | collective-permute-start | bytes 393224 | tf_op jit(solution)/shard_map/ppermute | solution.py:177
  5.2 1.6 %collective-permute-start.2 = (bf16[1152,128]{1,0:T(8,128)(2,1)S(1)}, bf16[1152,128]{1,0:T(8,128)(2,1)S(1)}, u32[]{:S(2)}, u32[]{:S(2)}) collective-permute-start(bf16[1152,128]{1,0:T(8,128)(2,1)S(1)} %get-tuple-element.9.rest_0_.refs_0_), channel_id=1, source_target_pairs={{0,8},{8,0},{16,24},{24,16},{1,9},{9,1},{17,25},{25,17},{2,10},{10... | collective-permute-start | bytes 884744 | tf_op jit(solution)/shard_map/ppermute | solution.py:177
  6.8 0.0 copy-done
  6.8 1.1 %pack.3 = (bf16[1152,128]{1,0:T(8,128)(2,1)S(1)}, bf16[64,1024]{1,0:T(8,128)(2,1)S(1)}) custom-call(bf16[64,2048]{1,0:T(8,128)(2,1)} %q_ref.3, bf16[512,256]{1,0:T(8,128)(2,1)} %ck_ref.3, bf16[512,256]{1,0:T(8,128)(2,1)} %cv_ref.3, bf16[64,256]{1,0:T(8,128)(2,1)} %nk_ref.3, bf16[64,256]{1,0:T(8,128)(2,1)} %nv_ref.3, bf16[1152,128]{1,0:T(8,128)(2,1)} %copy-done), custom_call_target="tpu_custom_call" | custom-call | tf_op jit(solution)/shard_map/pack/pallas_call | solution.py:195
  7.9 0.5 %collective-permute-start.1 = (bf16[64,1024]{1,0:T(8,128)(2,1)S(1)}, bf16[64,1024]{1,0:T(8,128)(2,1)S(1)}, u32[]{:S(2)}, u32[]{:S(2)}) collective-permute-start(bf16[64,1024]{1,0:T(8,128)(2,1)S(1)} %get-tuple-element.10.q_ref), channel_id=1, source_target_pairs={{0,8},{8,0},{16,24},{24,16},{1,9},{9,1},{17,25},{25,17},{2,10},{10... | collective-permute-start | bytes 393224 | tf_op jit(solution)/shard_map/ppermute | solution.py:177
  8.4 0.2 collective-permute-start
  9.3 0.0 copy-start.1
  9.3 1.0 %copy-done.1 = bf16[1152,128]{1,0:T(8,128)(2,1)S(1)} copy-done((bf16[1152,128]{1,0:T(8,128)(2,1)S(1)}, bf16[1152,128]{1,0:T(8,128)(2,1)}, u32[]{:S(2)}) %copy-start.1) | copy-done | bytes 294936
  10.2 1.1 %work.8.refs_1_ = f32[136,512]{1,0:T(8,128)S(1)} custom-call(s32[1]{0:T(128)S(6)} %copy.9.len_ref, bf16[64,1024]{1,0:T(8,128)(2,1)S(1)} %get-tuple-element.12.q_ref, bf16[1152,128]{1,0:T(8,128)(2,1)S(1)} %copy-done.1, bf16[1152,128]{1,0:T(8,128)(2,1)S(1)} %get-tuple-element.11.refs_1_.refs_0_), custom_call_target="tpu_custom_call" | custom-call | flops 6039797760 | bytes 1048576 | tf_op jit(solution)/shard_map/work/pallas_call | solution.py:213
  11.3 0.0 copy-start.2
  11.3 1.1 %work.9.refs_1_ = f32[136,512]{1,0:T(8,128)S(1)} custom-call(s32[1]{0:T(128)S(6)} %copy.9.len_ref, bf16[64,1024]{1,0:T(8,128)(2,1)S(1)} %get-tuple-element.10.q_ref, bf16[1152,128]{1,0:T(8,128)(2,1)S(1)} %get-tuple-element.11.refs_1_.refs_0_, f32[136,512]{1,0:T(8,128)S(1)} %work.8.refs_1_), custom_call_target="tpu_custom_call" | custom-call | flops 6039797760 | bytes 1048576 | tf_op jit(solution)/shard_map/work/pallas_call | solution.py:213
  12.4 0.0 collective-permute-done.3.q_ref
  12.4 0.0 copy-done.2
  12.4 1.1 %work.10.refs_1_ = f32[136,512]{1,0:T(8,128)S(1)} custom-call(s32[1]{0:T(128)S(6)} %copy.9.len_ref, bf16[64,1024]{1,0:T(8,128)(2,1)S(1)} %collective-permute-done.3.q_ref, bf16[1152,128]{1,0:T(8,128)(2,1)S(1)} %copy-done.2, f32[136,512]{1,0:T(8,128)S(1)} %work.9.refs_1_), custom_call_target="tpu_custom_call" | custom-call | flops 6039797760 | bytes 1048576 | tf_op jit(solution)/shard_map/work/pallas_call | solution.py:213
  13.5 9.5 %collective-permute-done.2.refs_0_ = bf16[1152,128]{1,0:T(8,128)(2,1)S(1)} collective-permute-done((bf16[1152,128]{1,0:T(8,128)(2,1)S(1)}, bf16[1152,128]{1,0:T(8,128)(2,1)S(1)}, u32[]{:S(2)}, u32[]{:S(2)}) %collective-permute-start.2) | collective-permute-done | bytes 294944 | tf_op jit(solution)/shard_map/ppermute | solution.py:177
  23.1 1.1 %work.11.refs_2_ = bf16[144,512]{1,0:T(8,128)(2,1)S(1)} custom-call(s32[1]{0:T(128)S(6)} %copy.9.len_ref, bf16[64,1024]{1,0:T(8,128)(2,1)S(1)} %collective-permute-done.3.q_ref, bf16[1152,128]{1,0:T(8,128)(2,1)S(1)} %collective-permute-done.2.refs_0_, f32[136,512]{1,0:T(8,128)S(1)} %work.10.refs_1_), custom_call_target="tpu_custom_call" | custom-call | flops 6039797760 | bytes 1048576 | tf_op jit(solution)/shard_map/work/pallas_call | solution.py:213
  24.2 0.7 %collective-permute-start.5 = (bf16[144,512]{1,0:T(8,128)(2,1)S(1)}, bf16[144,512]{1,0:T(8,128)(2,1)S(1)}, u32[]{:S(2)}, u32[]{:S(2)}) collective-permute-start(bf16[144,512]{1,0:T(8,128)(2,1)S(1)} %work.11.refs_2_), channel_id=1, source_target_pairs={{0,16},{8,24},{16,0},{24,8},{1,17},{9,25},{17,1},{25,9},{2,18},{10... | collective-permute-start | bytes 442376 | tf_op jit(solution)/shard_map/ppermute | solution.py:177
  24.8 1.1 %work.12.refs_1_.own_ref = f32[136,512]{1,0:T(8,128)S(1)} custom-call(s32[1]{0:T(128)S(6)} %copy.9.len_ref, bf16[64,1024]{1,0:T(8,128)(2,1)S(1)} %get-tuple-element.12.q_ref, bf16[1152,128]{1,0:T(8,128)(2,1)S(1)} %collective-permute-done.2.refs_0_, f32[136,512]{1,0:T(8,128)S(1)} %work.8.refs_1_, bf16[144,512]{1,0:T(8,128)(2,1)S(1)} %work.11.refs_2_), custom_call_target="tpu_custom_call" | custom-call | flops 6039797760 | bytes 1048576 | tf_op jit(solution)/shard_map/work/pallas_call | solution.py:213
  25.9 0.0 collective-permute-done.1.q_ref
  25.9 1.1 %work.13.refs_1_ = f32[136,512]{1,0:T(8,128)S(1)} custom-call(s32[1]{0:T(128)S(6)} %copy.9.len_ref, bf16[64,1024]{1,0:T(8,128)(2,1)S(1)} %collective-permute-done.1.q_ref, bf16[1152,128]{1,0:T(8,128)(2,1)S(1)} %get-tuple-element.11.refs_1_.refs_0_, f32[136,512]{1,0:T(8,128)S(1)} %work.12.refs_1_.own_ref), custom_call_target="tpu_custom_call" | custom-call | flops 6039797760 | bytes 1048576 | tf_op jit(solution)/shard_map/work/pallas_call | solution.py:213
  27.0 0.0 collective-permute-done.refs_0_
  27.0 1.1 %work.14.refs_2_ = bf16[144,512]{1,0:T(8,128)(2,1)S(1)} custom-call(s32[1]{0:T(128)S(6)} %copy.9.len_ref, bf16[64,1024]{1,0:T(8,128)(2,1)S(1)} %collective-permute-done.1.q_ref, bf16[1152,128]{1,0:T(8,128)(2,1)S(1)} %collective-permute-done.refs_0_, f32[136,512]{1,0:T(8,128)S(1)} %work.13.refs_1_), custom_call_target="tpu_custom_call" | custom-call | flops 6039797760 | bytes 1048576 | tf_op jit(solution)/shard_map/work/pallas_call | solution.py:213
  28.1 2.5 %collective-permute-start.4 = (bf16[144,512]{1,0:T(8,128)(2,1)S(1)}, bf16[144,512]{1,0:T(8,128)(2,1)S(1)}, u32[]{:S(2)}, u32[]{:S(2)}) collective-permute-start(bf16[144,512]{1,0:T(8,128)(2,1)S(1)} %work.14.refs_2_), channel_id=1, source_target_pairs={{0,8},{8,0},{16,24},{24,16},{1,9},{9,1},{17,25},{25,17},{2,10},{10... | collective-permute-start | bytes 442376 | tf_op jit(solution)/shard_map/ppermute | solution.py:177
  30.7 1.1 %work.15.refs_0_.own_ref = f32[136,512]{1,0:T(8,128)S(1)} custom-call(s32[1]{0:T(128)S(6)} %copy.9.len_ref, bf16[64,1024]{1,0:T(8,128)(2,1)S(1)} %get-tuple-element.10.q_ref, bf16[1152,128]{1,0:T(8,128)(2,1)S(1)} %collective-permute-done.refs_0_, f32[136,512]{1,0:T(8,128)S(1)} %work.9.refs_1_, bf16[144,512]{1,0:T(8,128)(2,1)S(1)} %work.14.refs_2_), custom_call_target="tpu_custom_call" | custom-call | flops 6039797760 | bytes 1048576 | tf_op jit(solution)/shard_map/work/pallas_call | solution.py:213
  31.8 0.0 collective-permute-done.5.got_ref
  31.8 0.8 %merge.2.refs_0_ = bf16[64,2048]{1,0:T(8,128)(2,1)} custom-call(f32[136,512]{1,0:T(8,128)S(1)} %work.12.refs_1_.own_ref, bf16[144,512]{1,0:T(8,128)(2,1)S(1)} %collective-permute-done.5.got_ref, f32[136,512]{1,0:T(8,128)S(1)} %work.15.refs_0_.own_ref), custom_call_target="tpu_custom_call" | custom-call | tf_op jit(solution)/shard_map/merge/pallas_call | solution.py:229
  32.6 1.2 %collective-permute-done.4.got_ref = bf16[144,512]{1,0:T(8,128)(2,1)S(1)} collective-permute-done((bf16[144,512]{1,0:T(8,128)(2,1)S(1)}, bf16[144,512]{1,0:T(8,128)(2,1)S(1)}, u32[]{:S(2)}, u32[]{:S(2)}) %collective-permute-start.4) | collective-permute-done | bytes 147488 | tf_op jit(solution)/shard_map/ppermute | solution.py:177
  33.8 0.8 %merge.3 = bf16[64,2048]{1,0:T(8,128)(2,1)} custom-call(f32[136,512]{1,0:T(8,128)S(1)} %work.15.refs_0_.own_ref, bf16[144,512]{1,0:T(8,128)(2,1)S(1)} %collective-permute-done.4.got_ref, bf16[64,2048]{1,0:T(8,128)(2,1)} %merge.2.refs_0_), custom_call_target="tpu_custom_call", output_to_operand_aliasing={{}: (2, {})} | custom-call | tf_op jit(solution)/shard_map/merge/pallas_call | solution.py:229
Async XLA Ops:
  1.1 5.7 %copy-start = (bf16[1152,128]{1,0:T(8,128)(2,1)}, bf16[1152,128]{1,0:T(8,128)(2,1)S(1)}, u32[]{:S(2)}) copy-start(bf16[1152,128]{1,0:T(8,128)(2,1)S(1)} %get-tuple-element.9.rest_0_.refs_0_) | copy-start | bytes 884740
  1.1 11.3 %collective-permute-start.3 = (bf16[64,1024]{1,0:T(8,128)(2,1)S(1)}, bf16[64,1024]{1,0:T(8,128)(2,1)S(1)}, u32[]{:S(2)}, u32[]{:S(2)}) collective-permute-start(bf16[64,1024]{1,0:T(8,128)(2,1)S(1)} %get-tuple-element.12.q_ref), channel_id=1, source_target_pairs={{0,16},{8,24},{16,0},{24,8},{1,17},{9,25},{17,1},{25,9},{2,18},{10... | collective-permute-start | bytes 393224 | tf_op jit(solution)/shard_map/ppermute | solution.py:177
  5.2 17.8 %collective-permute-start.2 = (bf16[1152,128]{1,0:T(8,128)(2,1)S(1)}, bf16[1152,128]{1,0:T(8,128)(2,1)S(1)}, u32[]{:S(2)}, u32[]{:S(2)}) collective-permute-start(bf16[1152,128]{1,0:T(8,128)(2,1)S(1)} %get-tuple-element.9.rest_0_.refs_0_), channel_id=1, source_target_pairs={{0,8},{8,0},{16,24},{24,16},{1,9},{9,1},{17,25},{25,17},{2,10},{10... | collective-permute-start | bytes 884744 | tf_op jit(solution)/shard_map/ppermute | solution.py:177
  7.9 18.0 %collective-permute-start.1 = (bf16[64,1024]{1,0:T(8,128)(2,1)S(1)}, bf16[64,1024]{1,0:T(8,128)(2,1)S(1)}, u32[]{:S(2)}, u32[]{:S(2)}) collective-permute-start(bf16[64,1024]{1,0:T(8,128)(2,1)S(1)} %get-tuple-element.10.q_ref), channel_id=1, source_target_pairs={{0,8},{8,0},{16,24},{24,16},{1,9},{9,1},{17,25},{25,17},{2,10},{10... | collective-permute-start | bytes 393224 | tf_op jit(solution)/shard_map/ppermute | solution.py:177
  8.4 18.6 %collective-permute-start = (bf16[1152,128]{1,0:T(8,128)(2,1)S(1)}, bf16[1152,128]{1,0:T(8,128)(2,1)S(1)}, u32[]{:S(2)}, u32[]{:S(2)}) collective-permute-start(bf16[1152,128]{1,0:T(8,128)(2,1)S(1)} %get-tuple-element.11.refs_1_.refs_0_), channel_id=1, source_target_pairs={{0,16},{8,24},{16,0},{24,8},{1,17},{9,25},{17,1},{25,9},{2,18},{10... | collective-permute-start | bytes 884744 | tf_op jit(solution)/shard_map/ppermute | solution.py:177
  9.3 1.0 %copy-start.1 = (bf16[1152,128]{1,0:T(8,128)(2,1)S(1)}, bf16[1152,128]{1,0:T(8,128)(2,1)}, u32[]{:S(2)}) copy-start(bf16[1152,128]{1,0:T(8,128)(2,1)} %copy-done) | copy-start | bytes 884740
  11.3 1.1 %copy-start.2 = (bf16[1152,128]{1,0:T(8,128)(2,1)S(1)}, bf16[1152,128]{1,0:T(8,128)(2,1)}, u32[]{:S(2)}) copy-start(bf16[1152,128]{1,0:T(8,128)(2,1)} %copy-done) | copy-start | bytes 884740
  24.2 7.6 %collective-permute-start.5 = (bf16[144,512]{1,0:T(8,128)(2,1)S(1)}, bf16[144,512]{1,0:T(8,128)(2,1)S(1)}, u32[]{:S(2)}, u32[]{:S(2)}) collective-permute-start(bf16[144,512]{1,0:T(8,128)(2,1)S(1)} %work.11.refs_2_), channel_id=1, source_target_pairs={{0,16},{8,24},{16,0},{24,8},{1,17},{9,25},{17,1},{25,9},{2,18},{10... | collective-permute-start | bytes 442376 | tf_op jit(solution)/shard_map/ppermute | solution.py:177
  28.1 5.7 %collective-permute-start.4 = (bf16[144,512]{1,0:T(8,128)(2,1)S(1)}, bf16[144,512]{1,0:T(8,128)(2,1)S(1)}, u32[]{:S(2)}, u32[]{:S(2)}) collective-permute-start(bf16[144,512]{1,0:T(8,128)(2,1)S(1)} %work.14.refs_2_), channel_id=1, source_target_pairs={{0,8},{8,0},{16,24},{24,16},{1,9},{9,1},{17,25},{25,17},{2,10},{10... | collective-permute-start | bytes 442376 | tf_op jit(solution)/shard_map/ppermute | solution.py:177

commit v4 on v3

--- a/solution.py
+++ b/solution.py
@@ -10,8 +10,7 @@
 HEAD_DIM = 128
 LOW = -1e30
 SLOPE = HEAD_DIM ** (-0.5) * 1.4426950408889634
-STATS = 16
-STEP = 4
+STEP = 8
 
 VMEM = pl.BlockSpec(memory_space=pltpu.VMEM)
 SMEM = pl.BlockSpec(memory_space=pltpu.SMEM)
@@ -81,21 +80,22 @@
     ref[HEAD_DIM : HEAD_DIM + 1, lanes] = top * SLOPE + jnp.log2(total)
 
 
-def store_sent(ref, lanes, state):
-    top, total, summed = state
-    log = top * SLOPE + jnp.log2(total)
-    high = log.astype(jnp.bfloat16).astype(jnp.float32)
-    rest = log - high
-    middle = rest.astype(jnp.bfloat16).astype(jnp.float32)
-    row = lax.broadcasted_iota(jnp.int32, (STATS, log.shape[1]), 0)
-    stats = jnp.where(
-        row == 0, high, jnp.where(row == 1, middle, jnp.where(row == 2, rest - middle, 0.0))
-    )
-    ref[0:HEAD_DIM, lanes] = (summed * (1.0 / total)).astype(jnp.bfloat16)
-    ref[HEAD_DIM : HEAD_DIM + STATS, lanes] = stats.astype(jnp.bfloat16)
-
-
-STORES = {"state": store_state, "own": store_own, "sent": store_sent}
+def store_sent(ref, blocks):
+    row = lax.broadcasted_iota(jnp.int32, (ref.shape[0] - len(blocks) * HEAD_DIM, HEAD_DIM), 0)
+    stats = jnp.zeros(row.shape, jnp.float32)
+    for n, (top, total, summed) in enumerate(blocks):
+        log = top * SLOPE + jnp.log2(total)
+        high = log.astype(jnp.bfloat16).astype(jnp.float32)
+        rest = log - high
+        middle = rest.astype(jnp.bfloat16).astype(jnp.float32)
+        for i, part in enumerate((high, middle, rest - middle)):
+            stats = jnp.where(row == 3 * n + i, part, stats)
+        ref[n * HEAD_DIM : (n + 1) * HEAD_DIM, :] = (summed * (1.0 / total)).astype(jnp.bfloat16)
+    ref[len(blocks) * HEAD_DIM :, :] = stats.astype(jnp.bfloat16)
+
+
+def sent_rows(blocks):
+    return blocks * HEAD_DIM + -(-3 * blocks // 16) * 16
 
 
 def attend_kernel(dims, blocks, q_xor, store, carried, after, len_ref, q_ref, *refs):
@@ -103,6 +103,7 @@
     kv_refs, out_ref = refs[: len(blocks)], refs[-1]
     me = lax.axis_index("ctx")
     groups = q_ref.shape[1] // HEAD_DIM
+    sent = []
     for at in range(0, groups, step):
         query = stacked_heads(q_ref, at, step)
         lanes = pl.ds(at * new_rows, step * new_rows)
@@ -112,7 +113,15 @@
                 query, kv_ref, me ^ block, me ^ q_xor, len_ref[0], cache_rows, new_rows
             )
             state = ours if state is None else joined(state, ours)
-        STORES[store](out_ref, lanes, state)
+        if store == "state":
+            store_state(out_ref, lanes, state)
+        elif store == "own":
+            store_own(out_ref, lanes, state)
+        else:
+            for lane in range(0, step * new_rows, HEAD_DIM):
+                sent.append([part[:, lane : lane + HEAD_DIM] for part in state])
+    if store == "sent":
+        store_sent(out_ref, sent)
 
 
 def merge_kernel(dims, columns, aliased, own_ref, got_ref, *refs):
@@ -120,17 +129,17 @@
     out_ref, block_ref, sem = refs[-3:]
     first, own_first, groups = columns
     pair = HEAD_DIM // new_rows
+    stats = got_ref[groups // pair * HEAD_DIM :, :].astype(jnp.float32)
     for at in range(0, groups, pair):
-        lanes = pl.ds(at * new_rows, pair * new_rows)
         own_lanes = pl.ds((own_first + at) * new_rows, pair * new_rows)
-        stats = got_ref[HEAD_DIM : HEAD_DIM + STATS, lanes].astype(jnp.float32)
-        theirs = stats[0:1] + stats[1:2] + stats[2:3]
+        n = at // pair
+        theirs = sum(stats[3 * n + i : 3 * n + i + 1] for i in range(3))
         mine = own_ref[HEAD_DIM : HEAD_DIM + 1, own_lanes]
         top = jnp.maximum(mine, theirs)
         left, right = jnp.exp2(mine - top), jnp.exp2(theirs - top)
         scale = 1.0 / (left + right)
         whole = own_ref[0:HEAD_DIM, own_lanes] * (left * scale) + got_ref[
-            0:HEAD_DIM, lanes
+            n * HEAD_DIM : (n + 1) * HEAD_DIM, :
         ].astype(jnp.float32) * (right * scale)
         turned = whole.T.astype(jnp.bfloat16)
         for g in range(pair):
@@ -143,25 +152,25 @@
     copy.wait()
 
 
-def pack_kernel(head, pieces, q_ref, ck_ref, cv_ref, nk_ref, nv_ref, *rest):
-    sems = rest[-1]
-    kv, q_refs = rest[-2 - pieces], rest[-1 - pieces : -1]
+def pack_kernel(head, with_kv, with_q, *refs):
+    q_ref, ck_ref, cv_ref, nk_ref, nv_ref = refs[:5]
+    sems, outs = refs[-1], list(refs[-1 - with_kv - with_q : -1])
     cache_rows, new_rows = ck_ref.shape[0], nk_ref.shape[0]
     key_rows = cache_rows + new_rows
-    width = q_refs[0].shape[1]
     columns = pl.ds(head * HEAD_DIM, HEAD_DIM)
-    copies = [
-        (source.at[:, columns], kv.at[pl.ds(at, rows), :])
+    copies = []
+    if with_kv:
+        kv = outs.pop(0)
         for source, at, rows in (
             (ck_ref, 0, cache_rows),
             (nk_ref, cache_rows, new_rows),
             (cv_ref, key_rows, cache_rows),
             (nv_ref, key_rows + cache_rows, new_rows),
-        )
-    ] + [
-        (q_ref.at[:, pl.ds((head * pieces + piece) * width, width)], q_refs[piece])
-        for piece in range(pieces)
-    ]
+        ):
+            copies.append((source.at[:, columns], kv.at[pl.ds(at, rows), :]))
+    if with_q:
+        width = outs[0].shape[1]
+        copies.append((q_ref.at[:, pl.ds(head * width, width)], outs[0]))
     handles = [
         pltpu.make_async_copy(source, target, sems.at[n])
         for n, (source, target) in enumerate(copies)
@@ -191,14 +200,15 @@
         for argument in (queries, cache_keys, cache_values, new_keys, new_values)
     ]
 
-    def pack(head, pieces, after):
+    def pack(head, with_kv, with_q, after):
+        outs = [pltpu.VMEM((2 * key_rows, HEAD_DIM), bf16)] * with_kv
+        outs += [pltpu.VMEM((new_rows, groups * HEAD_DIM), bf16)] * with_q
         return pl.pallas_call(
-            functools.partial(pack_kernel, head, pieces),
-            out_shape=[pltpu.VMEM((2 * key_rows, HEAD_DIM), bf16)]
-            + [pltpu.VMEM((new_rows, groups * HEAD_DIM // pieces), bf16)] * pieces,
+            functools.partial(pack_kernel, head, with_kv, with_q),
+            out_shape=outs,
             in_specs=[HBM] * 5 + [ANY] * len(after),
-            out_specs=[VMEM] * (1 + pieces),
-            scratch_shapes=[pltpu.SemaphoreType.DMA((4 + pieces,))],
+            out_specs=[VMEM] * len(outs),
+            scratch_shapes=[pltpu.SemaphoreType.DMA((4 * with_kv + with_q,))],
             name="pack",
         )(*arguments, *after)
 
@@ -206,7 +216,7 @@
         rows = query.shape[1] // HEAD_DIM * new_rows
         pairs = key_rows * rows * len(blocks)
         if store == "sent":
-            out = pltpu.VMEM((HEAD_DIM + STATS, rows), bf16)
+            out = pltpu.VMEM((sent_rows(rows // HEAD_DIM), HEAD_DIM), bf16)
         else:
             out = pltpu.VMEM((HEAD_DIM + 8, rows), f32)
         carried = () if state is None else (state,)
@@ -240,20 +250,22 @@
             name="merge",
         )(own, got, *aliased, *after)
 
-    kv0, q0 = pack(0, 1, ())
+    kv0, q0 = pack(0, 1, 1, ())
     far_kv0, far_q0 = traded(kv0, 1), traded(q0, 2)
-    kv1, q1 = pack(1, 1, (kv0,))
-    far_kv1, far_q1 = traded(kv1, 2), traded(q1, 1)
+    (kv1,) = pack(1, 1, 0, (kv0,))
+    far_kv1 = traded(kv1, 2)
     mine0 = work(q0, [(0, kv0)], 0, "state", after=(kv1,))
-    mine1 = work(q1, [(0, kv1)], 0, "state", after=(mine0,))
+    (q1,) = pack(1, 0, 1, (mine0,))
+    far_q1 = traded(q1, 1)
+    mine1 = work(q1, [(0, kv1)], 0, "state")
     theirs0 = work(far_q0, [(0, kv0)], 2, "state", after=(mine1,))
-    sent0 = work(far_q0, [(1, far_kv0)], 2, "sent", state=theirs0)
+    sent0 = work(far_q0, [(1, far_kv0)], 2, "sent", state=theirs0, after=(mine1,))
+    theirs1 = work(far_q1, [(0, kv1)], 1, "state", after=(sent0,))
     got0 = traded(sent0, 2)
-    own0 = work(q0, [(1, far_kv0)], 0, "own", state=mine0, after=(sent0,))
-    theirs1 = work(far_q1, [(0, kv1)], 1, "state", after=(own0,))
     sent1 = work(far_q1, [(2, far_kv1)], 1, "sent", state=theirs1)
     got1 = traded(sent1, 1)
-    own1 = work(q1, [(2, far_kv1)], 0, "own", state=mine1, after=(sent1,))
+    own0 = work(q0, [(1, far_kv0)], 0, "own", state=mine0, after=(sent1,))
+    own1 = work(q1, [(2, far_kv1)], 0, "own", state=mine1, after=(own0,))
     out = merge(own0, got0, (0, 0, groups), after=(own1,))
     return merge(own1, got1, (groups, 0, groups), out)
 

time: 34.8 us -> 33 us (0.948)
  Pallas kernels: 12.5 us -> 10.6 us
  starting transfers between devices: 9.59 us -> 8.54 us
  local copies, waits for them, and re-layouts: 0.96 us -> 1.68 us
  waiting for transfers between devices: 10.7 us -> 11.1 us
    pallas_call x8, Pallas kernels: 8.71 us -> 5.98 us  [work(): pl.pallas_call(functools.partial(attend_kernel, dims, tuple((b for b, _ i...]
    ppermute x6, starting transfers between devices: 9.59 us -> 8.54 us  [traded(): lax.ppermute(value, 'ctx', [(source, source ^ xor) for source in range(co...]
    pallas_call x2 -> x3, Pallas kernels: 2.21 us -> 3.04 us  [pack(): pl.pallas_call(functools.partial(pack_kernel, head, with_kv, with_q), out...]
    unnamed x6 -> x10, local copies, waits for them, and re-layouts: 0.96 us -> 1.68 us
    ppermute x6, waiting for transfers between devices: 10.7 us -> 11.1 us  [traded(): lax.ppermute(value, 'ctx', [(source, source ^ xor) for source in range(co...]
  transfers between devices with their start and end apart: 6 -> 6, of which waited for: 2 -> 4; matrix products, arithmetic and copies ran while one was open for 0% -> 0% of each run, Pallas kernels for 31% -> 27%
where the time goes in v4:
time: 33 us; the launch traced here: 32.8 us
  waiting for transfers between devices  11.1 us (34%)
  Pallas kernels  10.6 us (32%)
  starting transfers between devices  8.54 us (26%)
  local copies, waits for them, and re-layouts  1.68 us (5%)
  between operations  0.82 us (2%)
    ppermute x6, waiting for transfers between devices, traded(): lax.ppermute(value, 'ctx', [(source, source ^ xor) for source in range(co...  11.1 us
    ppermute x6, starting transfers between devices, traded(): lax.ppermute(value, 'ctx', [(source, source ^ xor) for source in range(co...  8.54 us
    pallas_call x8, Pallas kernels, work(): pl.pallas_call(functools.partial(attend_kernel, dims, tuple((b for b, _ i...  5.98 us
    pallas_call x3, Pallas kernels, pack(): pl.pallas_call(functools.partial(pack_kernel, head, with_kv, with_q), out...  3.04 us
    unnamed x10, local copies, waits for them, and re-layouts  1.68 us
    pallas_call x2, Pallas kernels, merge(): pl.pallas_call(functools.partial(merge_kernel, dims, columns, bool(aliase...  1.59 us
  transfers between devices with their start and end apart: 6, of which 4 were waited for; matrix products, arithmetic and copies ran while one was open for 0% of the time, Pallas kernels for 27%

profile of v4, /device:TPU:0, one launch (start us, length us, event | category | flops | bytes accessed | tf_op | source)
XLA Modules:
  0.0 32.8 jit_solution(6612165855772527890)
XLA Ops:
  0.0 1.1 %pack.3 = (bf16[1152,128]{1,0:T(8,128)(2,1)S(1)}, bf16[64,1024]{1,0:T(8,128)(2,1)S(1)}) custom-call(bf16[64,2048]{1,0:T(8,128)(2,1)} %refs_0_.5, bf16[512,256]{1,0:T(8,128)(2,1)} %refs_1_.5, bf16[512,256]{1,0:T(8,128)(2,1)} %refs_2_.5, bf16[64,256]{1,0:T(8,128)(2,1)} %refs_3_.5, bf16[64,256]{1,0:T(8,128)(2,1)} %refs_4_.5), custom_call_target="tpu_custom_call" | custom-call | tf_op jit(solution)/shard_map/pack/pallas_call | solution.py:206
  1.1 0.0 copy-start
  1.1 4.1 %collective-permute-start.3 = (bf16[64,1024]{1,0:T(8,128)(2,1)S(1)}, bf16[64,1024]{1,0:T(8,128)(2,1)S(1)}, u32[]{:S(2)}, u32[]{:S(2)}) collective-permute-start(bf16[64,1024]{1,0:T(8,128)(2,1)S(1)} %get-tuple-element.7.q_ref), channel_id=1, source_target_pairs={{0,16},{8,24},{16,0},{24,8},{1,17},{9,25},{17,1},{25,9},{2,18},{10... | collective-permute-start | bytes 393224 | tf_op jit(solution)/shard_map/ppermute | solution.py:186
  5.2 1.6 %collective-permute-start.1 = (bf16[1152,128]{1,0:T(8,128)(2,1)S(1)}, bf16[1152,128]{1,0:T(8,128)(2,1)S(1)}, u32[]{:S(2)}, u32[]{:S(2)}) collective-permute-start(bf16[1152,128]{1,0:T(8,128)(2,1)S(1)} %get-tuple-element.8.refs_5_.refs_0_), channel_id=1, source_target_pairs={{0,8},{8,0},{16,24},{24,16},{1,9},{9,1},{17,25},{25,17},{2,10},{10... | collective-permute-start | bytes 884744 | tf_op jit(solution)/shard_map/ppermute | solution.py:186
  6.8 0.0 copy-done
  6.8 1.0 %pack.4.refs_1_.refs_0_ = bf16[1152,128]{1,0:T(8,128)(2,1)S(1)} custom-call(bf16[64,2048]{1,0:T(8,128)(2,1)} %refs_0_.5, bf16[512,256]{1,0:T(8,128)(2,1)} %refs_1_.5, bf16[512,256]{1,0:T(8,128)(2,1)} %refs_2_.5, bf16[64,256]{1,0:T(8,128)(2,1)} %refs_3_.5, bf16[64,256]{1,0:T(8,128)(2,1)} %refs_4_.5, bf16[1152,128]{1,0:T(8,128)(2,1)} %copy-done), custom_call_target="tpu_custom_call" | custom-call | tf_op jit(solution)/shard_map/pack/pallas_call | solution.py:206
  7.8 0.4 %collective-permute-start = (bf16[1152,128]{1,0:T(8,128)(2,1)S(1)}, bf16[1152,128]{1,0:T(8,128)(2,1)S(1)}, u32[]{:S(2)}, u32[]{:S(2)}) collective-permute-start(bf16[1152,128]{1,0:T(8,128)(2,1)S(1)} %pack.4.refs_1_.refs_0_), channel_id=1, source_target_pairs={{0,16},{8,24},{16,0},{24,8},{1,17},{9,25},{17,1},{25,9},{2,18},{10... | collective-permute-start | bytes 884744 | tf_op jit(solution)/shard_map/ppermute | solution.py:186
  8.9 0.0 copy-start.1
  8.9 1.0 %copy-done.1 = bf16[1152,128]{1,0:T(8,128)(2,1)S(1)} copy-done((bf16[1152,128]{1,0:T(8,128)(2,1)S(1)}, bf16[1152,128]{1,0:T(8,128)(2,1)}, u32[]{:S(2)}) %copy-start.1) | copy-done | bytes 294936
  9.8 0.7 %work.8.refs_5_.refs_1_ = f32[136,512]{1,0:T(8,128)S(1)} custom-call(s32[1]{0:T(128)S(6)} %copy.9.len_ref, bf16[64,1024]{1,0:T(8,128)(2,1)S(1)} %get-tuple-element.7.q_ref, bf16[1152,128]{1,0:T(8,128)(2,1)S(1)} %copy-done.1, bf16[1152,128]{1,0:T(8,128)(2,1)S(1)} %pack.4.refs_1_.refs_0_), custom_call_target="tpu_custom_call" | custom-call | flops 6039797760 | bytes 1048576 | tf_op jit(solution)/shard_map/work/pallas_call | solution.py:223
  10.6 0.0 copy-start.3
  10.6 0.7 %copy-done.3 = f32[136,512]{1,0:T(8,128)} copy-done((f32[136,512]{1,0:T(8,128)}, f32[136,512]{1,0:T(8,128)S(1)}, u32[]{:S(2)}) %copy-start.3) | copy-done | bytes 278552
  11.3 0.9 %pack.5.q_ref = bf16[64,1024]{1,0:T(8,128)(2,1)S(1)} custom-call(bf16[64,2048]{1,0:T(8,128)(2,1)} %refs_0_.5, bf16[512,256]{1,0:T(8,128)(2,1)} %refs_1_.5, bf16[512,256]{1,0:T(8,128)(2,1)} %refs_2_.5, bf16[64,256]{1,0:T(8,128)(2,1)} %refs_3_.5, bf16[64,256]{1,0:T(8,128)(2,1)} %refs_4_.5, f32[136,512]{1,0:T(8,128)} %copy-done.3), custom_call_target="tpu_custom_call" | custom-call | tf_op jit(solution)/shard_map/pack/pallas_call | solution.py:206
  12.2 0.0 copy-start.2
  12.3 0.4 %collective-permute-start.2 = (bf16[64,1024]{1,0:T(8,128)(2,1)S(1)}, bf16[64,1024]{1,0:T(8,128)(2,1)S(1)}, u32[]{:S(2)}, u32[]{:S(2)}) collective-permute-start(bf16[64,1024]{1,0:T(8,128)(2,1)S(1)} %pack.5.q_ref), channel_id=1, source_target_pairs={{0,8},{8,0},{16,24},{24,16},{1,9},{9,1},{17,25},{25,17},{2,10},{10... | collective-permute-start | bytes 393224 | tf_op jit(solution)/shard_map/ppermute | solution.py:186
  12.6 0.7 %work.9.refs_1_.refs_2_ = f32[136,512]{1,0:T(8,128)S(1)} custom-call(s32[1]{0:T(128)S(6)} %copy.9.len_ref, bf16[64,1024]{1,0:T(8,128)(2,1)S(1)} %pack.5.q_ref, bf16[1152,128]{1,0:T(8,128)(2,1)S(1)} %pack.4.refs_1_.refs_0_), custom_call_target="tpu_custom_call" | custom-call | flops 6039797760 | bytes 1048576 | tf_op jit(solution)/shard_map/work/pallas_call | solution.py:223
  13.4 0.0 collective-permute-done.3.q_ref
  13.4 0.0 copy-done.2
  13.4 0.7 %work.10.refs_1_ = f32[136,512]{1,0:T(8,128)S(1)} custom-call(s32[1]{0:T(128)S(6)} %copy.9.len_ref, bf16[64,1024]{1,0:T(8,128)(2,1)S(1)} %collective-permute-done.3.q_ref, bf16[1152,128]{1,0:T(8,128)(2,1)S(1)} %copy-done.2, f32[136,512]{1,0:T(8,128)S(1)} %work.9.refs_1_.refs_2_), custom_call_target="tpu_custom_call" | custom-call | flops 6039797760 | bytes 1048576 | tf_op jit(solution)/shard_map/work/pallas_call | solution.py:223
  14.1 7.3 %collective-permute-done.1.refs_0_ = bf16[1152,128]{1,0:T(8,128)(2,1)S(1)} collective-permute-done((bf16[1152,128]{1,0:T(8,128)(2,1)S(1)}, bf16[1152,128]{1,0:T(8,128)(2,1)S(1)}, u32[]{:S(2)}, u32[]{:S(2)}) %collective-permute-start.1) | collective-permute-done | bytes 294944 | tf_op jit(solution)/shard_map/ppermute | solution.py:186
  21.4 0.8 %work.11.refs_1_ = bf16[528,128]{1,0:T(8,128)(2,1)S(1)} custom-call(s32[1]{0:T(128)S(6)} %copy.9.len_ref, bf16[64,1024]{1,0:T(8,128)(2,1)S(1)} %collective-permute-done.3.q_ref, bf16[1152,128]{1,0:T(8,128)(2,1)S(1)} %collective-permute-done.1.refs_0_, f32[136,512]{1,0:T(8,128)S(1)} %work.10.refs_1_, f32[136,512]{1,0:T(8,128)S(1)} %work.9.refs_1_.refs_2_), custom_call_target="tpu_custom_call" | custom-call | flops 6039797760 | bytes 1048576 | tf_op jit(solution)/shard_map/work/pallas_call | solution.py:223
  22.2 0.1 collective-permute-start.5
  22.3 2.5 %collective-permute-done.2.q_ref = bf16[64,1024]{1,0:T(8,128)(2,1)S(1)} collective-permute-done((bf16[64,1024]{1,0:T(8,128)(2,1)S(1)}, bf16[64,1024]{1,0:T(8,128)(2,1)S(1)}, u32[]{:S(2)}, u32[]{:S(2)}) %collective-permute-start.2) | collective-permute-done | bytes 131104 | tf_op jit(solution)/shard_map/ppermute | solution.py:186
  24.7 0.7 %work.12.refs_1_ = f32[136,512]{1,0:T(8,128)S(1)} custom-call(s32[1]{0:T(128)S(6)} %copy.9.len_ref, bf16[64,1024]{1,0:T(8,128)(2,1)S(1)} %collective-permute-done.2.q_ref, bf16[1152,128]{1,0:T(8,128)(2,1)S(1)} %pack.4.refs_1_.refs_0_, bf16[528,128]{1,0:T(8,128)(2,1)S(1)} %work.11.refs_1_), custom_call_target="tpu_custom_call" | custom-call | flops 6039797760 | bytes 1048576 | tf_op jit(solution)/shard_map/work/pallas_call | solution.py:223
  25.5 0.0 copy-start.4
  25.5 0.4 %collective-permute-done.refs_0_ = bf16[1152,128]{1,0:T(8,128)(2,1)S(1)} collective-permute-done((bf16[1152,128]{1,0:T(8,128)(2,1)S(1)}, bf16[1152,128]{1,0:T(8,128)(2,1)S(1)}, u32[]{:S(2)}, u32[]{:S(2)}) %collective-permute-start) | collective-permute-done | bytes 294944 | tf_op jit(solution)/shard_map/ppermute | solution.py:186
  25.9 0.8 %work.13.refs_2_ = bf16[528,128]{1,0:T(8,128)(2,1)S(1)} custom-call(s32[1]{0:T(128)S(6)} %copy.9.len_ref, bf16[64,1024]{1,0:T(8,128)(2,1)S(1)} %collective-permute-done.2.q_ref, bf16[1152,128]{1,0:T(8,128)(2,1)S(1)} %collective-permute-done.refs_0_, f32[136,512]{1,0:T(8,128)S(1)} %work.12.refs_1_), custom_call_target="tpu_custom_call" | custom-call | flops 6039797760 | bytes 1048576 | tf_op jit(solution)/shard_map/work/pallas_call | solution.py:223
  26.7 2.0 %collective-permute-start.4 = (bf16[528,128]{1,0:T(8,128)(2,1)S(1)}, bf16[528,128]{1,0:T(8,128)(2,1)S(1)}, u32[]{:S(2)}, u32[]{:S(2)}) collective-permute-start(bf16[528,128]{1,0:T(8,128)(2,1)S(1)} %work.13.refs_2_), channel_id=1, source_target_pairs={{0,8},{8,0},{16,24},{24,16},{1,9},{9,1},{17,25},{25,17},{2,10},{10... | collective-permute-start | bytes 405512 | tf_op jit(solution)/shard_map/ppermute | solution.py:186
  28.7 0.0 copy-done.4
  28.7 0.7 %work.14.refs_2_.own_ref = f32[136,512]{1,0:T(8,128)S(1)} custom-call(s32[1]{0:T(128)S(6)} %copy.9.len_ref, bf16[64,1024]{1,0:T(8,128)(2,1)S(1)} %get-tuple-element.7.q_ref, bf16[1152,128]{1,0:T(8,128)(2,1)S(1)} %collective-permute-done.1.refs_0_, f32[136,512]{1,0:T(8,128)S(1)} %copy-done.4, bf16[528,128]{1,0:T(8,128)(2,1)S(1)} %work.13.refs_2_), custom_call_target="tpu_custom_call" | custom-call | flops 6039797760 | bytes 1048576 | tf_op jit(solution)/shard_map/work/pallas_call | solution.py:223
  29.5 0.7 %work.15.refs_0_.own_ref = f32[136,512]{1,0:T(8,128)S(1)} custom-call(s32[1]{0:T(128)S(6)} %copy.9.len_ref, bf16[64,1024]{1,0:T(8,128)(2,1)S(1)} %pack.5.q_ref, bf16[1152,128]{1,0:T(8,128)(2,1)S(1)} %collective-permute-done.refs_0_, f32[136,512]{1,0:T(8,128)S(1)} %work.9.refs_1_.refs_2_, f32[136,512]{1,0:T(8,128)S(1)} %work.14.refs_2_.own_ref), custom_call_target="tpu_custom_call" | custom-call | flops 6039797760 | bytes 1048576 | tf_op jit(solution)/shard_map/work/pallas_call | solution.py:223
  30.2 0.0 collective-permute-done.5.got_ref
  30.2 0.8 %merge.2.refs_0_ = bf16[64,2048]{1,0:T(8,128)(2,1)} custom-call(f32[136,512]{1,0:T(8,128)S(1)} %work.14.refs_2_.own_ref, bf16[528,128]{1,0:T(8,128)(2,1)S(1)} %collective-permute-done.5.got_ref, f32[136,512]{1,0:T(8,128)S(1)} %work.15.refs_0_.own_ref), custom_call_target="tpu_custom_call" | custom-call | tf_op jit(solution)/shard_map/merge/pallas_call | solution.py:239
  31.0 0.9 %collective-permute-done.4.got_ref = bf16[528,128]{1,0:T(8,128)(2,1)S(1)} collective-permute-done((bf16[528,128]{1,0:T(8,128)(2,1)S(1)}, bf16[528,128]{1,0:T(8,128)(2,1)S(1)}, u32[]{:S(2)}, u32[]{:S(2)}) %collective-permute-start.4) | collective-permute-done | bytes 135200 | tf_op jit(solution)/shard_map/ppermute | solution.py:186
  32.0 0.8 %merge.3 = bf16[64,2048]{1,0:T(8,128)(2,1)} custom-call(f32[136,512]{1,0:T(8,128)S(1)} %work.15.refs_0_.own_ref, bf16[528,128]{1,0:T(8,128)(2,1)S(1)} %collective-permute-done.4.got_ref, bf16[64,2048]{1,0:T(8,128)(2,1)} %merge.2.refs_0_), custom_call_target="tpu_custom_call", output_to_operand_aliasing={{}: (2, {})} | custom-call | tf_op jit(solution)/shard_map/merge/pallas_call | solution.py:239
Async XLA Ops:
  1.1 5.7 %copy-start = (bf16[1152,128]{1,0:T(8,128)(2,1)}, bf16[1152,128]{1,0:T(8,128)(2,1)S(1)}, u32[]{:S(2)}) copy-start(bf16[1152,128]{1,0:T(8,128)(2,1)S(1)} %get-tuple-element.8.refs_5_.refs_0_) | copy-start | bytes 884740
  1.1 12.2 %collective-permute-start.3 = (bf16[64,1024]{1,0:T(8,128)(2,1)S(1)}, bf16[64,1024]{1,0:T(8,128)(2,1)S(1)}, u32[]{:S(2)}, u32[]{:S(2)}) collective-permute-start(bf16[64,1024]{1,0:T(8,128)(2,1)S(1)} %get-tuple-element.7.q_ref), channel_id=1, source_target_pairs={{0,16},{8,24},{16,0},{24,8},{1,17},{9,25},{17,1},{25,9},{2,18},{10... | collective-permute-start | bytes 393224 | tf_op jit(solution)/shard_map/ppermute | solution.py:186
  5.2 16.2 %collective-permute-start.1 = (bf16[1152,128]{1,0:T(8,128)(2,1)S(1)}, bf16[1152,128]{1,0:T(8,128)(2,1)S(1)}, u32[]{:S(2)}, u32[]{:S(2)}) collective-permute-start(bf16[1152,128]{1,0:T(8,128)(2,1)S(1)} %get-tuple-element.8.refs_5_.refs_0_), channel_id=1, source_target_pairs={{0,8},{8,0},{16,24},{24,16},{1,9},{9,1},{17,25},{25,17},{2,10},{10... | collective-permute-start | bytes 884744 | tf_op jit(solution)/shard_map/ppermute | solution.py:186
  7.8 18.1 %collective-permute-start = (bf16[1152,128]{1,0:T(8,128)(2,1)S(1)}, bf16[1152,128]{1,0:T(8,128)(2,1)S(1)}, u32[]{:S(2)}, u32[]{:S(2)}) collective-permute-start(bf16[1152,128]{1,0:T(8,128)(2,1)S(1)} %pack.4.refs_1_.refs_0_), channel_id=1, source_target_pairs={{0,16},{8,24},{16,0},{24,8},{1,17},{9,25},{17,1},{25,9},{2,18},{10... | collective-permute-start | bytes 884744 | tf_op jit(solution)/shard_map/ppermute | solution.py:186
  8.9 1.0 %copy-start.1 = (bf16[1152,128]{1,0:T(8,128)(2,1)S(1)}, bf16[1152,128]{1,0:T(8,128)(2,1)}, u32[]{:S(2)}) copy-start(bf16[1152,128]{1,0:T(8,128)(2,1)} %copy-done) | copy-start | bytes 884740
  10.6 0.7 %copy-start.3 = (f32[136,512]{1,0:T(8,128)}, f32[136,512]{1,0:T(8,128)S(1)}, u32[]{:S(2)}) copy-start(f32[136,512]{1,0:T(8,128)S(1)} %work.8.refs_5_.refs_1_) | copy-start | bytes 835588
  12.2 1.1 %copy-start.2 = (bf16[1152,128]{1,0:T(8,128)(2,1)S(1)}, bf16[1152,128]{1,0:T(8,128)(2,1)}, u32[]{:S(2)}) copy-start(bf16[1152,128]{1,0:T(8,128)(2,1)} %copy-done) | copy-start | bytes 884740
  12.3 12.5 %collective-permute-start.2 = (bf16[64,1024]{1,0:T(8,128)(2,1)S(1)}, bf16[64,1024]{1,0:T(8,128)(2,1)S(1)}, u32[]{:S(2)}, u32[]{:S(2)}) collective-permute-start(bf16[64,1024]{1,0:T(8,128)(2,1)S(1)} %pack.5.q_ref), channel_id=1, source_target_pairs={{0,8},{8,0},{16,24},{24,16},{1,9},{9,1},{17,25},{25,17},{2,10},{10... | collective-permute-start | bytes 393224 | tf_op jit(solution)/shard_map/ppermute | solution.py:186
  22.2 8.0 %collective-permute-start.5 = (bf16[528,128]{1,0:T(8,128)(2,1)S(1)}, bf16[528,128]{1,0:T(8,128)(2,1)S(1)}, u32[]{:S(2)}, u32[]{:S(2)}) collective-permute-start(bf16[528,128]{1,0:T(8,128)(2,1)S(1)} %work.11.refs_1_), channel_id=1, source_target_pairs={{0,16},{8,24},{16,0},{24,8},{1,17},{9,25},{17,1},{25,9},{2,18},{10... | collective-permute-start | bytes 405512 | tf_op jit(solution)/shard_map/ppermute | solution.py:186
  25.5 3.2 %copy-start.4 = (f32[136,512]{1,0:T(8,128)S(1)}, f32[136,512]{1,0:T(8,128)}, u32[]{:S(2)}) copy-start(f32[136,512]{1,0:T(8,128)} %copy-done.3) | copy-start | bytes 835588
  26.7 5.3 %collective-permute-start.4 = (bf16[528,128]{1,0:T(8,128)(2,1)S(1)}, bf16[528,128]{1,0:T(8,128)(2,1)S(1)}, u32[]{:S(2)}, u32[]{:S(2)}) collective-permute-start(bf16[528,128]{1,0:T(8,128)(2,1)S(1)} %work.13.refs_2_), channel_id=1, source_target_pairs={{0,8},{8,0},{16,24},{24,16},{1,9},{9,1},{17,25},{25,17},{2,10},{10... | collective-permute-start | bytes 405512 | tf_op jit(solution)/shard_map/ppermute | solution.py:186

commit v5 on v4

--- a/solution.py
+++ b/solution.py
@@ -10,7 +10,6 @@
 HEAD_DIM = 128
 LOW = -1e30
 SLOPE = HEAD_DIM ** (-0.5) * 1.4426950408889634
-STEP = 8
 
 VMEM = pl.BlockSpec(memory_space=pltpu.VMEM)
 SMEM = pl.BlockSpec(memory_space=pltpu.SMEM)
@@ -98,7 +97,7 @@
     return blocks * HEAD_DIM + -(-3 * blocks // 16) * 16
 
 
-def attend_kernel(dims, blocks, q_xor, store, carried, after, len_ref, q_ref, *refs):
+def attend_kernel(dims, blocks, q_xor, store, carried, len_ref, q_ref, *refs):
     cache_rows, new_rows, step = dims
     kv_refs, out_ref = refs[: len(blocks)], refs[-1]
     me = lax.axis_index("ctx")
@@ -124,7 +123,7 @@
         store_sent(out_ref, sent)
 
 
-def merge_kernel(dims, columns, aliased, own_ref, got_ref, *refs):
+def merge_kernel(dims, columns, own_ref, got_ref, *refs):
     cache_rows, new_rows, _ = dims
     out_ref, block_ref, sem = refs[-3:]
     first, own_first, groups = columns
@@ -192,7 +191,7 @@
     heads = kv_width // HEAD_DIM
     groups = queries.shape[1] // kv_width
     key_rows = cache_rows + new_rows
-    dims = (cache_rows, new_rows, STEP)
+    dims = (cache_rows, new_rows, groups)
     bf16, f32 = jnp.bfloat16, jnp.float32
     shape = jax.ShapeDtypeStruct
     arguments = [
@@ -209,6 +208,7 @@
             in_specs=[HBM] * 5 + [ANY] * len(after),
             out_specs=[VMEM] * len(outs),
             scratch_shapes=[pltpu.SemaphoreType.DMA((4 * with_kv + with_q,))],
+            compiler_params=pltpu.CompilerParams(vmem_limit_bytes=2 * 1024 * 1024),
             name="pack",
         )(*arguments, *after)
 
@@ -222,7 +222,7 @@
         carried = () if state is None else (state,)
         return pl.pallas_call(
             functools.partial(
-                attend_kernel, dims, tuple(b for b, _ in blocks), q_xor, store, bool(carried), len(after)
+                attend_kernel, dims, tuple(b for b, _ in blocks), q_xor, store, bool(carried)
             ),
             out_shape=out,
             in_specs=[SMEM] + [VMEM] * (1 + len(blocks) + len(carried)) + [ANY] * len(after),
@@ -237,7 +237,7 @@
     def merge(own, got, columns, out=None, after=()):
         aliased = () if out is None else (out,)
         return pl.pallas_call(
-            functools.partial(merge_kernel, dims, columns, bool(aliased)),
+            functools.partial(merge_kernel, dims, columns),
             out_shape=shape(queries.shape, bf16),
             in_specs=[VMEM] * 2 + [HBM] * len(aliased) + [ANY] * len(after),
             out_specs=HBM,
@@ -252,20 +252,20 @@
 
     kv0, q0 = pack(0, 1, 1, ())
     far_kv0, far_q0 = traded(kv0, 1), traded(q0, 2)
-    (kv1,) = pack(1, 1, 0, (kv0,))
-    far_kv1 = traded(kv1, 2)
+    kv1, q1 = pack(1, 1, 1, (kv0,))
+    far_kv1 = traded(kv1, 3)
     mine0 = work(q0, [(0, kv0)], 0, "state", after=(kv1,))
-    (q1,) = pack(1, 0, 1, (mine0,))
-    far_q1 = traded(q1, 1)
-    mine1 = work(q1, [(0, kv1)], 0, "state")
+    sent_q1, mine0 = lax.optimization_barrier((q1, mine0))
+    far_q1 = traded(sent_q1, 1)
+    mine1 = work(q1, [(0, kv1)], 0, "state", after=(mine0,))
     theirs0 = work(far_q0, [(0, kv0)], 2, "state", after=(mine1,))
     sent0 = work(far_q0, [(1, far_kv0)], 2, "sent", state=theirs0, after=(mine1,))
+    got0 = traded(sent0, 2)
     theirs1 = work(far_q1, [(0, kv1)], 1, "state", after=(sent0,))
-    got0 = traded(sent0, 2)
-    sent1 = work(far_q1, [(2, far_kv1)], 1, "sent", state=theirs1)
+    sent1 = work(far_q1, [(3, far_kv1)], 1, "sent", state=theirs1)
     got1 = traded(sent1, 1)
     own0 = work(q0, [(1, far_kv0)], 0, "own", state=mine0, after=(sent1,))
-    own1 = work(q1, [(2, far_kv1)], 0, "own", state=mine1, after=(own0,))
+    own1 = work(q1, [(3, far_kv1)], 0, "own", state=mine1, after=(own0,))
     out = merge(own0, got0, (0, 0, groups), after=(own1,))
     return merge(own1, got1, (groups, 0, groups), out)
 
@@ -358,6 +358,12 @@
     return result.reshape(query_rows, kv_width * groups).astype(jnp.bfloat16)
 
 
+def local(*arguments):
+    if lax.axis_size("ctx") == 4 and arguments[1].shape[1] == 2 * HEAD_DIM:
+        return local_four(*arguments)
+    return local_ring(*arguments)
+
+
 def solution(mesh):
     in_specs = (
         P(("dp", "ctx"), "tp"),
@@ -368,5 +374,4 @@
         P("dp"),
     )
     out_specs = P(("dp", "ctx"), "tp")
-    local = local_four if mesh.shape["ctx"] == 4 else local_ring
     return jax.shard_map(local, mesh=mesh, in_specs=in_specs, out_specs=out_specs, check_vma=False)

time: 33 us -> 32.7 us (level)
  waiting for transfers between devices: 11.1 us -> 13 us
  local copies, waits for them, and re-layouts: 1.68 us -> 0 us
  Pallas kernels: 10.6 us -> 9.82 us
  starting transfers between devices: 8.54 us -> 8.96 us
    ppermute x6, waiting for transfers between devices: 11.1 us -> 13 us  [traded(): lax.ppermute(value, 'ctx', [(source, source ^ xor) for source in range(co...]
    unnamed x10 -> x0, local copies, waits for them, and re-layouts: 1.68 us -> none
    pallas_call x3 -> x2, Pallas kernels: 3.04 us -> 2.21 us  [pack(): pl.pallas_call(functools.partial(pack_kernel, head, with_kv, with_q), out...]
    ppermute x6, starting transfers between devices: 8.54 us -> 8.96 us  [traded(): lax.ppermute(value, 'ctx', [(source, source ^ xor) for source in range(co...]
  transfers between devices with their start and end apart: 6 -> 6, of which waited for: 4 -> 5; matrix products, arithmetic and copies ran while one was open for 0% -> 0% of each run, Pallas kernels for 27% -> 24%
where the time goes in v5:
time: 32.7 us; the launch traced here: 32.6 us
  waiting for transfers between devices  13 us (40%)
  Pallas kernels  9.82 us (30%)
  starting transfers between devices  8.96 us (27%)
  between operations  0.76 us (2%)
    ppermute x6, waiting for transfers between devices, traded(): lax.ppermute(value, 'ctx', [(source, source ^ xor) for source in range(co...  13 us
    ppermute x6, starting transfers between devices, traded(): lax.ppermute(value, 'ctx', [(source, source ^ xor) for source in range(co...  8.96 us
    pallas_call x8, Pallas kernels, work(): pl.pallas_call(functools.partial(attend_kernel, dims, tuple((b for b, _ i...  6.01 us
    pallas_call x2, Pallas kernels, pack(): pl.pallas_call(functools.partial(pack_kernel, head, with_kv, with_q), out...  2.21 us
    pallas_call x2, Pallas kernels, merge(): pl.pallas_call(functools.partial(merge_kernel, dims, columns), out_shape=...  1.59 us
  transfers between devices with their start and end apart: 6, of which 5 were waited for; matrix products, arithmetic and copies ran while one was open for 0% of the time, Pallas kernels for 24%

profile of v5, /device:TPU:0, one launch (start us, length us, event | category | flops | bytes accessed | tf_op | source)
XLA Modules:
  0.0 32.6 jit_solution(14848783038253327551)
XLA Ops:
  0.0 1.1 %pack.2 = (bf16[1152,128]{1,0:T(8,128)(2,1)S(1)}, bf16[64,1024]{1,0:T(8,128)(2,1)S(1)}) custom-call(bf16[64,2048]{1,0:T(8,128)(2,1)} %refs_0_.3, bf16[512,256]{1,0:T(8,128)(2,1)} %refs_1_.3, bf16[512,256]{1,0:T(8,128)(2,1)} %refs_2_.3, bf16[64,256]{1,0:T(8,128)(2,1)} %refs_3_.3, bf16[64,256]{1,0:T(8,128)(2,1)} %refs_4_.3), custom_call_target="tpu_custom_call" | custom-call | tf_op jit(solution)/shard_map/pack/pallas_call | solution.py:205
  1.1 4.1 %collective-permute-start.3 = (bf16[64,1024]{1,0:T(8,128)(2,1)S(1)}, bf16[64,1024]{1,0:T(8,128)(2,1)S(1)}, u32[]{:S(2)}, u32[]{:S(2)}) collective-permute-start(bf16[64,1024]{1,0:T(8,128)(2,1)S(1)} %get-tuple-element.14.q_ref), channel_id=1, source_target_pairs={{0,16},{8,24},{16,0},{24,8},{1,17},{9,25},{17,1},{25,9},{2,18},{10... | collective-permute-start | bytes 393224 | tf_op jit(solution)/shard_map/ppermute | solution.py:185
  5.2 1.6 %collective-permute-start.1 = (bf16[1152,128]{1,0:T(8,128)(2,1)S(1)}, bf16[1152,128]{1,0:T(8,128)(2,1)S(1)}, u32[]{:S(2)}, u32[]{:S(2)}) collective-permute-start(bf16[1152,128]{1,0:T(8,128)(2,1)S(1)} %get-tuple-element.11.refs_5_.refs_0_), channel_id=1, source_target_pairs={{0,8},{8,0},{16,24},{24,16},{1,9},{9,1},{17,25},{25,17},{2,10},{10... | collective-permute-start | bytes 884744 | tf_op jit(solution)/shard_map/ppermute | solution.py:185
  6.8 1.1 %pack.3 = (bf16[1152,128]{1,0:T(8,128)(2,1)S(1)}, bf16[64,1024]{1,0:T(8,128)(2,1)S(1)}) custom-call(bf16[64,2048]{1,0:T(8,128)(2,1)} %refs_0_.3, bf16[512,256]{1,0:T(8,128)(2,1)} %refs_1_.3, bf16[512,256]{1,0:T(8,128)(2,1)} %refs_2_.3, bf16[64,256]{1,0:T(8,128)(2,1)} %refs_3_.3, bf16[64,256]{1,0:T(8,128)(2,1)} %refs_4_.3, ...), custom_call_target="tpu_custom_call" | custom-call | tf_op jit(solution)/shard_map/pack/pallas_call | solution.py:205
  7.9 0.1 collective-permute-start
  8.6 0.7 %work.8.refs_1_ = f32[136,512]{1,0:T(8,128)S(1)} custom-call(s32[1]{0:T(128)S(6)} %copy.9.len_ref, bf16[64,1024]{1,0:T(8,128)(2,1)S(1)} %get-tuple-element.14.q_ref, bf16[1152,128]{1,0:T(8,128)(2,1)S(1)} %get-tuple-element.11.refs_5_.refs_0_, bf16[1152,128]{1,0:T(8,128)(2,1)S(1)} %get-tuple-element.13.refs_1_.refs_0_), custom_call_target="tpu_custom_call" | custom-call | flops 6039797760 | bytes 1048576 | tf_op jit(solution)/shard_map/work/pallas_call | solution.py:223
  9.4 1.0 %collective-permute-start.2 = (bf16[64,1024]{1,0:T(8,128)(2,1)S(1)}, bf16[64,1024]{1,0:T(8,128)(2,1)S(1)}, u32[]{:S(2)}, u32[]{:S(2)}) collective-permute-start(bf16[64,1024]{1,0:T(8,128)(2,1)S(1)} %get-tuple-element.16.q_ref), channel_id=1, source_target_pairs={{0,8},{8,0},{16,24},{24,16},{1,9},{9,1},{17,25},{25,17},{2,10},{10... | collective-permute-start | bytes 393224 | tf_op jit(solution)/shard_map/ppermute | solution.py:185
  10.3 0.7 %work.9.refs_1_.refs_2_ = f32[136,512]{1,0:T(8,128)S(1)} custom-call(s32[1]{0:T(128)S(6)} %copy.9.len_ref, bf16[64,1024]{1,0:T(8,128)(2,1)S(1)} %get-tuple-element.16.q_ref, bf16[1152,128]{1,0:T(8,128)(2,1)S(1)} %get-tuple-element.13.refs_1_.refs_0_, f32[136,512]{1,0:T(8,128)S(1)} %work.8.refs_1_), custom_call_target="tpu_custom_call" | custom-call | flops 6039797760 | bytes 1048576 | tf_op jit(solution)/shard_map/work/pallas_call | solution.py:223
  11.1 1.3 %collective-permute-done.3.q_ref = bf16[64,1024]{1,0:T(8,128)(2,1)S(1)} collective-permute-done((bf16[64,1024]{1,0:T(8,128)(2,1)S(1)}, bf16[64,1024]{1,0:T(8,128)(2,1)S(1)}, u32[]{:S(2)}, u32[]{:S(2)}) %collective-permute-start.3) | collective-permute-done | bytes 131104 | tf_op jit(solution)/shard_map/ppermute | solution.py:185
  12.4 0.7 %work.10.refs_1_ = f32[136,512]{1,0:T(8,128)S(1)} custom-call(s32[1]{0:T(128)S(6)} %copy.9.len_ref, bf16[64,1024]{1,0:T(8,128)(2,1)S(1)} %collective-permute-done.3.q_ref, bf16[1152,128]{1,0:T(8,128)(2,1)S(1)} %get-tuple-element.11.refs_5_.refs_0_, f32[136,512]{1,0:T(8,128)S(1)} %work.9.refs_1_.refs_2_), custom_call_target="tpu_custom_call" | custom-call | flops 6039797760 | bytes 1048576 | tf_op jit(solution)/shard_map/work/pallas_call | solution.py:223
  13.1 9.4 %collective-permute-done.1.refs_0_ = bf16[1152,128]{1,0:T(8,128)(2,1)S(1)} collective-permute-done((bf16[1152,128]{1,0:T(8,128)(2,1)S(1)}, bf16[1152,128]{1,0:T(8,128)(2,1)S(1)}, u32[]{:S(2)}, u32[]{:S(2)}) %collective-permute-start.1) | collective-permute-done | bytes 294944 | tf_op jit(solution)/shard_map/ppermute | solution.py:185
  22.5 0.8 %work.11.refs_1_ = bf16[528,128]{1,0:T(8,128)(2,1)S(1)} custom-call(s32[1]{0:T(128)S(6)} %copy.9.len_ref, bf16[64,1024]{1,0:T(8,128)(2,1)S(1)} %collective-permute-done.3.q_ref, bf16[1152,128]{1,0:T(8,128)(2,1)S(1)} %collective-permute-done.1.refs_0_, f32[136,512]{1,0:T(8,128)S(1)} %work.10.refs_1_, f32[136,512]{1,0:T(8,128)S(1)} %work.9.refs_1_.refs_2_), custom_call_target="tpu_custom_call" | custom-call | flops 6039797760 | bytes 1048576 | tf_op jit(solution)/shard_map/work/pallas_call | solution.py:223
  23.3 0.2 collective-permute-start.5
  23.5 1.7 %collective-permute-done.2.q_ref = bf16[64,1024]{1,0:T(8,128)(2,1)S(1)} collective-permute-done((bf16[64,1024]{1,0:T(8,128)(2,1)S(1)}, bf16[64,1024]{1,0:T(8,128)(2,1)S(1)}, u32[]{:S(2)}, u32[]{:S(2)}) %collective-permute-start.2) | collective-permute-done | bytes 131104 | tf_op jit(solution)/shard_map/ppermute | solution.py:185
  25.1 0.8 %work.12.refs_1_ = f32[136,512]{1,0:T(8,128)S(1)} custom-call(s32[1]{0:T(128)S(6)} %copy.9.len_ref, bf16[64,1024]{1,0:T(8,128)(2,1)S(1)} %collective-permute-done.2.q_ref, bf16[1152,128]{1,0:T(8,128)(2,1)S(1)} %get-tuple-element.13.refs_1_.refs_0_, bf16[528,128]{1,0:T(8,128)(2,1)S(1)} %work.11.refs_1_), custom_call_target="tpu_custom_call" | custom-call | flops 6039797760 | bytes 1048576 | tf_op jit(solution)/shard_map/work/pallas_call | solution.py:223
  25.9 0.0 collective-permute-done.refs_0_
  25.9 0.8 %work.13.refs_2_ = bf16[528,128]{1,0:T(8,128)(2,1)S(1)} custom-call(s32[1]{0:T(128)S(6)} %copy.9.len_ref, bf16[64,1024]{1,0:T(8,128)(2,1)S(1)} %collective-permute-done.2.q_ref, bf16[1152,128]{1,0:T(8,128)(2,1)S(1)} %collective-permute-done.refs_0_, f32[136,512]{1,0:T(8,128)S(1)} %work.12.refs_1_), custom_call_target="tpu_custom_call" | custom-call | flops 6039797760 | bytes 1048576 | tf_op jit(solution)/shard_map/work/pallas_call | solution.py:223
  26.7 2.0 %collective-permute-start.4 = (bf16[528,128]{1,0:T(8,128)(2,1)S(1)}, bf16[528,128]{1,0:T(8,128)(2,1)S(1)}, u32[]{:S(2)}, u32[]{:S(2)}) collective-permute-start(bf16[528,128]{1,0:T(8,128)(2,1)S(1)} %work.13.refs_2_), channel_id=1, source_target_pairs={{0,8},{8,0},{16,24},{24,16},{1,9},{9,1},{17,25},{25,17},{2,10},{10... | collective-permute-start | bytes 405512 | tf_op jit(solution)/shard_map/ppermute | solution.py:185
  28.7 0.8 %work.14.refs_2_.own_ref = f32[136,512]{1,0:T(8,128)S(1)} custom-call(s32[1]{0:T(128)S(6)} %copy.9.len_ref, bf16[64,1024]{1,0:T(8,128)(2,1)S(1)} %get-tuple-element.14.q_ref, bf16[1152,128]{1,0:T(8,128)(2,1)S(1)} %collective-permute-done.1.refs_0_, f32[136,512]{1,0:T(8,128)S(1)} %work.8.refs_1_, bf16[528,128]{1,0:T(8,128)(2,1)S(1)} %work.13.refs_2_), custom_call_target="tpu_custom_call" | custom-call | flops 6039797760 | bytes 1048576 | tf_op jit(solution)/shard_map/work/pallas_call | solution.py:223
  29.5 0.8 %work.15.refs_0_.own_ref = f32[136,512]{1,0:T(8,128)S(1)} custom-call(s32[1]{0:T(128)S(6)} %copy.9.len_ref, bf16[64,1024]{1,0:T(8,128)(2,1)S(1)} %get-tuple-element.16.q_ref, bf16[1152,128]{1,0:T(8,128)(2,1)S(1)} %collective-permute-done.refs_0_, f32[136,512]{1,0:T(8,128)S(1)} %work.9.refs_1_.refs_2_, f32[136,512]{1,0:T(8,128)S(1)} %work.14.refs_2_.own_ref), custom_call_target="tpu_custom_call" | custom-call | flops 6039797760 | bytes 1048576 | tf_op jit(solution)/shard_map/work/pallas_call | solution.py:223
  30.2 0.1 collective-permute-done.5.got_ref
  30.3 0.8 %merge.2.refs_0_ = bf16[64,2048]{1,0:T(8,128)(2,1)} custom-call(f32[136,512]{1,0:T(8,128)S(1)} %work.14.refs_2_.own_ref, bf16[528,128]{1,0:T(8,128)(2,1)S(1)} %collective-permute-done.5.got_ref, f32[136,512]{1,0:T(8,128)S(1)} %work.15.refs_0_.own_ref), custom_call_target="tpu_custom_call" | custom-call | tf_op jit(solution)/shard_map/merge/pallas_call | solution.py:239
  31.1 0.6 %collective-permute-done.4.got_ref = bf16[528,128]{1,0:T(8,128)(2,1)S(1)} collective-permute-done((bf16[528,128]{1,0:T(8,128)(2,1)S(1)}, bf16[528,128]{1,0:T(8,128)(2,1)S(1)}, u32[]{:S(2)}, u32[]{:S(2)}) %collective-permute-start.4) | collective-permute-done | bytes 135200 | tf_op jit(solution)/shard_map/ppermute | solution.py:185
  31.8 0.8 %merge.3 = bf16[64,2048]{1,0:T(8,128)(2,1)} custom-call(f32[136,512]{1,0:T(8,128)S(1)} %work.15.refs_0_.own_ref, bf16[528,128]{1,0:T(8,128)(2,1)S(1)} %collective-permute-done.4.got_ref, bf16[64,2048]{1,0:T(8,128)(2,1)} %merge.2.refs_0_), custom_call_target="tpu_custom_call", output_to_operand_aliasing={{}: (2, {})} | custom-call | tf_op jit(solution)/shard_map/merge/pallas_call | solution.py:239
Async XLA Ops:
  1.1 11.2 %collective-permute-start.3 = (bf16[64,1024]{1,0:T(8,128)(2,1)S(1)}, bf16[64,1024]{1,0:T(8,128)(2,1)S(1)}, u32[]{:S(2)}, u32[]{:S(2)}) collective-permute-start(bf16[64,1024]{1,0:T(8,128)(2,1)S(1)} %get-tuple-element.14.q_ref), channel_id=1, source_target_pairs={{0,16},{8,24},{16,0},{24,8},{1,17},{9,25},{17,1},{25,9},{2,18},{10... | collective-permute-start | bytes 393224 | tf_op jit(solution)/shard_map/ppermute | solution.py:185
  5.2 17.3 %collective-permute-start.1 = (bf16[1152,128]{1,0:T(8,128)(2,1)S(1)}, bf16[1152,128]{1,0:T(8,128)(2,1)S(1)}, u32[]{:S(2)}, u32[]{:S(2)}) collective-permute-start(bf16[1152,128]{1,0:T(8,128)(2,1)S(1)} %get-tuple-element.11.refs_5_.refs_0_), channel_id=1, source_target_pairs={{0,8},{8,0},{16,24},{24,16},{1,9},{9,1},{17,25},{25,17},{2,10},{10... | collective-permute-start | bytes 884744 | tf_op jit(solution)/shard_map/ppermute | solution.py:185
  7.9 18.0 %collective-permute-start = (bf16[1152,128]{1,0:T(8,128)(2,1)S(1)}, bf16[1152,128]{1,0:T(8,128)(2,1)S(1)}, u32[]{:S(2)}, u32[]{:S(2)}) collective-permute-start(bf16[1152,128]{1,0:T(8,128)(2,1)S(1)} %get-tuple-element.13.refs_1_.refs_0_), channel_id=1, source_target_pairs={{0,24},{8,16},{16,8},{24,0},{1,25},{9,17},{17,9},{25,1},{2,26},{10... | collective-permute-start | bytes 884744 | tf_op jit(solution)/shard_map/ppermute | solution.py:185
  9.4 15.7 %collective-permute-start.2 = (bf16[64,1024]{1,0:T(8,128)(2,1)S(1)}, bf16[64,1024]{1,0:T(8,128)(2,1)S(1)}, u32[]{:S(2)}, u32[]{:S(2)}) collective-permute-start(bf16[64,1024]{1,0:T(8,128)(2,1)S(1)} %get-tuple-element.16.q_ref), channel_id=1, source_target_pairs={{0,8},{8,0},{16,24},{24,16},{1,9},{9,1},{17,25},{25,17},{2,10},{10... | collective-permute-start | bytes 393224 | tf_op jit(solution)/shard_map/ppermute | solution.py:185
  23.3 7.1 %collective-permute-start.5 = (bf16[528,128]{1,0:T(8,128)(2,1)S(1)}, bf16[528,128]{1,0:T(8,128)(2,1)S(1)}, u32[]{:S(2)}, u32[]{:S(2)}) collective-permute-start(bf16[528,128]{1,0:T(8,128)(2,1)S(1)} %work.11.refs_1_), channel_id=1, source_target_pairs={{0,16},{8,24},{16,0},{24,8},{1,17},{9,25},{17,1},{25,9},{2,18},{10... | collective-permute-start | bytes 405512 | tf_op jit(solution)/shard_map/ppermute | solution.py:185
  26.7 5.1 %collective-permute-start.4 = (bf16[528,128]{1,0:T(8,128)(2,1)S(1)}, bf16[528,128]{1,0:T(8,128)(2,1)S(1)}, u32[]{:S(2)}, u32[]{:S(2)}) collective-permute-start(bf16[528,128]{1,0:T(8,128)(2,1)S(1)} %work.13.refs_2_), channel_id=1, source_target_pairs={{0,8},{8,0},{16,24},{24,16},{1,9},{9,1},{17,25},{25,17},{2,10},{10... | collective-permute-start | bytes 405512 | tf_op jit(solution)/shard_map/ppermute | solution.py:185

commit v6 on v5

--- a/solution.py
+++ b/solution.py
@@ -18,9 +18,14 @@
 LIMIT = 24 * 1024 * 1024
 
 
-def attend(query, kv_ref, source, token_dev, length, cache_rows, new_rows):
+def attend(query, kv_refs, source, token_dev, length, cache_rows, new_rows):
     key_rows = cache_rows + new_rows
-    keys = kv_ref[0:key_rows, :]
+    if len(kv_refs) == 1:
+        keys, values = kv_refs[0][0:key_rows, :], kv_refs[0][key_rows : 2 * key_rows, :]
+    else:
+        old, fresh_rows = kv_refs
+        keys = jnp.concatenate([old[0:cache_rows, :], fresh_rows[0:new_rows, :]], 0)
+        values = jnp.concatenate([old[cache_rows:, :], fresh_rows[new_rows:, :]], 0)
     scores = lax.dot_general(
         keys, query, (((1,), (1,)), ((), ())), preferred_element_type=jnp.float32
     )
@@ -36,7 +41,6 @@
     top = jnp.max(scores, axis=0, keepdims=True)
     weights = jnp.exp2((scores - top) * SLOPE)
     total = jnp.sum(weights, axis=0, keepdims=True)
-    values = kv_ref[key_rows : 2 * key_rows, :]
     summed = lax.dot_general(
         values,
         weights.astype(jnp.bfloat16),
@@ -99,15 +103,18 @@
 
 def attend_kernel(dims, blocks, q_xor, store, carried, len_ref, q_ref, *refs):
     cache_rows, new_rows, step = dims
-    kv_refs, out_ref = refs[: len(blocks)], refs[-1]
+    out_ref, kv_refs = refs[-1], []
+    for _, count in blocks:
+        kv_refs.append(refs[:count])
+        refs = refs[count:]
     me = lax.axis_index("ctx")
     groups = q_ref.shape[1] // HEAD_DIM
     sent = []
     for at in range(0, groups, step):
         query = stacked_heads(q_ref, at, step)
         lanes = pl.ds(at * new_rows, step * new_rows)
-        state = load_state(refs[len(blocks)], lanes) if carried else None
-        for block, kv_ref in zip(blocks, kv_refs):
+        state = load_state(refs[0], lanes) if carried else None
+        for (block, _), kv_ref in zip(blocks, kv_refs):
             ours = attend(
                 query, kv_ref, me ^ block, me ^ q_xor, len_ref[0], cache_rows, new_rows
             )
@@ -151,25 +158,21 @@
     copy.wait()
 
 
-def pack_kernel(head, with_kv, with_q, *refs):
-    q_ref, ck_ref, cv_ref, nk_ref, nv_ref = refs[:5]
-    sems, outs = refs[-1], list(refs[-1 - with_kv - with_q : -1])
+def pack_kernel(head, apart, q_ref, ck_ref, cv_ref, nk_ref, nv_ref, *refs):
+    sems, outs = refs[-1], refs[-3 - apart : -1]
     cache_rows, new_rows = ck_ref.shape[0], nk_ref.shape[0]
     key_rows = cache_rows + new_rows
     columns = pl.ds(head * HEAD_DIM, HEAD_DIM)
-    copies = []
-    if with_kv:
-        kv = outs.pop(0)
-        for source, at, rows in (
-            (ck_ref, 0, cache_rows),
-            (nk_ref, cache_rows, new_rows),
-            (cv_ref, key_rows, cache_rows),
-            (nv_ref, key_rows + cache_rows, new_rows),
-        ):
-            copies.append((source.at[:, columns], kv.at[pl.ds(at, rows), :]))
-    if with_q:
-        width = outs[0].shape[1]
-        copies.append((q_ref.at[:, pl.ds(head * width, width)], outs[0]))
+    if apart:
+        places = ((0, 0), (0, cache_rows), (1, 0), (1, new_rows))
+    else:
+        places = ((0, 0), (0, key_rows), (0, cache_rows), (0, key_rows + cache_rows))
+    copies = [
+        (source.at[:, columns], outs[array].at[pl.ds(at, source.shape[0]), :])
+        for source, (array, at) in zip((ck_ref, cv_ref, nk_ref, nv_ref), places)
+    ]
+    width = outs[-1].shape[1]
+    copies.append((q_ref.at[:, pl.ds(head * width, width)], outs[-1]))
     handles = [
         pltpu.make_async_copy(source, target, sems.at[n])
         for n, (source, target) in enumerate(copies)
@@ -180,9 +183,9 @@
         handle.wait()
 
 
-def traded(value, xor):
-    count = lax.axis_size("ctx")
-    return lax.ppermute(value, "ctx", [(source, source ^ xor) for source in range(count)])
+def traded(value, xor, onward=False):
+    pairs = [(source, source ^ xor) for source in range(lax.axis_size("ctx"))]
+    return lax.ppermute(value, "ctx", [(a, b) for a, b in pairs if a < b or not onward])
 
 
 def local_four(queries, cache_keys, cache_values, new_keys, new_values, prefix_len):
@@ -199,15 +202,15 @@
         for argument in (queries, cache_keys, cache_values, new_keys, new_values)
     ]
 
-    def pack(head, with_kv, with_q, after):
-        outs = [pltpu.VMEM((2 * key_rows, HEAD_DIM), bf16)] * with_kv
-        outs += [pltpu.VMEM((new_rows, groups * HEAD_DIM), bf16)] * with_q
+    def pack(head, apart, after):
+        rows = [2 * cache_rows, 2 * new_rows] if apart else [2 * key_rows]
         return pl.pallas_call(
-            functools.partial(pack_kernel, head, with_kv, with_q),
-            out_shape=outs,
+            functools.partial(pack_kernel, head, apart),
+            out_shape=[pltpu.VMEM((n, HEAD_DIM), bf16) for n in rows]
+            + [pltpu.VMEM((new_rows, groups * HEAD_DIM), bf16)],
             in_specs=[HBM] * 5 + [ANY] * len(after),
-            out_specs=[VMEM] * len(outs),
-            scratch_shapes=[pltpu.SemaphoreType.DMA((4 * with_kv + with_q,))],
+            out_specs=[VMEM] * (len(rows) + 1),
+            scratch_shapes=[pltpu.SemaphoreType.DMA((5,))],
             compiler_params=pltpu.CompilerParams(vmem_limit_bytes=2 * 1024 * 1024),
             name="pack",
         )(*arguments, *after)
@@ -220,19 +223,20 @@
         else:
             out = pltpu.VMEM((HEAD_DIM + 8, rows), f32)
         carried = () if state is None else (state,)
+        refs = [r for _, ref in blocks for r in ref]
         return pl.pallas_call(
             functools.partial(
-                attend_kernel, dims, tuple(b for b, _ in blocks), q_xor, store, bool(carried)
+                attend_kernel, dims, tuple((b, len(ref)) for b, ref in blocks), q_xor, store, bool(carried)
             ),
             out_shape=out,
-            in_specs=[SMEM] + [VMEM] * (1 + len(blocks) + len(carried)) + [ANY] * len(after),
+            in_specs=[SMEM] + [VMEM] * (1 + len(refs) + len(carried)) + [ANY] * len(after),
             out_specs=VMEM,
             compiler_params=pltpu.CompilerParams(vmem_limit_bytes=LIMIT),
             cost_estimate=pl.CostEstimate(
                 flops=4 * HEAD_DIM * pairs * 40, bytes_accessed=1 << 20, transcendentals=pairs
             ),
             name="work",
-        )(prefix_len, query, *[ref for _, ref in blocks], *carried, *after)
+        )(prefix_len, query, *refs, *carried, *after)
 
     def merge(own, got, columns, out=None, after=()):
         aliased = () if out is None else (out,)
@@ -250,22 +254,24 @@
             name="merge",
         )(own, got, *aliased, *after)
 
-    kv0, q0 = pack(0, 1, 1, ())
+    kv0, q0 = pack(0, 0, ())
     far_kv0, far_q0 = traded(kv0, 1), traded(q0, 2)
-    kv1, q1 = pack(1, 1, 1, (kv0,))
-    far_kv1 = traded(kv1, 3)
-    mine0 = work(q0, [(0, kv0)], 0, "state", after=(kv1,))
+    old1, new1, q1 = pack(1, 1, (kv0,))
+    far_old1 = traded(old1, 3)
+    mine0 = work(q0, [(0, (kv0,))], 0, "state", after=(old1,))
     sent_q1, mine0 = lax.optimization_barrier((q1, mine0))
     far_q1 = traded(sent_q1, 1)
-    mine1 = work(q1, [(0, kv1)], 0, "state", after=(mine0,))
-    theirs0 = work(far_q0, [(0, kv0)], 2, "state", after=(mine1,))
-    sent0 = work(far_q0, [(1, far_kv0)], 2, "sent", state=theirs0, after=(mine1,))
+    mine1 = work(q1, [(0, (old1, new1))], 0, "state", after=(mine0,))
+    sent_new1, mine1 = lax.optimization_barrier((new1, mine1))
+    far_new1 = traded(sent_new1, 3, True)
+    theirs0 = work(far_q0, [(0, (kv0,))], 2, "state", after=(mine1,))
+    sent0 = work(far_q0, [(1, (far_kv0,))], 2, "sent", state=theirs0, after=(mine1,))
     got0 = traded(sent0, 2)
-    theirs1 = work(far_q1, [(0, kv1)], 1, "state", after=(sent0,))
-    sent1 = work(far_q1, [(3, far_kv1)], 1, "sent", state=theirs1)
+    theirs1 = work(far_q1, [(0, (old1, new1))], 1, "state", after=(sent0,))
+    sent1 = work(far_q1, [(3, (far_old1, far_new1))], 1, "sent", state=theirs1)
     got1 = traded(sent1, 1)
-    own0 = work(q0, [(1, far_kv0)], 0, "own", state=mine0, after=(sent1,))
-    own1 = work(q1, [(3, far_kv1)], 0, "own", state=mine1, after=(own0,))
+    own0 = work(q0, [(1, (far_kv0,))], 0, "own", state=mine0, after=(sent1,))
+    own1 = work(q1, [(3, (far_old1, far_new1))], 0, "own", state=mine1, after=(own0,))
     out = merge(own0, got0, (0, 0, groups), after=(own1,))
     return merge(own1, got1, (groups, 0, groups), out)
 

time: 32.7 us -> 32.8 us (level)
  starting transfers between devices: 8.96 us -> 12.9 us
  waiting for transfers between devices: 13 us -> 9.15 us
    ppermute x6 -> x7, starting transfers between devices: 8.96 us -> 12.9 us  [traded(): lax.ppermute(value, 'ctx', [(a, b) for a, b in pairs if a < b or not onwa...]
    ppermute x6 -> x7, waiting for transfers between devices: 13 us -> 9.15 us  [traded(): lax.ppermute(value, 'ctx', [(a, b) for a, b in pairs if a < b or not onwa...]
  transfers between devices with their start and end apart: 6 -> 7, of which waited for: 5 -> 4; matrix products, arithmetic and copies ran while one was open for 0% -> 0% of each run, Pallas kernels for 24% -> 24%
where the time goes in v6:
time: 32.8 us; the launch traced here: 32.6 us
  starting transfers between devices  12.9 us (39%)
  Pallas kernels  9.8 us (30%)
  waiting for transfers between devices  9.15 us (28%)
  between operations  0.79 us (2%)
    ppermute x7, starting transfers between devices, traded(): lax.ppermute(value, 'ctx', [(a, b) for a, b in pairs if a < b or not onwa...  12.9 us
    ppermute x7, waiting for transfers between devices, traded(): lax.ppermute(value, 'ctx', [(a, b) for a, b in pairs if a < b or not onwa...  9.15 us
    pallas_call x8, Pallas kernels, work(): pl.pallas_call(functools.partial(attend_kernel, dims, tuple(((b, len(ref)...  5.99 us
    pallas_call x2, Pallas kernels, pack(): pl.pallas_call(functools.partial(pack_kernel, head, apart), out_shape=[pl...  2.21 us
    pallas_call x2, Pallas kernels, merge(): pl.pallas_call(functools.partial(merge_kernel, dims, columns), out_shape=...  1.59 us
  transfers between devices with their start and end apart: 7, of which 4 were waited for; matrix products, arithmetic and copies ran while one was open for 0% of the time, Pallas kernels for 24%

profile of v6, /device:TPU:0, one launch (start us, length us, event | category | flops | bytes accessed | tf_op | source)
XLA Modules:
  0.0 32.6 jit_solution(3975759177373873644)
XLA Ops:
  0.0 1.1 %pack.2 = (bf16[1152,128]{1,0:T(8,128)(2,1)S(1)}, bf16[64,1024]{1,0:T(8,128)(2,1)S(1)}) custom-call(bf16[64,2048]{1,0:T(8,128)(2,1)} %q_ref.3, bf16[512,256]{1,0:T(8,128)(2,1)} %ck_ref.3, bf16[512,256]{1,0:T(8,128)(2,1)} %cv_ref.3, bf16[64,256]{1,0:T(8,128)(2,1)} %nk_ref.3, bf16[64,256]{1,0:T(8,128)(2,1)} %nv_ref.3), custom_call_target="tpu_custom_call" | custom-call | tf_op jit(solution)/shard_map/pack/pallas_call | solution.py:207
  1.1 4.1 %collective-permute-start.4 = (bf16[64,1024]{1,0:T(8,128)(2,1)S(1)}, bf16[64,1024]{1,0:T(8,128)(2,1)S(1)}, u32[]{:S(2)}, u32[]{:S(2)}) collective-permute-start(bf16[64,1024]{1,0:T(8,128)(2,1)S(1)} %get-tuple-element.18.q_ref), channel_id=1, source_target_pairs={{0,16},{8,24},{16,0},{24,8},{1,17},{9,25},{17,1},{25,9},{2,18},{10... | collective-permute-start | bytes 393224 | tf_op jit(solution)/shard_map/ppermute | solution.py:188
  5.2 1.6 %collective-permute-start.2 = (bf16[1152,128]{1,0:T(8,128)(2,1)S(1)}, bf16[1152,128]{1,0:T(8,128)(2,1)S(1)}, u32[]{:S(2)}, u32[]{:S(2)}) collective-permute-start(bf16[1152,128]{1,0:T(8,128)(2,1)S(1)} %get-tuple-element.14.refs_0_), channel_id=1, source_target_pairs={{0,8},{8,0},{16,24},{24,16},{1,9},{9,1},{17,25},{25,17},{2,10},{10... | collective-permute-start | bytes 884744 | tf_op jit(solution)/shard_map/ppermute | solution.py:188
  6.8 1.1 %pack.3 = (bf16[1024,128]{1,0:T(8,128)(2,1)S(1)}, bf16[128,128]{1,0:T(8,128)(2,1)S(1)}, bf16[64,1024]{1,0:T(8,128)(2,1)S(1)}) custom-call(bf16[64,2048]{1,0:T(8,128)(2,1)} %q_ref.3, bf16[512,256]{1,0:T(8,128)(2,1)} %ck_ref.3, bf16[512,256]{1,0:T(8,128)(2,1)} %cv_ref.3, bf16[64,256]{1,0:T(8,128)(2,1)} %nk_ref.3, bf16[64,256]{1,0:T(8,128)(2,1)} %nv_ref.3, ...), custom_call_target="tpu_custom_call" | custom-call | tf_op jit(solution)/shard_map/pack/pallas_call | solution.py:207
  7.9 0.1 collective-permute-start
  8.6 0.7 %work.8.refs_2_.refs_1_ = f32[136,512]{1,0:T(8,128)S(1)} custom-call(s32[1]{0:T(128)S(6)} %copy.9.len_ref, bf16[64,1024]{1,0:T(8,128)(2,1)S(1)} %get-tuple-element.18.q_ref, bf16[1152,128]{1,0:T(8,128)(2,1)S(1)} %get-tuple-element.14.refs_0_, bf16[1024,128]{1,0:T(8,128)(2,1)S(1)} %get-tuple-element.16.refs_1_.refs_0_), custom_call_target="tpu_custom_call" | custom-call | flops 6039797760 | bytes 1048576 | tf_op jit(solution)/shard_map/work/pallas_call | solution.py:227
  9.4 1.0 %collective-permute-start.3 = (bf16[64,1024]{1,0:T(8,128)(2,1)S(1)}, bf16[64,1024]{1,0:T(8,128)(2,1)S(1)}, u32[]{:S(2)}, u32[]{:S(2)}) collective-permute-start(bf16[64,1024]{1,0:T(8,128)(2,1)S(1)} %get-tuple-element.22.q_ref), channel_id=1, source_target_pairs={{0,8},{8,0},{16,24},{24,16},{1,9},{9,1},{17,25},{25,17},{2,10},{10... | collective-permute-start | bytes 393224 | tf_op jit(solution)/shard_map/ppermute | solution.py:188
  10.3 0.7 %work.9.refs_1_.refs_2_ = f32[136,512]{1,0:T(8,128)S(1)} custom-call(s32[1]{0:T(128)S(6)} %copy.9.len_ref, bf16[64,1024]{1,0:T(8,128)(2,1)S(1)} %get-tuple-element.22.q_ref, bf16[1024,128]{1,0:T(8,128)(2,1)S(1)} %get-tuple-element.16.refs_1_.refs_0_, bf16[128,128]{1,0:T(8,128)(2,1)S(1)} %get-tuple-element.20.refs_1_, f32[136,512]{1,0:T(8,128)S(1)} %work.8.refs_2_.refs_1_), custom_call_target="tpu_custom_call" | custom-call | flops 6039797760 | bytes 1048576 | tf_op jit(solution)/shard_map/work/pallas_call | solution.py:227
  11.1 4.8 %collective-permute-start.1 = (bf16[128,128]{1,0:T(8,128)(2,1)S(1)}, bf16[128,128]{1,0:T(8,128)(2,1)S(1)}, u32[]{:S(2)}, u32[]{:S(2)}) collective-permute-start(bf16[128,128]{1,0:T(8,128)(2,1)S(1)} %get-tuple-element.20.refs_1_), channel_id=1, source_target_pairs={{0,24},{8,16},{1,25},{9,17},{2,26},{10,18},{3,27},{11,19},{4,28},{... | collective-permute-start | bytes 98312 | tf_op jit(solution)/shard_map/ppermute | solution.py:188
  15.9 0.0 collective-permute-done.4.q_ref
  16.0 0.7 %work.10.refs_1_ = f32[136,512]{1,0:T(8,128)S(1)} custom-call(s32[1]{0:T(128)S(6)} %copy.9.len_ref, bf16[64,1024]{1,0:T(8,128)(2,1)S(1)} %collective-permute-done.4.q_ref, bf16[1152,128]{1,0:T(8,128)(2,1)S(1)} %get-tuple-element.14.refs_0_, f32[136,512]{1,0:T(8,128)S(1)} %work.9.refs_1_.refs_2_), custom_call_target="tpu_custom_call" | custom-call | flops 6039797760 | bytes 1048576 | tf_op jit(solution)/shard_map/work/pallas_call | solution.py:227
  16.7 5.9 %collective-permute-done.2.refs_0_ = bf16[1152,128]{1,0:T(8,128)(2,1)S(1)} collective-permute-done((bf16[1152,128]{1,0:T(8,128)(2,1)S(1)}, bf16[1152,128]{1,0:T(8,128)(2,1)S(1)}, u32[]{:S(2)}, u32[]{:S(2)}) %collective-permute-start.2) | collective-permute-done | bytes 294944 | tf_op jit(solution)/shard_map/ppermute | solution.py:188
  22.6 0.8 %work.11.refs_2_ = bf16[528,128]{1,0:T(8,128)(2,1)S(1)} custom-call(s32[1]{0:T(128)S(6)} %copy.9.len_ref, bf16[64,1024]{1,0:T(8,128)(2,1)S(1)} %collective-permute-done.4.q_ref, bf16[1152,128]{1,0:T(8,128)(2,1)S(1)} %collective-permute-done.2.refs_0_, f32[136,512]{1,0:T(8,128)S(1)} %work.10.refs_1_, f32[136,512]{1,0:T(8,128)S(1)} %work.9.refs_1_.refs_2_), custom_call_target="tpu_custom_call" | custom-call | flops 6039797760 | bytes 1048576 | tf_op jit(solution)/shard_map/work/pallas_call | solution.py:227
  23.4 0.1 collective-permute-start.6
  23.5 1.7 %collective-permute-done.3.q_ref = bf16[64,1024]{1,0:T(8,128)(2,1)S(1)} collective-permute-done((bf16[64,1024]{1,0:T(8,128)(2,1)S(1)}, bf16[64,1024]{1,0:T(8,128)(2,1)S(1)}, u32[]{:S(2)}, u32[]{:S(2)}) %collective-permute-start.3) | collective-permute-done | bytes 131104 | tf_op jit(solution)/shard_map/ppermute | solution.py:188
  25.2 0.7 %work.12.refs_2_ = f32[136,512]{1,0:T(8,128)S(1)} custom-call(s32[1]{0:T(128)S(6)} %copy.9.len_ref, bf16[64,1024]{1,0:T(8,128)(2,1)S(1)} %collective-permute-done.3.q_ref, bf16[1024,128]{1,0:T(8,128)(2,1)S(1)} %get-tuple-element.16.refs_1_.refs_0_, bf16[128,128]{1,0:T(8,128)(2,1)S(1)} %get-tuple-element.20.refs_1_, bf16[528,128]{1,0:T(8,128)(2,1)S(1)} %work.11.refs_2_), custom_call_target="tpu_custom_call" | custom-call | flops 6039797760 | bytes 1048576 | tf_op jit(solution)/shard_map/work/pallas_call | solution.py:227
  26.0 0.0 collective-permute-done.1.refs_1_
  26.0 0.0 collective-permute-done.refs_0_
  26.0 0.8 %work.13.refs_2_ = bf16[528,128]{1,0:T(8,128)(2,1)S(1)} custom-call(s32[1]{0:T(128)S(6)} %copy.9.len_ref, bf16[64,1024]{1,0:T(8,128)(2,1)S(1)} %collective-permute-done.3.q_ref, bf16[1024,128]{1,0:T(8,128)(2,1)S(1)} %collective-permute-done.refs_0_, bf16[128,128]{1,0:T(8,128)(2,1)S(1)} %collective-permute-done.1.refs_1_, f32[136,512]{1,0:T(8,128)S(1)} %work.12.refs_2_), custom_call_target="tpu_custom_call" | custom-call | flops 6039797760 | bytes 1048576 | tf_op jit(solution)/shard_map/work/pallas_call | solution.py:227
  26.7 1.3 %collective-permute-start.5 = (bf16[528,128]{1,0:T(8,128)(2,1)S(1)}, bf16[528,128]{1,0:T(8,128)(2,1)S(1)}, u32[]{:S(2)}, u32[]{:S(2)}) collective-permute-start(bf16[528,128]{1,0:T(8,128)(2,1)S(1)} %work.13.refs_2_), channel_id=1, source_target_pairs={{0,8},{8,0},{16,24},{24,16},{1,9},{9,1},{17,25},{25,17},{2,10},{10... | collective-permute-start | bytes 405512 | tf_op jit(solution)/shard_map/ppermute | solution.py:188
  28.0 0.8 %work.14.refs_3_.own_ref = f32[136,512]{1,0:T(8,128)S(1)} custom-call(s32[1]{0:T(128)S(6)} %copy.9.len_ref, bf16[64,1024]{1,0:T(8,128)(2,1)S(1)} %get-tuple-element.18.q_ref, bf16[1152,128]{1,0:T(8,128)(2,1)S(1)} %collective-permute-done.2.refs_0_, f32[136,512]{1,0:T(8,128)S(1)} %work.8.refs_2_.refs_1_, bf16[528,128]{1,0:T(8,128)(2,1)S(1)} %work.13.refs_2_), custom_call_target="tpu_custom_call" | custom-call | flops 6039797760 | bytes 1048576 | tf_op jit(solution)/shard_map/work/pallas_call | solution.py:227
  28.8 0.8 %work.15.refs_0_.own_ref = f32[136,512]{1,0:T(8,128)S(1)} custom-call(s32[1]{0:T(128)S(6)} %copy.9.len_ref, bf16[64,1024]{1,0:T(8,128)(2,1)S(1)} %get-tuple-element.22.q_ref, bf16[1024,128]{1,0:T(8,128)(2,1)S(1)} %collective-permute-done.refs_0_, bf16[128,128]{1,0:T(8,128)(2,1)S(1)} %collective-permute-done.1.refs_1_, f32[136,512]{1,0:T(8,128)S(1)} %work.9.refs_1_.refs_2_, ...), custom_call_target="tpu_custom_call" | custom-call | flops 6039797760 | bytes 1048576 | tf_op jit(solution)/shard_map/work/pallas_call | solution.py:227
  29.5 0.1 collective-permute-done.6.got_ref
  29.6 0.8 %merge.2.refs_0_ = bf16[64,2048]{1,0:T(8,128)(2,1)} custom-call(f32[136,512]{1,0:T(8,128)S(1)} %work.14.refs_3_.own_ref, bf16[528,128]{1,0:T(8,128)(2,1)S(1)} %collective-permute-done.6.got_ref, f32[136,512]{1,0:T(8,128)S(1)} %work.15.refs_0_.own_ref), custom_call_target="tpu_custom_call" | custom-call | tf_op jit(solution)/shard_map/merge/pallas_call | solution.py:243
  30.4 1.4 %collective-permute-done.5.got_ref = bf16[528,128]{1,0:T(8,128)(2,1)S(1)} collective-permute-done((bf16[528,128]{1,0:T(8,128)(2,1)S(1)}, bf16[528,128]{1,0:T(8,128)(2,1)S(1)}, u32[]{:S(2)}, u32[]{:S(2)}) %collective-permute-start.5) | collective-permute-done | bytes 135200 | tf_op jit(solution)/shard_map/ppermute | solution.py:188
  31.8 0.8 %merge.3 = bf16[64,2048]{1,0:T(8,128)(2,1)} custom-call(f32[136,512]{1,0:T(8,128)S(1)} %work.15.refs_0_.own_ref, bf16[528,128]{1,0:T(8,128)(2,1)S(1)} %collective-permute-done.5.got_ref, bf16[64,2048]{1,0:T(8,128)(2,1)} %merge.2.refs_0_), custom_call_target="tpu_custom_call", output_to_operand_aliasing={{}: (2, {})} | custom-call | tf_op jit(solution)/shard_map/merge/pallas_call | solution.py:243
Async XLA Ops:
  1.1 14.8 %collective-permute-start.4 = (bf16[64,1024]{1,0:T(8,128)(2,1)S(1)}, bf16[64,1024]{1,0:T(8,128)(2,1)S(1)}, u32[]{:S(2)}, u32[]{:S(2)}) collective-permute-start(bf16[64,1024]{1,0:T(8,128)(2,1)S(1)} %get-tuple-element.18.q_ref), channel_id=1, source_target_pairs={{0,16},{8,24},{16,0},{24,8},{1,17},{9,25},{17,1},{25,9},{2,18},{10... | collective-permute-start | bytes 393224 | tf_op jit(solution)/shard_map/ppermute | solution.py:188
  5.2 17.4 %collective-permute-start.2 = (bf16[1152,128]{1,0:T(8,128)(2,1)S(1)}, bf16[1152,128]{1,0:T(8,128)(2,1)S(1)}, u32[]{:S(2)}, u32[]{:S(2)}) collective-permute-start(bf16[1152,128]{1,0:T(8,128)(2,1)S(1)} %get-tuple-element.14.refs_0_), channel_id=1, source_target_pairs={{0,8},{8,0},{16,24},{24,16},{1,9},{9,1},{17,25},{25,17},{2,10},{10... | collective-permute-start | bytes 884744 | tf_op jit(solution)/shard_map/ppermute | solution.py:188
  7.9 18.1 %collective-permute-start = (bf16[1024,128]{1,0:T(8,128)(2,1)S(1)}, bf16[1024,128]{1,0:T(8,128)(2,1)S(1)}, u32[]{:S(2)}, u32[]{:S(2)}) collective-permute-start(bf16[1024,128]{1,0:T(8,128)(2,1)S(1)} %get-tuple-element.16.refs_1_.refs_0_), channel_id=1, source_target_pairs={{0,24},{8,16},{16,8},{24,0},{1,25},{9,17},{17,9},{25,1},{2,26},{10... | collective-permute-start | bytes 786440 | tf_op jit(solution)/shard_map/ppermute | solution.py:188
  9.4 15.8 %collective-permute-start.3 = (bf16[64,1024]{1,0:T(8,128)(2,1)S(1)}, bf16[64,1024]{1,0:T(8,128)(2,1)S(1)}, u32[]{:S(2)}, u32[]{:S(2)}) collective-permute-start(bf16[64,1024]{1,0:T(8,128)(2,1)S(1)} %get-tuple-element.22.q_ref), channel_id=1, source_target_pairs={{0,8},{8,0},{16,24},{24,16},{1,9},{9,1},{17,25},{25,17},{2,10},{10... | collective-permute-start | bytes 393224 | tf_op jit(solution)/shard_map/ppermute | solution.py:188
  11.1 14.9 %collective-permute-start.1 = (bf16[128,128]{1,0:T(8,128)(2,1)S(1)}, bf16[128,128]{1,0:T(8,128)(2,1)S(1)}, u32[]{:S(2)}, u32[]{:S(2)}) collective-permute-start(bf16[128,128]{1,0:T(8,128)(2,1)S(1)} %get-tuple-element.20.refs_1_), channel_id=1, source_target_pairs={{0,24},{8,16},{1,25},{9,17},{2,26},{10,18},{3,27},{11,19},{4,28},{... | collective-permute-start | bytes 98312 | tf_op jit(solution)/shard_map/ppermute | solution.py:188
  23.4 6.2 %collective-permute-start.6 = (bf16[528,128]{1,0:T(8,128)(2,1)S(1)}, bf16[528,128]{1,0:T(8,128)(2,1)S(1)}, u32[]{:S(2)}, u32[]{:S(2)}) collective-permute-start(bf16[528,128]{1,0:T(8,128)(2,1)S(1)} %work.11.refs_2_), channel_id=1, source_target_pairs={{0,16},{8,24},{16,0},{24,8},{1,17},{9,25},{17,1},{25,9},{2,18},{10... | collective-permute-start | bytes 405512 | tf_op jit(solution)/shard_map/ppermute | solution.py:188
  26.7 5.1 %collective-permute-start.5 = (bf16[528,128]{1,0:T(8,128)(2,1)S(1)}, bf16[528,128]{1,0:T(8,128)(2,1)S(1)}, u32[]{:S(2)}, u32[]{:S(2)}) collective-permute-start(bf16[528,128]{1,0:T(8,128)(2,1)S(1)} %work.13.refs_2_), channel_id=1, source_target_pairs={{0,8},{8,0},{16,24},{24,16},{1,9},{9,1},{17,25},{25,17},{2,10},{10... | collective-permute-start | bytes 405512 | tf_op jit(solution)/shard_map/ppermute | solution.py:188

commit v7 on v6

--- a/solution.py
+++ b/solution.py
@@ -257,21 +257,20 @@
     kv0, q0 = pack(0, 0, ())
     far_kv0, far_q0 = traded(kv0, 1), traded(q0, 2)
     old1, new1, q1 = pack(1, 1, (kv0,))
-    far_old1 = traded(old1, 3)
+    far_old1 = traded(old1, 2)
     mine0 = work(q0, [(0, (kv0,))], 0, "state", after=(old1,))
-    sent_q1, mine0 = lax.optimization_barrier((q1, mine0))
+    mine1 = work(q1, [(0, (old1, new1))], 0, "state", after=(mine0,))
+    sent_q1, mine1 = lax.optimization_barrier((q1, mine1))
     far_q1 = traded(sent_q1, 1)
-    mine1 = work(q1, [(0, (old1, new1))], 0, "state", after=(mine0,))
-    sent_new1, mine1 = lax.optimization_barrier((new1, mine1))
-    far_new1 = traded(sent_new1, 3, True)
     theirs0 = work(far_q0, [(0, (kv0,))], 2, "state", after=(mine1,))
+    sent_new1, theirs0 = lax.optimization_barrier((new1, theirs0))
+    far_new1 = traded(sent_new1, 2, True)
     sent0 = work(far_q0, [(1, (far_kv0,))], 2, "sent", state=theirs0, after=(mine1,))
     got0 = traded(sent0, 2)
-    theirs1 = work(far_q1, [(0, (old1, new1))], 1, "state", after=(sent0,))
-    sent1 = work(far_q1, [(3, (far_old1, far_new1))], 1, "sent", state=theirs1)
+    sent1 = work(far_q1, [(0, (old1, new1)), (2, (far_old1, far_new1))], 1, "sent", after=(sent0,))
     got1 = traded(sent1, 1)
     own0 = work(q0, [(1, (far_kv0,))], 0, "own", state=mine0, after=(sent1,))
-    own1 = work(q1, [(3, (far_old1, far_new1))], 0, "own", state=mine1, after=(own0,))
+    own1 = work(q1, [(2, (far_old1, far_new1))], 0, "own", state=mine1, after=(own0,))
     out = merge(own0, got0, (0, 0, groups), after=(own1,))
     return merge(own1, got1, (groups, 0, groups), out)
 

time: 32.8 us -> 32.5 us (level)
  starting transfers between devices: 12.9 us -> 11 us
  waiting for transfers between devices: 9.15 us -> 10.9 us
    ppermute x7, starting transfers between devices: 12.9 us -> 11 us  [traded(): lax.ppermute(value, 'ctx', [(a, b) for a, b in pairs if a < b or not onwa...]
    ppermute x7, waiting for transfers between devices: 9.15 us -> 10.9 us  [traded(): lax.ppermute(value, 'ctx', [(a, b) for a, b in pairs if a < b or not onwa...]
    pallas_call x8 -> x7, Pallas kernels: 5.99 us -> 5.86 us  [work(): pl.pallas_call(functools.partial(attend_kernel, dims, tuple(((b, len(ref)...]
where the time goes in v7:
time: 32.5 us; the launch traced here: 32.3 us
  starting transfers between devices  11 us (34%)
  waiting for transfers between devices  10.9 us (34%)
  Pallas kernels  9.67 us (30%)
  between operations  0.76 us (2%)
    ppermute x7, starting transfers between devices, traded(): lax.ppermute(value, 'ctx', [(a, b) for a, b in pairs if a < b or not onwa...  11 us
    ppermute x7, waiting for transfers between devices, traded(): lax.ppermute(value, 'ctx', [(a, b) for a, b in pairs if a < b or not onwa...  10.9 us
    pallas_call x7, Pallas kernels, work(): pl.pallas_call(functools.partial(attend_kernel, dims, tuple(((b, len(ref)...  5.86 us
    pallas_call x2, Pallas kernels, pack(): pl.pallas_call(functools.partial(pack_kernel, head, apart), out_shape=[pl...  2.21 us
    pallas_call x2, Pallas kernels, merge(): pl.pallas_call(functools.partial(merge_kernel, dims, columns), out_shape=...  1.59 us
  transfers between devices with their start and end apart: 7, of which 4 were waited for; matrix products, arithmetic and copies ran while one was open for 0% of the time, Pallas kernels for 24%

profile of v7, /device:TPU:0, one launch (start us, length us, event | category | flops | bytes accessed | tf_op | source)
XLA Modules:
  0.0 32.3 jit_solution(3557843223077790739)
XLA Ops:
  0.0 1.1 %pack.2 = (bf16[1152,128]{1,0:T(8,128)(2,1)S(1)}, bf16[64,1024]{1,0:T(8,128)(2,1)S(1)}) custom-call(bf16[64,2048]{1,0:T(8,128)(2,1)} %q_ref.3, bf16[512,256]{1,0:T(8,128)(2,1)} %ck_ref.3, bf16[512,256]{1,0:T(8,128)(2,1)} %cv_ref.3, bf16[64,256]{1,0:T(8,128)(2,1)} %nk_ref.3, bf16[64,256]{1,0:T(8,128)(2,1)} %nv_ref.3), custom_call_target="tpu_custom_call" | custom-call | tf_op jit(solution)/shard_map/pack/pallas_call | solution.py:207
  1.1 4.1 %collective-permute-start.1 = (bf16[64,1024]{1,0:T(8,128)(2,1)S(1)}, bf16[64,1024]{1,0:T(8,128)(2,1)S(1)}, u32[]{:S(2)}, u32[]{:S(2)}) collective-permute-start(bf16[64,1024]{1,0:T(8,128)(2,1)S(1)} %get-tuple-element.18.q_ref), channel_id=1, source_target_pairs={{0,16},{8,24},{16,0},{24,8},{1,17},{9,25},{17,1},{25,9},{2,18},{10... | collective-permute-start | bytes 393224 | tf_op jit(solution)/shard_map/ppermute | solution.py:188
  5.2 1.6 %collective-permute-start.3 = (bf16[1152,128]{1,0:T(8,128)(2,1)S(1)}, bf16[1152,128]{1,0:T(8,128)(2,1)S(1)}, u32[]{:S(2)}, u32[]{:S(2)}) collective-permute-start(bf16[1152,128]{1,0:T(8,128)(2,1)S(1)} %get-tuple-element.14.refs_0_), channel_id=1, source_target_pairs={{0,8},{8,0},{16,24},{24,16},{1,9},{9,1},{17,25},{25,17},{2,10},{10... | collective-permute-start | bytes 884744 | tf_op jit(solution)/shard_map/ppermute | solution.py:188
  6.8 1.1 %pack.3 = (bf16[1024,128]{1,0:T(8,128)(2,1)S(1)}, bf16[128,128]{1,0:T(8,128)(2,1)S(1)}, bf16[64,1024]{1,0:T(8,128)(2,1)S(1)}) custom-call(bf16[64,2048]{1,0:T(8,128)(2,1)} %q_ref.3, bf16[512,256]{1,0:T(8,128)(2,1)} %ck_ref.3, bf16[512,256]{1,0:T(8,128)(2,1)} %cv_ref.3, bf16[64,256]{1,0:T(8,128)(2,1)} %nk_ref.3, bf16[64,256]{1,0:T(8,128)(2,1)} %nv_ref.3, ...), custom_call_target="tpu_custom_call" | custom-call | tf_op jit(solution)/shard_map/pack/pallas_call | solution.py:207
  7.9 0.4 %collective-permute-start = (bf16[1024,128]{1,0:T(8,128)(2,1)S(1)}, bf16[1024,128]{1,0:T(8,128)(2,1)S(1)}, u32[]{:S(2)}, u32[]{:S(2)}) collective-permute-start(bf16[1024,128]{1,0:T(8,128)(2,1)S(1)} %get-tuple-element.16.refs_1_.refs_0_), channel_id=1, source_target_pairs={{0,16},{8,24},{16,0},{24,8},{1,17},{9,25},{17,1},{25,9},{2,18},{10... | collective-permute-start | bytes 786440 | tf_op jit(solution)/shard_map/ppermute | solution.py:188
  9.0 0.7 %work.7.refs_2_.refs_1_ = f32[136,512]{1,0:T(8,128)S(1)} custom-call(s32[1]{0:T(128)S(6)} %copy.9.len_ref, bf16[64,1024]{1,0:T(8,128)(2,1)S(1)} %get-tuple-element.18.q_ref, bf16[1152,128]{1,0:T(8,128)(2,1)S(1)} %get-tuple-element.14.refs_0_, bf16[1024,128]{1,0:T(8,128)(2,1)S(1)} %get-tuple-element.16.refs_1_.refs_0_), custom_call_target="tpu_custom_call" | custom-call | flops 6039797760 | bytes 1048576 | tf_op jit(solution)/shard_map/work/pallas_call | solution.py:227
  9.7 0.8 %work.8.refs_1_.refs_2_ = f32[136,512]{1,0:T(8,128)S(1)} custom-call(s32[1]{0:T(128)S(6)} %copy.9.len_ref, bf16[64,1024]{1,0:T(8,128)(2,1)S(1)} %get-tuple-element.21.q_ref, bf16[1024,128]{1,0:T(8,128)(2,1)S(1)} %get-tuple-element.16.refs_1_.refs_0_, bf16[128,128]{1,0:T(8,128)(2,1)S(1)} %get-tuple-element.20.refs_1_, f32[136,512]{1,0:T(8,128)S(1)} %work.7.refs_2_.refs_1_), custom_call_target="tpu_custom_call" | custom-call | flops 6039797760 | bytes 1048576 | tf_op jit(solution)/shard_map/work/pallas_call | solution.py:227
  10.5 0.3 collective-permute-start.4
  10.7 1.5 %collective-permute-done.1.q_ref = bf16[64,1024]{1,0:T(8,128)(2,1)S(1)} collective-permute-done((bf16[64,1024]{1,0:T(8,128)(2,1)S(1)}, bf16[64,1024]{1,0:T(8,128)(2,1)S(1)}, u32[]{:S(2)}, u32[]{:S(2)}) %collective-permute-start.1) | collective-permute-done | bytes 131104 | tf_op jit(solution)/shard_map/ppermute | solution.py:188
  12.2 0.7 %work.9.refs_1_ = f32[136,512]{1,0:T(8,128)S(1)} custom-call(s32[1]{0:T(128)S(6)} %copy.9.len_ref, bf16[64,1024]{1,0:T(8,128)(2,1)S(1)} %collective-permute-done.1.q_ref, bf16[1152,128]{1,0:T(8,128)(2,1)S(1)} %get-tuple-element.14.refs_0_, f32[136,512]{1,0:T(8,128)S(1)} %work.8.refs_1_.refs_2_), custom_call_target="tpu_custom_call" | custom-call | flops 6039797760 | bytes 1048576 | tf_op jit(solution)/shard_map/work/pallas_call | solution.py:227
  13.0 3.2 %collective-permute-start.2 = (bf16[128,128]{1,0:T(8,128)(2,1)S(1)}, bf16[128,128]{1,0:T(8,128)(2,1)S(1)}, u32[]{:S(2)}, u32[]{:S(2)}) collective-permute-start(bf16[128,128]{1,0:T(8,128)(2,1)S(1)} %get-tuple-element.20.refs_1_), channel_id=1, source_target_pairs={{0,16},{8,24},{1,17},{9,25},{2,18},{10,26},{3,19},{11,27},{4,20},{... | collective-permute-start | bytes 98312 | tf_op jit(solution)/shard_map/ppermute | solution.py:188
  16.2 5.8 %collective-permute-done.3.refs_0_ = bf16[1152,128]{1,0:T(8,128)(2,1)S(1)} collective-permute-done((bf16[1152,128]{1,0:T(8,128)(2,1)S(1)}, bf16[1152,128]{1,0:T(8,128)(2,1)S(1)}, u32[]{:S(2)}, u32[]{:S(2)}) %collective-permute-start.3) | collective-permute-done | bytes 294944 | tf_op jit(solution)/shard_map/ppermute | solution.py:188
  22.0 0.8 %work.10.refs_4_ = bf16[528,128]{1,0:T(8,128)(2,1)S(1)} custom-call(s32[1]{0:T(128)S(6)} %copy.9.len_ref, bf16[64,1024]{1,0:T(8,128)(2,1)S(1)} %collective-permute-done.1.q_ref, bf16[1152,128]{1,0:T(8,128)(2,1)S(1)} %collective-permute-done.3.refs_0_, f32[136,512]{1,0:T(8,128)S(1)} %work.9.refs_1_, f32[136,512]{1,0:T(8,128)S(1)} %work.8.refs_1_.refs_2_), custom_call_target="tpu_custom_call" | custom-call | flops 6039797760 | bytes 1048576 | tf_op jit(solution)/shard_map/work/pallas_call | solution.py:227
  22.8 0.1 collective-permute-start.6
  22.9 2.2 %collective-permute-done.4.q_ref = bf16[64,1024]{1,0:T(8,128)(2,1)S(1)} collective-permute-done((bf16[64,1024]{1,0:T(8,128)(2,1)S(1)}, bf16[64,1024]{1,0:T(8,128)(2,1)S(1)}, u32[]{:S(2)}, u32[]{:S(2)}) %collective-permute-start.4) | collective-permute-done | bytes 131104 | tf_op jit(solution)/shard_map/ppermute | solution.py:188
  25.1 0.0 collective-permute-done.2.refs_3_.refs_1_
  25.1 0.0 collective-permute-done.refs_2_.refs_0_
  25.1 1.4 %work.11.refs_2_ = bf16[528,128]{1,0:T(8,128)(2,1)S(1)} custom-call(s32[1]{0:T(128)S(6)} %copy.9.len_ref, bf16[64,1024]{1,0:T(8,128)(2,1)S(1)} %collective-permute-done.4.q_ref, bf16[1024,128]{1,0:T(8,128)(2,1)S(1)} %get-tuple-element.16.refs_1_.refs_0_, bf16[128,128]{1,0:T(8,128)(2,1)S(1)} %get-tuple-element.20.refs_1_, ...), custom_call_target="tpu_custom_call" | custom-call | flops 12079595520 | bytes 1048576 | tf_op jit(solution)/shard_map/work/pallas_call | solution.py:227
  26.4 1.4 %collective-permute-start.5 = (bf16[528,128]{1,0:T(8,128)(2,1)S(1)}, bf16[528,128]{1,0:T(8,128)(2,1)S(1)}, u32[]{:S(2)}, u32[]{:S(2)}) collective-permute-start(bf16[528,128]{1,0:T(8,128)(2,1)S(1)} %work.11.refs_2_), channel_id=1, source_target_pairs={{0,8},{8,0},{16,24},{24,16},{1,9},{9,1},{17,25},{25,17},{2,10},{10... | collective-permute-start | bytes 405512 | tf_op jit(solution)/shard_map/ppermute | solution.py:188
  27.8 0.8 %work.12.refs_3_.own_ref = f32[136,512]{1,0:T(8,128)S(1)} custom-call(s32[1]{0:T(128)S(6)} %copy.9.len_ref, bf16[64,1024]{1,0:T(8,128)(2,1)S(1)} %get-tuple-element.18.q_ref, bf16[1152,128]{1,0:T(8,128)(2,1)S(1)} %collective-permute-done.3.refs_0_, f32[136,512]{1,0:T(8,128)S(1)} %work.7.refs_2_.refs_1_, bf16[528,128]{1,0:T(8,128)(2,1)S(1)} %work.11.refs_2_), custom_call_target="tpu_custom_call" | custom-call | flops 6039797760 | bytes 1048576 | tf_op jit(solution)/shard_map/work/pallas_call | solution.py:227
  28.6 0.8 %work.13.refs_0_.own_ref = f32[136,512]{1,0:T(8,128)S(1)} custom-call(s32[1]{0:T(128)S(6)} %copy.9.len_ref, bf16[64,1024]{1,0:T(8,128)(2,1)S(1)} %get-tuple-element.21.q_ref, bf16[1024,128]{1,0:T(8,128)(2,1)S(1)} %collective-permute-done.refs_2_.refs_0_, bf16[128,128]{1,0:T(8,128)(2,1)S(1)} %collective-permute-done.2.refs_3_.refs_1_, ...), custom_call_target="tpu_custom_call" | custom-call | flops 6039797760 | bytes 1048576 | tf_op jit(solution)/shard_map/work/pallas_call | solution.py:227
  29.4 0.0 collective-permute-done.6.got_ref
  29.4 0.8 %merge.2.refs_0_ = bf16[64,2048]{1,0:T(8,128)(2,1)} custom-call(f32[136,512]{1,0:T(8,128)S(1)} %work.12.refs_3_.own_ref, bf16[528,128]{1,0:T(8,128)(2,1)S(1)} %collective-permute-done.6.got_ref, f32[136,512]{1,0:T(8,128)S(1)} %work.13.refs_0_.own_ref), custom_call_target="tpu_custom_call" | custom-call | tf_op jit(solution)/shard_map/merge/pallas_call | solution.py:243
  30.2 1.4 %collective-permute-done.5.got_ref = bf16[528,128]{1,0:T(8,128)(2,1)S(1)} collective-permute-done((bf16[528,128]{1,0:T(8,128)(2,1)S(1)}, bf16[528,128]{1,0:T(8,128)(2,1)S(1)}, u32[]{:S(2)}, u32[]{:S(2)}) %collective-permute-start.5) | collective-permute-done | bytes 135200 | tf_op jit(solution)/shard_map/ppermute | solution.py:188
  31.5 0.8 %merge.3 = bf16[64,2048]{1,0:T(8,128)(2,1)} custom-call(f32[136,512]{1,0:T(8,128)S(1)} %work.13.refs_0_.own_ref, bf16[528,128]{1,0:T(8,128)(2,1)S(1)} %collective-permute-done.5.got_ref, bf16[64,2048]{1,0:T(8,128)(2,1)} %merge.2.refs_0_), custom_call_target="tpu_custom_call", output_to_operand_aliasing={{}: (2, {})} | custom-call | tf_op jit(solution)/shard_map/merge/pallas_call | solution.py:243
Async XLA Ops:
  1.1 11.1 %collective-permute-start.1 = (bf16[64,1024]{1,0:T(8,128)(2,1)S(1)}, bf16[64,1024]{1,0:T(8,128)(2,1)S(1)}, u32[]{:S(2)}, u32[]{:S(2)}) collective-permute-start(bf16[64,1024]{1,0:T(8,128)(2,1)S(1)} %get-tuple-element.18.q_ref), channel_id=1, source_target_pairs={{0,16},{8,24},{16,0},{24,8},{1,17},{9,25},{17,1},{25,9},{2,18},{10... | collective-permute-start | bytes 393224 | tf_op jit(solution)/shard_map/ppermute | solution.py:188
  5.2 16.8 %collective-permute-start.3 = (bf16[1152,128]{1,0:T(8,128)(2,1)S(1)}, bf16[1152,128]{1,0:T(8,128)(2,1)S(1)}, u32[]{:S(2)}, u32[]{:S(2)}) collective-permute-start(bf16[1152,128]{1,0:T(8,128)(2,1)S(1)} %get-tuple-element.14.refs_0_), channel_id=1, source_target_pairs={{0,8},{8,0},{16,24},{24,16},{1,9},{9,1},{17,25},{25,17},{2,10},{10... | collective-permute-start | bytes 884744 | tf_op jit(solution)/shard_map/ppermute | solution.py:188
  7.9 17.2 %collective-permute-start = (bf16[1024,128]{1,0:T(8,128)(2,1)S(1)}, bf16[1024,128]{1,0:T(8,128)(2,1)S(1)}, u32[]{:S(2)}, u32[]{:S(2)}) collective-permute-start(bf16[1024,128]{1,0:T(8,128)(2,1)S(1)} %get-tuple-element.16.refs_1_.refs_0_), channel_id=1, source_target_pairs={{0,16},{8,24},{16,0},{24,8},{1,17},{9,25},{17,1},{25,9},{2,18},{10... | collective-permute-start | bytes 786440 | tf_op jit(solution)/shard_map/ppermute | solution.py:188
  10.5 14.6 %collective-permute-start.4 = (bf16[64,1024]{1,0:T(8,128)(2,1)S(1)}, bf16[64,1024]{1,0:T(8,128)(2,1)S(1)}, u32[]{:S(2)}, u32[]{:S(2)}) collective-permute-start(bf16[64,1024]{1,0:T(8,128)(2,1)S(1)} %get-tuple-element.21.q_ref), channel_id=1, source_target_pairs={{0,8},{8,0},{16,24},{24,16},{1,9},{9,1},{17,25},{25,17},{2,10},{10... | collective-permute-start | bytes 393224 | tf_op jit(solution)/shard_map/ppermute | solution.py:188
  13.0 12.1 %collective-permute-start.2 = (bf16[128,128]{1,0:T(8,128)(2,1)S(1)}, bf16[128,128]{1,0:T(8,128)(2,1)S(1)}, u32[]{:S(2)}, u32[]{:S(2)}) collective-permute-start(bf16[128,128]{1,0:T(8,128)(2,1)S(1)} %get-tuple-element.20.refs_1_), channel_id=1, source_target_pairs={{0,16},{8,24},{1,17},{9,25},{2,18},{10,26},{3,19},{11,27},{4,20},{... | collective-permute-start | bytes 98312 | tf_op jit(solution)/shard_map/ppermute | solution.py:188
  22.8 6.6 %collective-permute-start.6 = (bf16[528,128]{1,0:T(8,128)(2,1)S(1)}, bf16[528,128]{1,0:T(8,128)(2,1)S(1)}, u32[]{:S(2)}, u32[]{:S(2)}) collective-permute-start(bf16[528,128]{1,0:T(8,128)(2,1)S(1)} %work.10.refs_4_), channel_id=1, source_target_pairs={{0,16},{8,24},{16,0},{24,8},{1,17},{9,25},{17,1},{25,9},{2,18},{10... | collective-permute-start | bytes 405512 | tf_op jit(solution)/shard_map/ppermute | solution.py:188
  26.4 5.1 %collective-permute-start.5 = (bf16[528,128]{1,0:T(8,128)(2,1)S(1)}, bf16[528,128]{1,0:T(8,128)(2,1)S(1)}, u32[]{:S(2)}, u32[]{:S(2)}) collective-permute-start(bf16[528,128]{1,0:T(8,128)(2,1)S(1)} %work.11.refs_2_), channel_id=1, source_target_pairs={{0,8},{8,0},{16,24},{24,16},{1,9},{9,1},{17,25},{25,17},{2,10},{10... | collective-permute-start | bytes 405512 | tf_op jit(solution)/shard_map/ppermute | solution.py:188

commit v8 on v7

--- a/solution.py
+++ b/solution.py
@@ -267,10 +267,10 @@
     far_new1 = traded(sent_new1, 2, True)
     sent0 = work(far_q0, [(1, (far_kv0,))], 2, "sent", state=theirs0, after=(mine1,))
     got0 = traded(sent0, 2)
-    sent1 = work(far_q1, [(0, (old1, new1)), (2, (far_old1, far_new1))], 1, "sent", after=(sent0,))
+    own0 = work(q0, [(1, (far_kv0,))], 0, "own", state=mine0, after=(sent0,))
+    sent1 = work(far_q1, [(0, (old1, new1)), (2, (far_old1, far_new1))], 1, "sent", after=(own0,))
     got1 = traded(sent1, 1)
-    own0 = work(q0, [(1, (far_kv0,))], 0, "own", state=mine0, after=(sent1,))
-    own1 = work(q1, [(2, (far_old1, far_new1))], 0, "own", state=mine1, after=(own0,))
+    own1 = work(q1, [(2, (far_old1, far_new1))], 0, "own", state=mine1, after=(sent1,))
     out = merge(own0, got0, (0, 0, groups), after=(own1,))
     return merge(own1, got1, (groups, 0, groups), out)
 

time: 32.5 us -> 32.5 us (level)
  transfers between devices with their start and end apart: 7 -> 7, of which waited for: 4 -> 5; matrix products, arithmetic and copies ran while one was open for 0% -> 0% of each run, Pallas kernels for 24% -> 24%
where the time goes in v8:
time: 32.5 us; the launch traced here: 32.3 us
  starting transfers between devices  11.1 us (34%)
  waiting for transfers between devices  10.8 us (33%)
  Pallas kernels  9.66 us (30%)
  between operations  0.75 us (2%)
    ppermute x7, starting transfers between devices, traded(): lax.ppermute(value, 'ctx', [(a, b) for a, b in pairs if a < b or not onwa...  11.1 us
    ppermute x7, waiting for transfers between devices, traded(): lax.ppermute(value, 'ctx', [(a, b) for a, b in pairs if a < b or not onwa...  10.8 us
    pallas_call x7, Pallas kernels, work(): pl.pallas_call(functools.partial(attend_kernel, dims, tuple(((b, len(ref)...  5.86 us
    pallas_call x2, Pallas kernels, pack(): pl.pallas_call(functools.partial(pack_kernel, head, apart), out_shape=[pl...  2.21 us
    pallas_call x2, Pallas kernels, merge(): pl.pallas_call(functools.partial(merge_kernel, dims, columns), out_shape=...  1.59 us
  transfers between devices with their start and end apart: 7, of which 5 were waited for; matrix products, arithmetic and copies ran while one was open for 0% of the time, Pallas kernels for 24%

profile of v8, /device:TPU:0, one launch (start us, length us, event | category | flops | bytes accessed | tf_op | source)
XLA Modules:
  0.0 32.3 jit_solution(62714295206867187)
XLA Ops:
  0.0 1.1 %pack.2 = (bf16[1152,128]{1,0:T(8,128)(2,1)S(1)}, bf16[64,1024]{1,0:T(8,128)(2,1)S(1)}) custom-call(bf16[64,2048]{1,0:T(8,128)(2,1)} %q_ref.3, bf16[512,256]{1,0:T(8,128)(2,1)} %ck_ref.3, bf16[512,256]{1,0:T(8,128)(2,1)} %cv_ref.3, bf16[64,256]{1,0:T(8,128)(2,1)} %nk_ref.3, bf16[64,256]{1,0:T(8,128)(2,1)} %nv_ref.3), custom_call_target="tpu_custom_call" | custom-call | tf_op jit(solution)/shard_map/pack/pallas_call | solution.py:207
  1.1 4.1 %collective-permute-start.1 = (bf16[64,1024]{1,0:T(8,128)(2,1)S(1)}, bf16[64,1024]{1,0:T(8,128)(2,1)S(1)}, u32[]{:S(2)}, u32[]{:S(2)}) collective-permute-start(bf16[64,1024]{1,0:T(8,128)(2,1)S(1)} %get-tuple-element.18.q_ref), channel_id=1, source_target_pairs={{0,16},{8,24},{16,0},{24,8},{1,17},{9,25},{17,1},{25,9},{2,18},{10... | collective-permute-start | bytes 393224 | tf_op jit(solution)/shard_map/ppermute | solution.py:188
  5.2 1.6 %collective-permute-start.4 = (bf16[1152,128]{1,0:T(8,128)(2,1)S(1)}, bf16[1152,128]{1,0:T(8,128)(2,1)S(1)}, u32[]{:S(2)}, u32[]{:S(2)}) collective-permute-start(bf16[1152,128]{1,0:T(8,128)(2,1)S(1)} %get-tuple-element.14.refs_0_), channel_id=1, source_target_pairs={{0,8},{8,0},{16,24},{24,16},{1,9},{9,1},{17,25},{25,17},{2,10},{10... | collective-permute-start | bytes 884744 | tf_op jit(solution)/shard_map/ppermute | solution.py:188
  6.8 1.1 %pack.3 = (bf16[1024,128]{1,0:T(8,128)(2,1)S(1)}, bf16[128,128]{1,0:T(8,128)(2,1)S(1)}, bf16[64,1024]{1,0:T(8,128)(2,1)S(1)}) custom-call(bf16[64,2048]{1,0:T(8,128)(2,1)} %q_ref.3, bf16[512,256]{1,0:T(8,128)(2,1)} %ck_ref.3, bf16[512,256]{1,0:T(8,128)(2,1)} %cv_ref.3, bf16[64,256]{1,0:T(8,128)(2,1)} %nk_ref.3, bf16[64,256]{1,0:T(8,128)(2,1)} %nv_ref.3, ...), custom_call_target="tpu_custom_call" | custom-call | tf_op jit(solution)/shard_map/pack/pallas_call | solution.py:207
  7.9 0.4 %collective-permute-start = (bf16[1024,128]{1,0:T(8,128)(2,1)S(1)}, bf16[1024,128]{1,0:T(8,128)(2,1)S(1)}, u32[]{:S(2)}, u32[]{:S(2)}) collective-permute-start(bf16[1024,128]{1,0:T(8,128)(2,1)S(1)} %get-tuple-element.16.refs_1_.refs_0_), channel_id=1, source_target_pairs={{0,16},{8,24},{16,0},{24,8},{1,17},{9,25},{17,1},{25,9},{2,18},{10... | collective-permute-start | bytes 786440 | tf_op jit(solution)/shard_map/ppermute | solution.py:188
  9.0 0.7 %work.7.refs_2_.refs_1_ = f32[136,512]{1,0:T(8,128)S(1)} custom-call(s32[1]{0:T(128)S(6)} %copy.9.len_ref, bf16[64,1024]{1,0:T(8,128)(2,1)S(1)} %get-tuple-element.18.q_ref, bf16[1152,128]{1,0:T(8,128)(2,1)S(1)} %get-tuple-element.14.refs_0_, bf16[1024,128]{1,0:T(8,128)(2,1)S(1)} %get-tuple-element.16.refs_1_.refs_0_), custom_call_target="tpu_custom_call" | custom-call | flops 6039797760 | bytes 1048576 | tf_op jit(solution)/shard_map/work/pallas_call | solution.py:227
  9.7 0.8 %work.8.refs_1_.refs_2_ = f32[136,512]{1,0:T(8,128)S(1)} custom-call(s32[1]{0:T(128)S(6)} %copy.9.len_ref, bf16[64,1024]{1,0:T(8,128)(2,1)S(1)} %get-tuple-element.21.q_ref, bf16[1024,128]{1,0:T(8,128)(2,1)S(1)} %get-tuple-element.16.refs_1_.refs_0_, bf16[128,128]{1,0:T(8,128)(2,1)S(1)} %get-tuple-element.20.refs_1_, f32[136,512]{1,0:T(8,128)S(1)} %work.7.refs_2_.refs_1_), custom_call_target="tpu_custom_call" | custom-call | flops 6039797760 | bytes 1048576 | tf_op jit(solution)/shard_map/work/pallas_call | solution.py:227
  10.5 0.3 collective-permute-start.3
  10.7 1.5 %collective-permute-done.1.q_ref = bf16[64,1024]{1,0:T(8,128)(2,1)S(1)} collective-permute-done((bf16[64,1024]{1,0:T(8,128)(2,1)S(1)}, bf16[64,1024]{1,0:T(8,128)(2,1)S(1)}, u32[]{:S(2)}, u32[]{:S(2)}) %collective-permute-start.1) | collective-permute-done | bytes 131104 | tf_op jit(solution)/shard_map/ppermute | solution.py:188
  12.2 0.7 %work.9.refs_1_ = f32[136,512]{1,0:T(8,128)S(1)} custom-call(s32[1]{0:T(128)S(6)} %copy.9.len_ref, bf16[64,1024]{1,0:T(8,128)(2,1)S(1)} %collective-permute-done.1.q_ref, bf16[1152,128]{1,0:T(8,128)(2,1)S(1)} %get-tuple-element.14.refs_0_, f32[136,512]{1,0:T(8,128)S(1)} %work.8.refs_1_.refs_2_), custom_call_target="tpu_custom_call" | custom-call | flops 6039797760 | bytes 1048576 | tf_op jit(solution)/shard_map/work/pallas_call | solution.py:227
  13.0 3.2 %collective-permute-start.2 = (bf16[128,128]{1,0:T(8,128)(2,1)S(1)}, bf16[128,128]{1,0:T(8,128)(2,1)S(1)}, u32[]{:S(2)}, u32[]{:S(2)}) collective-permute-start(bf16[128,128]{1,0:T(8,128)(2,1)S(1)} %get-tuple-element.20.refs_1_), channel_id=1, source_target_pairs={{0,16},{8,24},{1,17},{9,25},{2,18},{10,26},{3,19},{11,27},{4,20},{... | collective-permute-start | bytes 98312 | tf_op jit(solution)/shard_map/ppermute | solution.py:188
  16.2 5.8 %collective-permute-done.4.refs_0_ = bf16[1152,128]{1,0:T(8,128)(2,1)S(1)} collective-permute-done((bf16[1152,128]{1,0:T(8,128)(2,1)S(1)}, bf16[1152,128]{1,0:T(8,128)(2,1)S(1)}, u32[]{:S(2)}, u32[]{:S(2)}) %collective-permute-start.4) | collective-permute-done | bytes 294944 | tf_op jit(solution)/shard_map/ppermute | solution.py:188
  22.0 0.8 %work.10.refs_2_ = bf16[528,128]{1,0:T(8,128)(2,1)S(1)} custom-call(s32[1]{0:T(128)S(6)} %copy.9.len_ref, bf16[64,1024]{1,0:T(8,128)(2,1)S(1)} %collective-permute-done.1.q_ref, bf16[1152,128]{1,0:T(8,128)(2,1)S(1)} %collective-permute-done.4.refs_0_, f32[136,512]{1,0:T(8,128)S(1)} %work.9.refs_1_, f32[136,512]{1,0:T(8,128)S(1)} %work.8.refs_1_.refs_2_), custom_call_target="tpu_custom_call" | custom-call | flops 6039797760 | bytes 1048576 | tf_op jit(solution)/shard_map/work/pallas_call | solution.py:227
  22.8 0.1 collective-permute-start.6
  22.8 0.8 %work.11.refs_4_.own_ref = f32[136,512]{1,0:T(8,128)S(1)} custom-call(s32[1]{0:T(128)S(6)} %copy.9.len_ref, bf16[64,1024]{1,0:T(8,128)(2,1)S(1)} %get-tuple-element.18.q_ref, bf16[1152,128]{1,0:T(8,128)(2,1)S(1)} %collective-permute-done.4.refs_0_, f32[136,512]{1,0:T(8,128)S(1)} %work.7.refs_2_.refs_1_, bf16[528,128]{1,0:T(8,128)(2,1)S(1)} %work.10.refs_2_), custom_call_target="tpu_custom_call" | custom-call | flops 6039797760 | bytes 1048576 | tf_op jit(solution)/shard_map/work/pallas_call | solution.py:227
  23.6 1.4 %collective-permute-done.3.q_ref = bf16[64,1024]{1,0:T(8,128)(2,1)S(1)} collective-permute-done((bf16[64,1024]{1,0:T(8,128)(2,1)S(1)}, bf16[64,1024]{1,0:T(8,128)(2,1)S(1)}, u32[]{:S(2)}, u32[]{:S(2)}) %collective-permute-start.3) | collective-permute-done | bytes 131104 | tf_op jit(solution)/shard_map/ppermute | solution.py:188
  25.1 0.0 collective-permute-done.2.refs_3_.refs_1_
  25.1 0.0 collective-permute-done.refs_2_.refs_0_
  25.1 1.4 %work.12.refs_3_ = bf16[528,128]{1,0:T(8,128)(2,1)S(1)} custom-call(s32[1]{0:T(128)S(6)} %copy.9.len_ref, bf16[64,1024]{1,0:T(8,128)(2,1)S(1)} %collective-permute-done.3.q_ref, bf16[1024,128]{1,0:T(8,128)(2,1)S(1)} %get-tuple-element.16.refs_1_.refs_0_, bf16[128,128]{1,0:T(8,128)(2,1)S(1)} %get-tuple-element.20.refs_1_, ...), custom_call_target="tpu_custom_call" | custom-call | flops 12079595520 | bytes 1048576 | tf_op jit(solution)/shard_map/work/pallas_call | solution.py:227
  26.4 1.4 %collective-permute-start.5 = (bf16[528,128]{1,0:T(8,128)(2,1)S(1)}, bf16[528,128]{1,0:T(8,128)(2,1)S(1)}, u32[]{:S(2)}, u32[]{:S(2)}) collective-permute-start(bf16[528,128]{1,0:T(8,128)(2,1)S(1)} %work.12.refs_3_), channel_id=1, source_target_pairs={{0,8},{8,0},{16,24},{24,16},{1,9},{9,1},{17,25},{25,17},{2,10},{10... | collective-permute-start | bytes 405512 | tf_op jit(solution)/shard_map/ppermute | solution.py:188
  27.8 0.8 %work.13.refs_0_.own_ref = f32[136,512]{1,0:T(8,128)S(1)} custom-call(s32[1]{0:T(128)S(6)} %copy.9.len_ref, bf16[64,1024]{1,0:T(8,128)(2,1)S(1)} %get-tuple-element.21.q_ref, bf16[1024,128]{1,0:T(8,128)(2,1)S(1)} %collective-permute-done.refs_2_.refs_0_, bf16[128,128]{1,0:T(8,128)(2,1)S(1)} %collective-permute-done.2.refs_3_.refs_1_, ...), custom_call_target="tpu_custom_call" | custom-call | flops 6039797760 | bytes 1048576 | tf_op jit(solution)/shard_map/work/pallas_call | solution.py:227
  28.6 0.5 %collective-permute-done.6.got_ref = bf16[528,128]{1,0:T(8,128)(2,1)S(1)} collective-permute-done((bf16[528,128]{1,0:T(8,128)(2,1)S(1)}, bf16[528,128]{1,0:T(8,128)(2,1)S(1)}, u32[]{:S(2)}, u32[]{:S(2)}) %collective-permute-start.6) | collective-permute-done | bytes 135200 | tf_op jit(solution)/shard_map/ppermute | solution.py:188
  29.1 0.8 %merge.2.refs_0_ = bf16[64,2048]{1,0:T(8,128)(2,1)} custom-call(f32[136,512]{1,0:T(8,128)S(1)} %work.11.refs_4_.own_ref, bf16[528,128]{1,0:T(8,128)(2,1)S(1)} %collective-permute-done.6.got_ref, f32[136,512]{1,0:T(8,128)S(1)} %work.13.refs_0_.own_ref), custom_call_target="tpu_custom_call" | custom-call | tf_op jit(solution)/shard_map/merge/pallas_call | solution.py:243
  29.9 1.6 %collective-permute-done.5.got_ref = bf16[528,128]{1,0:T(8,128)(2,1)S(1)} collective-permute-done((bf16[528,128]{1,0:T(8,128)(2,1)S(1)}, bf16[528,128]{1,0:T(8,128)(2,1)S(1)}, u32[]{:S(2)}, u32[]{:S(2)}) %collective-permute-start.5) | collective-permute-done | bytes 135200 | tf_op jit(solution)/shard_map/ppermute | solution.py:188
  31.5 0.8 %merge.3 = bf16[64,2048]{1,0:T(8,128)(2,1)} custom-call(f32[136,512]{1,0:T(8,128)S(1)} %work.13.refs_0_.own_ref, bf16[528,128]{1,0:T(8,128)(2,1)S(1)} %collective-permute-done.5.got_ref, bf16[64,2048]{1,0:T(8,128)(2,1)} %merge.2.refs_0_), custom_call_target="tpu_custom_call", output_to_operand_aliasing={{}: (2, {})} | custom-call | tf_op jit(solution)/shard_map/merge/pallas_call | solution.py:243
Async XLA Ops:
  1.1 11.1 %collective-permute-start.1 = (bf16[64,1024]{1,0:T(8,128)(2,1)S(1)}, bf16[64,1024]{1,0:T(8,128)(2,1)S(1)}, u32[]{:S(2)}, u32[]{:S(2)}) collective-permute-start(bf16[64,1024]{1,0:T(8,128)(2,1)S(1)} %get-tuple-element.18.q_ref), channel_id=1, source_target_pairs={{0,16},{8,24},{16,0},{24,8},{1,17},{9,25},{17,1},{25,9},{2,18},{10... | collective-permute-start | bytes 393224 | tf_op jit(solution)/shard_map/ppermute | solution.py:188
  5.2 16.8 %collective-permute-start.4 = (bf16[1152,128]{1,0:T(8,128)(2,1)S(1)}, bf16[1152,128]{1,0:T(8,128)(2,1)S(1)}, u32[]{:S(2)}, u32[]{:S(2)}) collective-permute-start(bf16[1152,128]{1,0:T(8,128)(2,1)S(1)} %get-tuple-element.14.refs_0_), channel_id=1, source_target_pairs={{0,8},{8,0},{16,24},{24,16},{1,9},{9,1},{17,25},{25,17},{2,10},{10... | collective-permute-start | bytes 884744 | tf_op jit(solution)/shard_map/ppermute | solution.py:188
  7.9 17.2 %collective-permute-start = (bf16[1024,128]{1,0:T(8,128)(2,1)S(1)}, bf16[1024,128]{1,0:T(8,128)(2,1)S(1)}, u32[]{:S(2)}, u32[]{:S(2)}) collective-permute-start(bf16[1024,128]{1,0:T(8,128)(2,1)S(1)} %get-tuple-element.16.refs_1_.refs_0_), channel_id=1, source_target_pairs={{0,16},{8,24},{16,0},{24,8},{1,17},{9,25},{17,1},{25,9},{2,18},{10... | collective-permute-start | bytes 786440 | tf_op jit(solution)/shard_map/ppermute | solution.py:188
  10.5 14.6 %collective-permute-start.3 = (bf16[64,1024]{1,0:T(8,128)(2,1)S(1)}, bf16[64,1024]{1,0:T(8,128)(2,1)S(1)}, u32[]{:S(2)}, u32[]{:S(2)}) collective-permute-start(bf16[64,1024]{1,0:T(8,128)(2,1)S(1)} %get-tuple-element.21.q_ref), channel_id=1, source_target_pairs={{0,8},{8,0},{16,24},{24,16},{1,9},{9,1},{17,25},{25,17},{2,10},{10... | collective-permute-start | bytes 393224 | tf_op jit(solution)/shard_map/ppermute | solution.py:188
  13.0 12.1 %collective-permute-start.2 = (bf16[128,128]{1,0:T(8,128)(2,1)S(1)}, bf16[128,128]{1,0:T(8,128)(2,1)S(1)}, u32[]{:S(2)}, u32[]{:S(2)}) collective-permute-start(bf16[128,128]{1,0:T(8,128)(2,1)S(1)} %get-tuple-element.20.refs_1_), channel_id=1, source_target_pairs={{0,16},{8,24},{1,17},{9,25},{2,18},{10,26},{3,19},{11,27},{4,20},{... | collective-permute-start | bytes 98312 | tf_op jit(solution)/shard_map/ppermute | solution.py:188
  22.8 6.3 %collective-permute-start.6 = (bf16[528,128]{1,0:T(8,128)(2,1)S(1)}, bf16[528,128]{1,0:T(8,128)(2,1)S(1)}, u32[]{:S(2)}, u32[]{:S(2)}) collective-permute-start(bf16[528,128]{1,0:T(8,128)(2,1)S(1)} %work.10.refs_2_), channel_id=1, source_target_pairs={{0,16},{8,24},{16,0},{24,8},{1,17},{9,25},{17,1},{25,9},{2,18},{10... | collective-permute-start | bytes 405512 | tf_op jit(solution)/shard_map/ppermute | solution.py:188
  26.4 5.1 %collective-permute-start.5 = (bf16[528,128]{1,0:T(8,128)(2,1)S(1)}, bf16[528,128]{1,0:T(8,128)(2,1)S(1)}, u32[]{:S(2)}, u32[]{:S(2)}) collective-permute-start(bf16[528,128]{1,0:T(8,128)(2,1)S(1)} %work.12.refs_3_), channel_id=1, source_target_pairs={{0,8},{8,0},{16,24},{24,16},{1,9},{9,1},{17,25},{25,17},{2,10},{10... | collective-permute-start | bytes 405512 | tf_op jit(solution)/shard_map/ppermute | solution.py:188

commit v9 on v7

--- a/solution.py
+++ b/solution.py
@@ -257,14 +257,13 @@
     kv0, q0 = pack(0, 0, ())
     far_kv0, far_q0 = traded(kv0, 1), traded(q0, 2)
     old1, new1, q1 = pack(1, 1, (kv0,))
+    far_new1 = traded(new1, 2, True)
     far_old1 = traded(old1, 2)
     mine0 = work(q0, [(0, (kv0,))], 0, "state", after=(old1,))
     mine1 = work(q1, [(0, (old1, new1))], 0, "state", after=(mine0,))
     sent_q1, mine1 = lax.optimization_barrier((q1, mine1))
     far_q1 = traded(sent_q1, 1)
     theirs0 = work(far_q0, [(0, (kv0,))], 2, "state", after=(mine1,))
-    sent_new1, theirs0 = lax.optimization_barrier((new1, theirs0))
-    far_new1 = traded(sent_new1, 2, True)
     sent0 = work(far_q0, [(1, (far_kv0,))], 2, "sent", state=theirs0, after=(mine1,))
     got0 = traded(sent0, 2)
     sent1 = work(far_q1, [(0, (old1, new1)), (2, (far_old1, far_new1))], 1, "sent", after=(sent0,))

time: 32.5 us -> 32.8 us (level)
  starting transfers between devices: 11 us -> 13.2 us
  waiting for transfers between devices: 10.9 us -> 9 us
    ppermute x7, starting transfers between devices: 11 us -> 13.2 us  [traded(): lax.ppermute(value, 'ctx', [(a, b) for a, b in pairs if a < b or not onwa...]
    ppermute x7, waiting for transfers between devices: 10.9 us -> 9 us  [traded(): lax.ppermute(value, 'ctx', [(a, b) for a, b in pairs if a < b or not onwa...]
  transfers between devices with their start and end apart: 7 -> 7, of which waited for: 4 -> 3; matrix products, arithmetic and copies ran while one was open for 0% -> 0% of each run, Pallas kernels for 24% -> 24%
where the time goes in v9:
time: 32.8 us; the launch traced here: 32.6 us
  starting transfers between devices  13.2 us (40%)
  Pallas kernels  9.66 us (29%)
  waiting for transfers between devices  9 us (27%)
  between operations  0.76 us (2%)
    ppermute x7, starting transfers between devices, traded(): lax.ppermute(value, 'ctx', [(a, b) for a, b in pairs if a < b or not onwa...  13.2 us
    ppermute x7, waiting for transfers between devices, traded(): lax.ppermute(value, 'ctx', [(a, b) for a, b in pairs if a < b or not onwa...  9 us
    pallas_call x7, Pallas kernels, work(): pl.pallas_call(functools.partial(attend_kernel, dims, tuple(((b, len(ref)...  5.86 us
    pallas_call x2, Pallas kernels, pack(): pl.pallas_call(functools.partial(pack_kernel, head, apart), out_shape=[pl...  2.21 us
    pallas_call x2, Pallas kernels, merge(): pl.pallas_call(functools.partial(merge_kernel, dims, columns), out_shape=...  1.59 us
  transfers between devices with their start and end apart: 7, of which 3 were waited for; matrix products, arithmetic and copies ran while one was open for 0% of the time, Pallas kernels for 24%

profile of v9, /device:TPU:0, one launch (start us, length us, event | category | flops | bytes accessed | tf_op | source)
XLA Modules:
  0.0 32.6 jit_solution(3994609075617808173)
XLA Ops:
  0.0 1.1 %pack.2 = (bf16[1152,128]{1,0:T(8,128)(2,1)S(1)}, bf16[64,1024]{1,0:T(8,128)(2,1)S(1)}) custom-call(bf16[64,2048]{1,0:T(8,128)(2,1)} %q_ref.3, bf16[512,256]{1,0:T(8,128)(2,1)} %ck_ref.3, bf16[512,256]{1,0:T(8,128)(2,1)} %cv_ref.3, bf16[64,256]{1,0:T(8,128)(2,1)} %nk_ref.3, bf16[64,256]{1,0:T(8,128)(2,1)} %nv_ref.3), custom_call_target="tpu_custom_call" | custom-call | tf_op jit(solution)/shard_map/pack/pallas_call | solution.py:207
  1.1 4.1 %collective-permute-start.4 = (bf16[64,1024]{1,0:T(8,128)(2,1)S(1)}, bf16[64,1024]{1,0:T(8,128)(2,1)S(1)}, u32[]{:S(2)}, u32[]{:S(2)}) collective-permute-start(bf16[64,1024]{1,0:T(8,128)(2,1)S(1)} %get-tuple-element.16.q_ref), channel_id=1, source_target_pairs={{0,16},{8,24},{16,0},{24,8},{1,17},{9,25},{17,1},{25,9},{2,18},{10... | collective-permute-start | bytes 393224 | tf_op jit(solution)/shard_map/ppermute | solution.py:188
  5.2 1.6 %collective-permute-start.2 = (bf16[1152,128]{1,0:T(8,128)(2,1)S(1)}, bf16[1152,128]{1,0:T(8,128)(2,1)S(1)}, u32[]{:S(2)}, u32[]{:S(2)}) collective-permute-start(bf16[1152,128]{1,0:T(8,128)(2,1)S(1)} %get-tuple-element.12.refs_0_), channel_id=1, source_target_pairs={{0,8},{8,0},{16,24},{24,16},{1,9},{9,1},{17,25},{25,17},{2,10},{10... | collective-permute-start | bytes 884744 | tf_op jit(solution)/shard_map/ppermute | solution.py:188
  6.8 1.1 %pack.3 = (bf16[1024,128]{1,0:T(8,128)(2,1)S(1)}, bf16[128,128]{1,0:T(8,128)(2,1)S(1)}, bf16[64,1024]{1,0:T(8,128)(2,1)S(1)}) custom-call(bf16[64,2048]{1,0:T(8,128)(2,1)} %q_ref.3, bf16[512,256]{1,0:T(8,128)(2,1)} %ck_ref.3, bf16[512,256]{1,0:T(8,128)(2,1)} %cv_ref.3, bf16[64,256]{1,0:T(8,128)(2,1)} %nk_ref.3, bf16[64,256]{1,0:T(8,128)(2,1)} %nv_ref.3, ...), custom_call_target="tpu_custom_call" | custom-call | tf_op jit(solution)/shard_map/pack/pallas_call | solution.py:207
  7.9 0.4 %collective-permute-start = (bf16[1024,128]{1,0:T(8,128)(2,1)S(1)}, bf16[1024,128]{1,0:T(8,128)(2,1)S(1)}, u32[]{:S(2)}, u32[]{:S(2)}) collective-permute-start(bf16[1024,128]{1,0:T(8,128)(2,1)S(1)} %get-tuple-element.14.refs_1_.refs_0_), channel_id=1, source_target_pairs={{0,16},{8,24},{16,0},{24,8},{1,17},{9,25},{17,1},{25,9},{2,18},{10... | collective-permute-start | bytes 786440 | tf_op jit(solution)/shard_map/ppermute | solution.py:188
  8.3 4.5 %collective-permute-start.1 = (bf16[128,128]{1,0:T(8,128)(2,1)S(1)}, bf16[128,128]{1,0:T(8,128)(2,1)S(1)}, u32[]{:S(2)}, u32[]{:S(2)}) collective-permute-start(bf16[128,128]{1,0:T(8,128)(2,1)S(1)} %get-tuple-element.15.refs_1_), channel_id=1, source_target_pairs={{0,16},{8,24},{1,17},{9,25},{2,18},{10,26},{3,19},{11,27},{4,20},{... | collective-permute-start | bytes 98312 | tf_op jit(solution)/shard_map/ppermute | solution.py:188
  13.4 0.7 %work.7.refs_2_.refs_1_ = f32[136,512]{1,0:T(8,128)S(1)} custom-call(s32[1]{0:T(128)S(6)} %copy.9.len_ref, bf16[64,1024]{1,0:T(8,128)(2,1)S(1)} %get-tuple-element.16.q_ref, bf16[1152,128]{1,0:T(8,128)(2,1)S(1)} %get-tuple-element.12.refs_0_, bf16[1024,128]{1,0:T(8,128)(2,1)S(1)} %get-tuple-element.14.refs_1_.refs_0_), custom_call_target="tpu_custom_call" | custom-call | flops 6039797760 | bytes 1048576 | tf_op jit(solution)/shard_map/work/pallas_call | solution.py:227
  14.2 0.8 %work.8.refs_1_.refs_2_ = f32[136,512]{1,0:T(8,128)S(1)} custom-call(s32[1]{0:T(128)S(6)} %copy.9.len_ref, bf16[64,1024]{1,0:T(8,128)(2,1)S(1)} %get-tuple-element.18.q_ref, bf16[1024,128]{1,0:T(8,128)(2,1)S(1)} %get-tuple-element.14.refs_1_.refs_0_, bf16[128,128]{1,0:T(8,128)(2,1)S(1)} %get-tuple-element.15.refs_1_, f32[136,512]{1,0:T(8,128)S(1)} %work.7.refs_2_.refs_1_), custom_call_target="tpu_custom_call" | custom-call | flops 6039797760 | bytes 1048576 | tf_op jit(solution)/shard_map/work/pallas_call | solution.py:227
  15.0 0.5 %collective-permute-start.3 = (bf16[64,1024]{1,0:T(8,128)(2,1)S(1)}, bf16[64,1024]{1,0:T(8,128)(2,1)S(1)}, u32[]{:S(2)}, u32[]{:S(2)}) collective-permute-start(bf16[64,1024]{1,0:T(8,128)(2,1)S(1)} %get-tuple-element.18.q_ref), channel_id=1, source_target_pairs={{0,8},{8,0},{16,24},{24,16},{1,9},{9,1},{17,25},{25,17},{2,10},{10... | collective-permute-start | bytes 393224 | tf_op jit(solution)/shard_map/ppermute | solution.py:188
  15.5 0.0 collective-permute-done.4.q_ref
  15.5 0.7 %work.9.refs_1_ = f32[136,512]{1,0:T(8,128)S(1)} custom-call(s32[1]{0:T(128)S(6)} %copy.9.len_ref, bf16[64,1024]{1,0:T(8,128)(2,1)S(1)} %collective-permute-done.4.q_ref, bf16[1152,128]{1,0:T(8,128)(2,1)S(1)} %get-tuple-element.12.refs_0_, f32[136,512]{1,0:T(8,128)S(1)} %work.8.refs_1_.refs_2_), custom_call_target="tpu_custom_call" | custom-call | flops 6039797760 | bytes 1048576 | tf_op jit(solution)/shard_map/work/pallas_call | solution.py:227
  16.2 5.8 %collective-permute-done.2.refs_0_ = bf16[1152,128]{1,0:T(8,128)(2,1)S(1)} collective-permute-done((bf16[1152,128]{1,0:T(8,128)(2,1)S(1)}, bf16[1152,128]{1,0:T(8,128)(2,1)S(1)}, u32[]{:S(2)}, u32[]{:S(2)}) %collective-permute-start.2) | collective-permute-done | bytes 294944 | tf_op jit(solution)/shard_map/ppermute | solution.py:188
  22.0 0.8 %work.10.refs_4_ = bf16[528,128]{1,0:T(8,128)(2,1)S(1)} custom-call(s32[1]{0:T(128)S(6)} %copy.9.len_ref, bf16[64,1024]{1,0:T(8,128)(2,1)S(1)} %collective-permute-done.4.q_ref, bf16[1152,128]{1,0:T(8,128)(2,1)S(1)} %collective-permute-done.2.refs_0_, f32[136,512]{1,0:T(8,128)S(1)} %work.9.refs_1_, f32[136,512]{1,0:T(8,128)S(1)} %work.8.refs_1_.refs_2_), custom_call_target="tpu_custom_call" | custom-call | flops 6039797760 | bytes 1048576 | tf_op jit(solution)/shard_map/work/pallas_call | solution.py:227
  22.8 0.1 collective-permute-start.6
  22.9 0.0 collective-permute-done.1.refs_3_.refs_1_
  22.9 2.2 %collective-permute-done.3.q_ref = bf16[64,1024]{1,0:T(8,128)(2,1)S(1)} collective-permute-done((bf16[64,1024]{1,0:T(8,128)(2,1)S(1)}, bf16[64,1024]{1,0:T(8,128)(2,1)S(1)}, u32[]{:S(2)}, u32[]{:S(2)}) %collective-permute-start.3) | collective-permute-done | bytes 131104 | tf_op jit(solution)/shard_map/ppermute | solution.py:188
  25.1 0.0 collective-permute-done.refs_2_.refs_0_
  25.1 1.4 %work.11.refs_2_ = bf16[528,128]{1,0:T(8,128)(2,1)S(1)} custom-call(s32[1]{0:T(128)S(6)} %copy.9.len_ref, bf16[64,1024]{1,0:T(8,128)(2,1)S(1)} %collective-permute-done.3.q_ref, bf16[1024,128]{1,0:T(8,128)(2,1)S(1)} %get-tuple-element.14.refs_1_.refs_0_, bf16[128,128]{1,0:T(8,128)(2,1)S(1)} %get-tuple-element.15.refs_1_, ...), custom_call_target="tpu_custom_call" | custom-call | flops 12079595520 | bytes 1048576 | tf_op jit(solution)/shard_map/work/pallas_call | solution.py:227
  26.5 2.1 %collective-permute-start.5 = (bf16[528,128]{1,0:T(8,128)(2,1)S(1)}, bf16[528,128]{1,0:T(8,128)(2,1)S(1)}, u32[]{:S(2)}, u32[]{:S(2)}) collective-permute-start(bf16[528,128]{1,0:T(8,128)(2,1)S(1)} %work.11.refs_2_), channel_id=1, source_target_pairs={{0,8},{8,0},{16,24},{24,16},{1,9},{9,1},{17,25},{25,17},{2,10},{10... | collective-permute-start | bytes 405512 | tf_op jit(solution)/shard_map/ppermute | solution.py:188
  28.5 0.7 %work.12.refs_3_.own_ref = f32[136,512]{1,0:T(8,128)S(1)} custom-call(s32[1]{0:T(128)S(6)} %copy.9.len_ref, bf16[64,1024]{1,0:T(8,128)(2,1)S(1)} %get-tuple-element.16.q_ref, bf16[1152,128]{1,0:T(8,128)(2,1)S(1)} %collective-permute-done.2.refs_0_, f32[136,512]{1,0:T(8,128)S(1)} %work.7.refs_2_.refs_1_, bf16[528,128]{1,0:T(8,128)(2,1)S(1)} %work.11.refs_2_), custom_call_target="tpu_custom_call" | custom-call | flops 6039797760 | bytes 1048576 | tf_op jit(solution)/shard_map/work/pallas_call | solution.py:227
  29.3 0.8 %work.13.refs_0_.own_ref = f32[136,512]{1,0:T(8,128)S(1)} custom-call(s32[1]{0:T(128)S(6)} %copy.9.len_ref, bf16[64,1024]{1,0:T(8,128)(2,1)S(1)} %get-tuple-element.18.q_ref, bf16[1024,128]{1,0:T(8,128)(2,1)S(1)} %collective-permute-done.refs_2_.refs_0_, bf16[128,128]{1,0:T(8,128)(2,1)S(1)} %collective-permute-done.1.refs_3_.refs_1_, ...), custom_call_target="tpu_custom_call" | custom-call | flops 6039797760 | bytes 1048576 | tf_op jit(solution)/shard_map/work/pallas_call | solution.py:227
  30.0 0.0 collective-permute-done.6.got_ref
  30.1 0.8 %merge.2.refs_0_ = bf16[64,2048]{1,0:T(8,128)(2,1)} custom-call(f32[136,512]{1,0:T(8,128)S(1)} %work.12.refs_3_.own_ref, bf16[528,128]{1,0:T(8,128)(2,1)S(1)} %collective-permute-done.6.got_ref, f32[136,512]{1,0:T(8,128)S(1)} %work.13.refs_0_.own_ref), custom_call_target="tpu_custom_call" | custom-call | tf_op jit(solution)/shard_map/merge/pallas_call | solution.py:243
  30.9 1.0 %collective-permute-done.5.got_ref = bf16[528,128]{1,0:T(8,128)(2,1)S(1)} collective-permute-done((bf16[528,128]{1,0:T(8,128)(2,1)S(1)}, bf16[528,128]{1,0:T(8,128)(2,1)S(1)}, u32[]{:S(2)}, u32[]{:S(2)}) %collective-permute-start.5) | collective-permute-done | bytes 135200 | tf_op jit(solution)/shard_map/ppermute | solution.py:188
  31.9 0.8 %merge.3 = bf16[64,2048]{1,0:T(8,128)(2,1)} custom-call(f32[136,512]{1,0:T(8,128)S(1)} %work.13.refs_0_.own_ref, bf16[528,128]{1,0:T(8,128)(2,1)S(1)} %collective-permute-done.5.got_ref, bf16[64,2048]{1,0:T(8,128)(2,1)} %merge.2.refs_0_), custom_call_target="tpu_custom_call", output_to_operand_aliasing={{}: (2, {})} | custom-call | tf_op jit(solution)/shard_map/merge/pallas_call | solution.py:243
Async XLA Ops:
  1.1 14.4 %collective-permute-start.4 = (bf16[64,1024]{1,0:T(8,128)(2,1)S(1)}, bf16[64,1024]{1,0:T(8,128)(2,1)S(1)}, u32[]{:S(2)}, u32[]{:S(2)}) collective-permute-start(bf16[64,1024]{1,0:T(8,128)(2,1)S(1)} %get-tuple-element.16.q_ref), channel_id=1, source_target_pairs={{0,16},{8,24},{16,0},{24,8},{1,17},{9,25},{17,1},{25,9},{2,18},{10... | collective-permute-start | bytes 393224 | tf_op jit(solution)/shard_map/ppermute | solution.py:188
  5.2 16.8 %collective-permute-start.2 = (bf16[1152,128]{1,0:T(8,128)(2,1)S(1)}, bf16[1152,128]{1,0:T(8,128)(2,1)S(1)}, u32[]{:S(2)}, u32[]{:S(2)}) collective-permute-start(bf16[1152,128]{1,0:T(8,128)(2,1)S(1)} %get-tuple-element.12.refs_0_), channel_id=1, source_target_pairs={{0,8},{8,0},{16,24},{24,16},{1,9},{9,1},{17,25},{25,17},{2,10},{10... | collective-permute-start | bytes 884744 | tf_op jit(solution)/shard_map/ppermute | solution.py:188
  7.9 17.2 %collective-permute-start = (bf16[1024,128]{1,0:T(8,128)(2,1)S(1)}, bf16[1024,128]{1,0:T(8,128)(2,1)S(1)}, u32[]{:S(2)}, u32[]{:S(2)}) collective-permute-start(bf16[1024,128]{1,0:T(8,128)(2,1)S(1)} %get-tuple-element.14.refs_1_.refs_0_), channel_id=1, source_target_pairs={{0,16},{8,24},{16,0},{24,8},{1,17},{9,25},{17,1},{25,9},{2,18},{10... | collective-permute-start | bytes 786440 | tf_op jit(solution)/shard_map/ppermute | solution.py:188
  8.3 14.5 %collective-permute-start.1 = (bf16[128,128]{1,0:T(8,128)(2,1)S(1)}, bf16[128,128]{1,0:T(8,128)(2,1)S(1)}, u32[]{:S(2)}, u32[]{:S(2)}) collective-permute-start(bf16[128,128]{1,0:T(8,128)(2,1)S(1)} %get-tuple-element.15.refs_1_), channel_id=1, source_target_pairs={{0,16},{8,24},{1,17},{9,25},{2,18},{10,26},{3,19},{11,27},{4,20},{... | collective-permute-start | bytes 98312 | tf_op jit(solution)/shard_map/ppermute | solution.py:188
  15.0 10.1 %collective-permute-start.3 = (bf16[64,1024]{1,0:T(8,128)(2,1)S(1)}, bf16[64,1024]{1,0:T(8,128)(2,1)S(1)}, u32[]{:S(2)}, u32[]{:S(2)}) collective-permute-start(bf16[64,1024]{1,0:T(8,128)(2,1)S(1)} %get-tuple-element.18.q_ref), channel_id=1, source_target_pairs={{0,8},{8,0},{16,24},{24,16},{1,9},{9,1},{17,25},{25,17},{2,10},{10... | collective-permute-start | bytes 393224 | tf_op jit(solution)/shard_map/ppermute | solution.py:188
  22.8 7.3 %collective-permute-start.6 = (bf16[528,128]{1,0:T(8,128)(2,1)S(1)}, bf16[528,128]{1,0:T(8,128)(2,1)S(1)}, u32[]{:S(2)}, u32[]{:S(2)}) collective-permute-start(bf16[528,128]{1,0:T(8,128)(2,1)S(1)} %work.10.refs_4_), channel_id=1, source_target_pairs={{0,16},{8,24},{16,0},{24,8},{1,17},{9,25},{17,1},{25,9},{2,18},{10... | collective-permute-start | bytes 405512 | tf_op jit(solution)/shard_map/ppermute | solution.py:188
  26.5 5.4 %collective-permute-start.5 = (bf16[528,128]{1,0:T(8,128)(2,1)S(1)}, bf16[528,128]{1,0:T(8,128)(2,1)S(1)}, u32[]{:S(2)}, u32[]{:S(2)}) collective-permute-start(bf16[528,128]{1,0:T(8,128)(2,1)S(1)} %work.11.refs_2_), channel_id=1, source_target_pairs={{0,8},{8,0},{16,24},{24,16},{1,9},{9,1},{17,25},{25,17},{2,10},{10... | collective-permute-start | bytes 405512 | tf_op jit(solution)/shard_map/ppermute | solution.py:188
